TPU v7x, 32 devices: a whole 2x2x4 slice. The times are simulated.
32 devices in a mesh: gx: 2 (over x), gy: 4 (over z), sa: 4 (over y, core).
Axes of the slice: x: 2, y: 2, z: 4, core: 2. Of those that a mesh axis runs over, the one named last changes fastest.
Arguments:
- scalar_field: float32 [64, 1, 1024, 512], P('sa', None, 'gx', 'gy'), may hold values from -80 to 80, as said below
- start_basis: float32 [1024, 128], replicated, may hold values from -6 to 6
Outputs:
- core_tensor: float32 [64, 1, 128, 512], P(('sa', 'gx'), None, 'gy')
- leading_basis: float32 [1024, 128], P(('gx', 'gy', 'sa'))
Inputs may be any that keep to these rules, and one draw needn't show every extreme that they name: `scalar_field`: every entry is finite.
All inputs are finite; a program needn't handle non-finite values.
Results may differ from a plain program's by a relative error of at most 0.0003.
Values sent between devices are 32-bit elements; how exact they have to be, the bound alone decides.
No kernel may reach another device: no remote copies, remote signals or barrier semaphores. Data moves between devices by JAX's collectives and lax.ppermute only.
A program may use at most 64 MiB of HBM per device.

v0:
```python
import jax
import jax.numpy as jnp
from jax import lax
from jax.sharding import PartitionSpec as P

NX = 1024
S = 64
ITERS = 3


HIGHEST_PREC = lax.Precision.HIGHEST


def orthonormal(mapped):
    inner_gram = jnp.dot(
        mapped.T, mapped, precision=HIGHEST_PREC, preferred_element_type=jnp.float32
    )
    factor = jnp.linalg.cholesky(inner_gram)
    return jax.scipy.linalg.solve_triangular(factor, mapped.T, lower=True).T


def on_device(scalar_field, start_basis):
    fibres = lax.all_to_all(scalar_field, "gx", split_axis=0, concat_axis=2, tiled=True)
    total_cols = fibres.shape[3] * lax.axis_size("gy") * S * fibres.shape[1]
    devices = lax.axis_size(("gx", "gy", "sa"))
    rows_dev = NX // devices
    my_index = lax.axis_index(("gx", "gy", "sa"))
    cur_basis = start_basis
    partial_value = jnp.einsum(
        "stxy,stzy->xz", fibres, fibres, precision=HIGHEST_PREC, preferred_element_type=jnp.float32
    )
    gram_matrix = lax.psum(partial_value, ("gx", "gy", "sa")) / total_cols
    for iteration in range(ITERS):
        mapped = jnp.dot(
            gram_matrix, cur_basis, precision=HIGHEST_PREC, preferred_element_type=jnp.float32
        )
        cur_basis = orthonormal(orthonormal(mapped))
    own_rows = lax.dynamic_slice_in_dim(cur_basis, my_index * rows_dev, rows_dev, 0)
    projected = jnp.einsum(
        "xk,stxy->stky",
        cur_basis,
        fibres,
        precision=HIGHEST_PREC,
        preferred_element_type=jnp.float32,
    )
    core_tensor = lax.all_to_all(projected, "gy", split_axis=2, concat_axis=3, tiled=True)
    return (core_tensor, own_rows)


def solution(mesh):
    placed = (P("sa", None, "gx", "gy"), P())
    return jax.shard_map(
        on_device,
        mesh=mesh,
        in_specs=placed,
        out_specs=(P(("sa", "gx"), None, "gy", None), P(("gx", "gy", "sa"), None)),
        check_vma=False,
    )
```

profile of v0, /device:TPU:0, one launch (start us, length us, event | category | flops | bytes accessed | tf_op | source)
XLA Modules:
  0.0 425.3 jit_solution(17983433482042971169)
XLA Ops:
  7.2 0.0 copy-start
  7.2 0.0 all-reduce.2.cloned.1.call-start
  7.2 53.0 %all_to_all.33 = f32[16,1,512,128]{3,2,1,0:T(8,128)S(1)} all-to-all(f32[16,1,512,128]{3,2,1,0:T(8,128)} %param.5), channel_id=1, replica_groups=mesh['gx'=2,'gy'=4,'sa'=4] {'gx'}, dimensions={0} | all-to-all | bytes 8388608 | tf_op jit(solution)/shard_map/all_to_all | solution.py:23
  60.3 0.4 copy.13
  60.6 0.0 copy-start.1
  60.7 1.9 copy-done.1
  62.6 14.7 %convolution_bitcast_fusion = f32[1024,1024]{1,0:T(8,128)} fusion(f32[8,1024,128]{2,1,0:T(8,128)S(1)} %bitcast.106), kind=kOutput, calls=%fused_computation.6 | convolution fusion | flops 12884901888 | bytes 8388608 | tf_op jit(solution)/shard_map/stxy,stzy->xz/dot_general | solution.py:29
  77.3 0.0 all-reduce.2.cloned.1.call-update
  77.3 142.5 %all-reduce.2.cloned.1.call-done = f32[1024,1024]{1,0:T(8,128)} async-done(((f32[1024,1024]{1,0:T(8,128)}), f32[1024,1024]{1,0:T(8,128)}) %all-reduce.2.cloned.1.call-update) | async-done | bytes 4194320 | tf_op jit(solution)/shard_map/psum | solution.py:32
  219.8 0.0 copy-done
  219.8 5.6 %fusion.4 = f32[1024,128]{1,0:T(8,128)S(1)} fusion(f32[1024,128]{1,0:T(8,128)S(1)} %copy-done, f32[1024,1024]{1,0:T(8,128)} %all-reduce.2.cloned.1.call-done), kind=kOutput, calls=%fused_computation.4 | convolution fusion | flops 1611661312 | bytes 5242880 | tf_op jit(solution)/shard_map/dot_general | solution.py:34
  225.4 1.0 fusion.50
  226.4 0.1 copy.14
  226.6 11.7 %cholesky.104 = f32[128,128]{1,0:T(8,128)S(1)} custom-call(f32[128,128]{1,0:T(8,128)S(1)} %fusion.36), custom_call_target="Cholesky" | custom-call | tf_op jit(solution)/shard_map/jit(cholesky)/cholesky | solution.py:18
  238.3 0.6 compare_reduce_fusion.5
  238.9 0.7 fusion.16
  239.6 9.8 %custom-call.10 = f32[1,128,128]{1,2,0:T(8,128)S(1)} custom-call(f32[1,128,128]{2,1,0:T(8,128)S(1)} %fusion.16), custom_call_target="InvertDiagBlocksLowerTriangular" | custom-call | tf_op jit(solution)/shard_map/jit(_solve_triangular)/triangular_solve | solution.py:19
  249.4 0.6 fusion.14
  250.1 0.6 fusion.51
  250.7 0.1 copy.15
  250.8 11.7 %cholesky.115 = f32[128,128]{1,0:T(8,128)S(1)} custom-call(f32[128,128]{1,0:T(8,128)S(1)} %fusion.34), custom_call_target="Cholesky" | custom-call | tf_op jit(solution)/shard_map/jit(cholesky)/cholesky | solution.py:18
  274.3 0.6 compare_reduce_fusion.4
  274.9 0.7 fusion.17
  275.6 9.8 %custom-call.11 = f32[1,128,128]{1,2,0:T(8,128)S(1)} custom-call(f32[1,128,128]{2,1,0:T(8,128)S(1)} %fusion.17), custom_call_target="InvertDiagBlocksLowerTriangular" | custom-call | tf_op jit(solution)/shard_map/jit(_solve_triangular)/triangular_solve | solution.py:19
  285.4 0.6 fusion.32
  286.1 5.2 %fusion.2 = f32[1024,128]{1,0:T(8,128)S(1)} fusion(f32[128,1024]{1,0:T(8,128)S(1)} %fusion.32, f32[1024,1024]{1,0:T(8,128)} %all-reduce.2.cloned.1.call-done), kind=kOutput, calls=%fused_computation.2 | convolution fusion | flops 1611661312 | bytes 5242880 | tf_op jit(solution)/shard_map/dot_general | solution.py:34
  291.3 1.0 fusion.52
  292.3 0.1 copy.16
  292.4 11.7 %cholesky.126 = f32[128,128]{1,0:T(8,128)S(1)} custom-call(f32[128,128]{1,0:T(8,128)S(1)} %fusion.31), custom_call_target="Cholesky" | custom-call | tf_op jit(solution)/shard_map/jit(cholesky)/cholesky | solution.py:18
  304.2 0.6 compare_reduce_fusion.3
  304.8 0.7 fusion.18
  305.5 9.8 %custom-call.12 = f32[1,128,128]{1,2,0:T(8,128)S(1)} custom-call(f32[1,128,128]{2,1,0:T(8,128)S(1)} %fusion.18), custom_call_target="InvertDiagBlocksLowerTriangular" | custom-call | tf_op jit(solution)/shard_map/jit(_solve_triangular)/triangular_solve | solution.py:19
  315.3 0.6 fusion.12
  315.9 0.6 fusion.53
  316.5 0.1 copy.17
  316.6 11.7 %cholesky.137 = f32[128,128]{1,0:T(8,128)S(1)} custom-call(f32[128,128]{1,0:T(8,128)S(1)} %fusion.29), custom_call_target="Cholesky" | custom-call | tf_op jit(solution)/shard_map/jit(cholesky)/cholesky | solution.py:18
  328.8 0.6 compare_reduce_fusion.2
  329.4 0.7 fusion.19
  330.1 9.8 %custom-call.13 = f32[1,128,128]{1,2,0:T(8,128)S(1)} custom-call(f32[1,128,128]{2,1,0:T(8,128)S(1)} %fusion.19), custom_call_target="InvertDiagBlocksLowerTriangular" | custom-call | tf_op jit(solution)/shard_map/jit(_solve_triangular)/triangular_solve | solution.py:19
  339.9 0.6 fusion.27
  340.5 5.2 %fusion = f32[1024,128]{1,0:T(8,128)S(1)} fusion(f32[128,1024]{1,0:T(8,128)S(1)} %fusion.27, f32[1024,1024]{1,0:T(8,128)} %all-reduce.2.cloned.1.call-done), kind=kOutput, calls=%fused_computation | convolution fusion | flops 1611661312 | bytes 5242880 | tf_op jit(solution)/shard_map/dot_general | solution.py:34
  345.8 1.0 fusion.54
  346.8 0.1 copy.18
  346.9 11.7 %cholesky.148 = f32[128,128]{1,0:T(8,128)S(1)} custom-call(f32[128,128]{1,0:T(8,128)S(1)} %fusion.26), custom_call_target="Cholesky" | custom-call | tf_op jit(solution)/shard_map/jit(cholesky)/cholesky | solution.py:18
  358.6 0.6 compare_reduce_fusion.1
  359.3 0.7 fusion.20
  359.9 9.8 %custom-call.14 = f32[1,128,128]{1,2,0:T(8,128)S(1)} custom-call(f32[1,128,128]{2,1,0:T(8,128)S(1)} %fusion.20), custom_call_target="InvertDiagBlocksLowerTriangular" | custom-call | tf_op jit(solution)/shard_map/jit(_solve_triangular)/triangular_solve | solution.py:19
  369.8 0.6 fusion.10
  370.4 0.6 fusion.55
  371.0 0.1 copy.19
  371.1 11.7 %cholesky.159 = f32[128,128]{1,0:T(8,128)S(1)} custom-call(f32[128,128]{1,0:T(8,128)S(1)} %fusion.24), custom_call_target="Cholesky" | custom-call | tf_op jit(solution)/shard_map/jit(cholesky)/cholesky | solution.py:18
  383.0 0.6 compare_reduce_fusion
  383.7 0.7 fusion.21
  384.3 9.8 %custom-call.15 = f32[1,128,128]{1,2,0:T(8,128)S(1)} custom-call(f32[1,128,128]{2,1,0:T(8,128)S(1)} %fusion.21), custom_call_target="InvertDiagBlocksLowerTriangular" | custom-call | tf_op jit(solution)/shard_map/jit(_solve_triangular)/triangular_solve | solution.py:19
  394.1 0.6 fusion.22
  394.8 4.6 %convolution_bitcast_fusion.1 = f32[8,1,128,128]{3,2,0,1:T(8,128)S(1)} fusion(f32[8,1024,128]{2,1,0:T(8,128)} %bitcast.107, f32[128,1024]{1,0:T(8,128)S(1)} %fusion.22), kind=kOutput, calls=%fused_computation.10 | convolution fusion | flops 1610612736 | bytes 5242880 | tf_op jit(solution)/shard_map/xk,stxy->stky/dot_general | solution.py:39
  399.4 1.1 copy.20
  400.5 3.5 all-to-all-start.1
  404.0 0.1 dynamic-slice_bitcast_fusion
  404.1 0.7 copy.22
  404.7 12.2 %all-to-all-done.1 = f32[8,1,128,128]{3,0,1,2:T(8,128)S(1)} async-done(((f32[8,1,128,128]{3,0,1,2:T(8,128)}), f32[8,1,128,128]{3,0,1,2:T(8,128)S(1)}, u32[]{:S(2)}, u32[]{:S(2)}) %all-to-all-start.1) | async-done | bytes 524320 | tf_op jit(solution)/shard_map/all_to_all | solution.py:46
  416.9 0.3 copy.21
  417.3 1.0 all_to_all.30
  (12 shorter events, 0.3 us)
Async XLA Ops:
  7.2 212.7 %copy-start = (f32[1024,128]{1,0:T(8,128)S(1)}, f32[1024,128]{1,0:T(8,128)}, u32[]{:S(2)}) copy-start(f32[1024,128]{1,0:T(8,128)} %param.6) | copy-start | bytes 1572868
  7.2 212.6 %all-reduce.2.cloned.1.call-start = ((), (), s32[]{:S(2)}) async-start(), calls=%async_computation.2 | async-start | bytes 8388608 | tf_op jit(solution)/shard_map/psum | solution.py:32
  60.6 1.9 copy-start.1
  400.5 16.5 %all-to-all-start.1 = ((f32[8,1,128,128]{3,0,1,2:T(8,128)}), f32[8,1,128,128]{3,0,1,2:T(8,128)S(1)}, u32[]{:S(2)}, u32[]{:S(2)}) async-start(f32[8,1,128,128]{3,0,1,2:T(8,128)} %copy.20), calls=%async_computation.1 | async-start | bytes 1048576 | tf_op jit(solution)/shard_map/all_to_all | solution.py:46
Sparse Core Ops, SparseCore 0:
  77.5 142.3 all-reduce.1
where the time goes:
time: 433 us; the launch traced here: 425 us
  waiting for transfers between devices  155 us (36%)
  other arithmetic  137 us (32%)
  blocking collectives  53 us (12%)
  matrix products  44 us (10%)
  between operations  26.9 us (6%)
  local copies, waits for them, and re-layouts  6.05 us (1%)
    psum x1, waiting for transfers between devices, on_device(): gram_matrix = lax.psum(partial_value, ('gx', 'gy', 'sa')) / total_cols  142 us
    another operation x18, other arithmetic, orthonormal(): factor = jnp.linalg.cholesky(inner_gram)  74.3 us
    another operation x12, other arithmetic, orthonormal(): return jax.scipy.linalg.solve_triangular(factor, mapped.T, lower=True).T  62.8 us
    all_to_all x1, blocking collectives, on_device(): lax.all_to_all(scalar_field, 'gx', split_axis=0, concat_axis=2, tiled=True)  53 us
    dot_general x3, matrix products, on_device(): jnp.dot(gram_matrix, cur_basis, precision=HIGHEST_PREC, preferred_element...  16 us
    dot_general x1, matrix products, on_device(): jnp.einsum('stxy,stzy->xz', fibres, fibres, precision=HIGHEST_PREC, prefe...  14.7 us
    all_to_all x1, waiting for transfers between devices, on_device(): lax.all_to_all(projected, 'gy', split_axis=2, concat_axis=3, tiled=True)  12.2 us
  transfers between devices with their start and end apart: 2, of which 2 were waited for; matrix products, arithmetic and copies ran while one was open for 0% of the time, Pallas kernels for 0%

commit v1 on v0

v1 whole, which is shorter than its diff:
```python
import functools

import jax
import jax.numpy as jnp
from jax import lax
from jax.experimental import pallas as pl
from jax.experimental.pallas import tpu as pltpu
from jax.sharding import PartitionSpec as P

ITERS = 3
PANEL = 8
SMALL = 1e-6
HIGHEST_PREC = lax.Precision.HIGHEST
HIGH_PREC = lax.Precision.HIGH


def mul(left, right):
    return lax.dot_general(
        left, right, (((1,), (0,)), ((), ())), precision=HIGHEST_PREC, preferred_element_type=jnp.float32
    )


def mul_t(left, right):
    return lax.dot_general(
        left, right, (((1,), (1,)), ((), ())), precision=HIGHEST_PREC, preferred_element_type=jnp.float32
    )


def inverse_factor(matrix):
    order = matrix.shape[0]
    panels = order // PANEL
    shape = (PANEL, order)
    sub = lax.broadcasted_iota(jnp.int32, shape, 0)
    lane = lax.broadcasted_iota(jnp.int32, shape, 1)
    rows = [matrix[PANEL * q : PANEL * (q + 1), :] for q in range(panels)]
    inverse = [jnp.where(lane == sub + PANEL * q, 1.0, 0.0).astype(jnp.float32) for q in range(panels)]
    for p in range(panels):
        columns = {
            q: [
                jnp.broadcast_to(rows[q][:, PANEL * p + j : PANEL * p + j + 1], shape)
                for j in range(PANEL)
            ]
            for q in range(p, panels)
        }
        for j in range(PANEL):
            scale = lax.rsqrt(jnp.broadcast_to(columns[p][j][j : j + 1, :], shape))
            factor = {q: columns[q][j] * scale for q in range(p, panels)}
            row = jnp.broadcast_to(rows[p][j : j + 1, :], shape) * scale
            inverse_row = jnp.broadcast_to(inverse[p][j : j + 1, :], shape) * scale
            for k in range(j + 1, PANEL):
                pivot = jnp.broadcast_to(factor[p][k : k + 1, :], shape)
                for q in range(p, panels):
                    columns[q][k] = columns[q][k] - factor[q] * pivot
            below = jnp.where(sub > j, factor[p], 0.0)
            rows[p] = rows[p] - below * row
            inverse[p] = jnp.where(sub == j, inverse_row, inverse[p] - below * inverse_row)
            for q in range(p + 1, panels):
                rows[q] = rows[q] - factor[q] * row
                inverse[q] = inverse[q] - factor[q] * inverse_row
    return jnp.concatenate(inverse, axis=0)


def inverse_factor_near_one(error, row, col):
    def lower(a):
        return jnp.where(row > col, a, jnp.where(row == col, 0.5 * a, 0.0))

    first = lower(error)
    eye = jnp.where(row == col, 1.0, 0.0)
    return eye - first + (lower(mul_t(first, first)) + mul(first, first))


def subspace_kernel(first_ref, last_ref, cross_ref, start_ref, basis_ref, gram_ref, inverse_ref):
    half = first_ref.shape[0]
    rank = start_ref.shape[0]
    row = lax.broadcasted_iota(jnp.int32, (rank, rank), 0)
    col = lax.broadcasted_iota(jnp.int32, (rank, rank), 1)
    cross = cross_ref[...]
    gram_ref[:half, :half] = first_ref[...]
    gram_ref[half:, half:] = last_ref[...]
    gram_ref[:half, half:] = cross
    gram_ref[half:, :half] = cross.T
    basis_ref[...] = start_ref[...]

    def iteration(_, carry):
        mapped = mul(basis_ref[...], gram_ref[...])
        once = mul(inverse_factor(mul_t(mapped, mapped)), mapped)
        inner = mul_t(once, once)
        error = inner - jnp.where(row == col, 1.0, 0.0)
        small = jnp.sum(error * error) <= SMALL

        @pl.when(small)
        def _():
            inverse_ref[...] = inverse_factor_near_one(error, row, col)

        @pl.when(jnp.logical_not(small))
        def _():
            inverse_ref[...] = inverse_factor(inner)

        basis_ref[...] = mul(inverse_ref[...], once)
        return carry

    lax.fori_loop(0, ITERS, iteration, 0)


def subspace(first, last, cross, start):
    rank, order = start.shape
    return pl.pallas_call(
        subspace_kernel,
        out_shape=jax.ShapeDtypeStruct((rank, order), jnp.float32),
        in_specs=[pl.BlockSpec(memory_space=pltpu.VMEM)] * 4,
        out_specs=pl.BlockSpec(memory_space=pltpu.VMEM),
        scratch_shapes=[pltpu.VMEM((order, order), jnp.float32), pltpu.VMEM((rank, rank), jnp.float32)],
        compiler_params=pltpu.CompilerParams(vmem_limit_bytes=48 << 20),
        name="subspace",
    )(first, last, cross, start)


def flip(size, bit):
    return [(i, i ^ bit) for i in range(size)]


def turn(size, step):
    return [(i, (i + step) % size) for i in range(size)]


def blocks(array, count):
    return array.reshape((count, array.shape[0] // count) + array.shape[1:])


def part(array, index):
    return lax.dynamic_index_in_dim(array, index, 0, keepdims=False)


def scatter_flip(array, axis, bit):
    mine = (lax.axis_index(axis) & bit) // bit
    halves = blocks(array, 2)
    got = lax.ppermute(part(halves, 1 - mine), axis, flip(lax.axis_size(axis), bit))
    return part(halves, mine) + got


def gather_flip(array, axis, bit):
    mine = (lax.axis_index(axis) & bit) // bit
    got = lax.ppermute(array, axis, flip(lax.axis_size(axis), bit))
    low = jnp.where(mine == 0, array, got)
    high = jnp.where(mine == 0, got, array)
    return jnp.concatenate([low, high], axis=0)


def scatter_turn(array, axis):
    size = lax.axis_size(axis)
    mine = lax.axis_index(axis)
    parts = blocks(array, size)
    total = part(parts, mine)
    for step in range(1, size):
        total = total + lax.ppermute(part(parts, (mine + step) % size), axis, turn(size, step))
    return total


def gather_turn(array, axis):
    size = lax.axis_size(axis)
    mine = lax.axis_index(axis)
    out = jnp.zeros((size,) + array.shape, array.dtype)
    out = lax.dynamic_update_index_in_dim(out, array, mine, 0)
    for step in range(1, size):
        got = lax.ppermute(array, axis, turn(size, step))
        out = lax.dynamic_update_index_in_dim(out, got, (mine - step) % size, 0)
    return out.reshape((-1,) + array.shape[1:])


def pair_targets(size):
    moves = [(1, 0), (0, 2), (1, 2)]
    return [
        [(x * size + s, (x ^ dx) * size + (s ^ ds)) for x in range(2) for s in range(size)]
        for dx, ds in moves
    ], moves


def sum_cross(array):
    rows = array.shape[0]
    quarter = scatter_flip(array, "sa", 1)
    targets, moves = pair_targets(lax.axis_size("sa"))
    x = lax.axis_index("gx")
    y = lax.axis_index("sa") // 2
    parts = blocks(quarter, 4)
    total = part(parts, x * 2 + y)
    for target, (dx, ds) in zip(targets, moves):
        total = total + lax.ppermute(
            part(parts, (x ^ dx) * 2 + (y ^ (ds // 2))), ("gx", "sa"), target
        )
    size = lax.axis_size("gy")
    shares = [lax.ppermute(total, "gy", turn(size, step)) for step in range(1, size)]
    for share in shares:
        total = total + share
    out = jnp.zeros((4,) + total.shape, total.dtype)
    out = lax.dynamic_update_index_in_dim(out, total, x * 2 + y, 0)
    for target, (dx, ds) in zip(targets, moves):
        got = lax.ppermute(total, ("gx", "sa"), target)
        out = lax.dynamic_update_index_in_dim(out, got, (x ^ dx) * 2 + (y ^ (ds // 2)), 0)
    return gather_flip(out.reshape((rows // 2,) + array.shape[1:]), "sa", 1)


def sum_own(array):
    rows, cols = array.shape
    piece = scatter_turn(scatter_flip(scatter_flip(array, "sa", 1), "sa", 2), "gy")
    other = lax.ppermute(piece, "gx", flip(2, 1))
    both = jnp.concatenate([piece, other], axis=1)
    whole = gather_flip(gather_flip(gather_turn(both, "gy"), "sa", 2), "sa", 1)
    x = lax.axis_index("gx")
    own, far = whole[:, :cols], whole[:, cols:]
    return jnp.where(x == 0, own, far), jnp.where(x == 0, far, own)


def outer(left, right):
    return jnp.einsum(
        "stxy,stzy->xz", left, right, precision=HIGH_PREC, preferred_element_type=jnp.float32
    )


def project(basis, field):
    return jnp.einsum(
        "kx,stxy->stky", basis, field, precision=HIGH_PREC, preferred_element_type=jnp.float32
    )


def on_halves(field, start):
    x = lax.axis_index("gx")
    species = field.shape[0] // 2
    half = field.shape[2]
    columns = field.shape[0] * field.shape[1] * field.shape[3]
    columns = columns * lax.axis_size("gy") * lax.axis_size("sa")
    mine = lax.dynamic_slice_in_dim(field, x * species, species, 0)
    sent = lax.dynamic_slice_in_dim(field, (1 - x) * species, species, 0)
    count = 4
    received = [lax.ppermute(piece, "gx", flip(2, 1)) for piece in blocks(sent, count)]
    first, last = sum_own(outer(field, field))
    cross = 0.0
    for got, kept in zip(received, blocks(mine, count)):
        cross = cross + outer(jnp.where(x == 0, kept, got), jnp.where(x == 0, got, kept))
    cross = sum_cross(cross)
    basis = subspace(first / columns, last / columns, cross / columns, start.T)
    near = lax.dynamic_slice_in_dim(basis, x * half, half, 1)
    far = lax.dynamic_slice_in_dim(basis, (1 - x) * half, half, 1)
    projected = project(near, mine) + project(far, jnp.concatenate(received, axis=0))
    return basis, projected


def on_fibres(field, start):
    fibres = lax.all_to_all(field, "gx", split_axis=0, concat_axis=2, tiled=True)
    columns = fibres.shape[0] * fibres.shape[1] * fibres.shape[3]
    columns = columns * lax.axis_size(("gx", "gy", "sa"))
    half = fibres.shape[2] // 2
    gram = lax.psum(outer(fibres, fibres), ("gx", "gy", "sa")) / columns
    basis = subspace(gram[:half, :half], gram[half:, half:], gram[:half, half:], start.T)
    return basis, project(basis, fibres)


def on_device(scalar_field, start_basis):
    if lax.axis_size("gx") == 2 and lax.axis_size("sa") == 4:
        basis, projected = on_halves(scalar_field, start_basis)
    else:
        basis, projected = on_fibres(scalar_field, start_basis)
    rows_dev = start_basis.shape[0] // lax.axis_size(("gx", "gy", "sa"))
    my_index = lax.axis_index(("gx", "gy", "sa"))
    own_rows = lax.dynamic_slice_in_dim(basis.T, my_index * rows_dev, rows_dev, 0)
    core_tensor = lax.all_to_all(projected, "gy", split_axis=2, concat_axis=3, tiled=True)
    return (core_tensor, own_rows)


def solution(mesh):
    placed = (P("sa", None, "gx", "gy"), P())
    return jax.shard_map(
        on_device,
        mesh=mesh,
        in_specs=placed,
        out_specs=(P(("sa", "gx"), None, "gy", None), P(("gx", "gy", "sa"), None)),
        check_vma=False,
    )
```

time: 433 us -> 189 us (0.44); the launches traced: 425 us -> 188 us
  other arithmetic: 137 us -> 9.31 us
  waiting for transfers between devices: 155 us -> 63.5 us
  blocking collectives: 53 us -> 0 us
  starting transfers between devices: 3.51 us -> 39.4 us
  Pallas kernels: 0 us -> 31.3 us
  between operations: 26.9 us -> 0.94 us
  matrix products: 44 us -> 18.3 us
  local copies, waits for them, and re-layouts: 6.05 us -> 25.6 us
    psum x1 -> x0, waiting for transfers between devices: 142 us -> none  [on_device(): gram_matrix = lax.psum(partial_value, ('gx', 'gy', 'sa')) / total_cols]
    another operation x30 -> x0, other arithmetic: 137 us -> none  [the longest x18 74.3 us: orthonormal(): factor = jnp.linalg.cholesky(inner_gram)]
    all_to_all x1 -> x0, blocking collectives: 53 us -> none  [on_device(): lax.all_to_all(scalar_field, 'gx', split_axis=0, concat_axis=2, tiled=True)]
    ppermute x0 -> x26, waiting for transfers between devices: none -> 49.5 us  [the longest x4 25.6 us: on_halves(): lax.ppermute(piece, 'gx', flip(2, 1))]
    ppermute x0 -> x26, starting transfers between devices: none -> 32.9 us  [the longest x3 6.07 us: sum_cross(): lax.ppermute(total, 'gy', turn(size, step))]
    pallas_call x0 -> x1, Pallas kernels: none -> 31.3 us  [subspace(): pl.pallas_call(subspace_kernel, out_shape=jax.ShapeDtypeStruct((rank, ord...]
    dot_general x11 -> x7, matrix products: 40.1 us -> 18.3 us  [the longest x5 13.9 us: outer(): jnp.einsum('stxy,stzy->xz', left, right, precision=HIGH_PREC, preferred_e...]
    unnamed x5 -> x21, local copies, waits for them, and re-layouts: 2.61 us -> 12.1 us
  transfers between devices with their start and end apart: 2 -> 27, of which waited for: 2 -> 15; matrix products, arithmetic and copies ran while one was open for 0% -> 19% of each run, Pallas kernels for 0% -> 0%
where the time goes in v1:
time: 189 us; the launch traced here: 188 us
  waiting for transfers between devices  63.5 us (34%)
  starting transfers between devices  39.4 us (21%)
  Pallas kernels  31.3 us (17%)
  local copies, waits for them, and re-layouts  25.6 us (14%)
  matrix products  18.3 us (10%)
  other arithmetic  9.31 us (5%)
    pallas_call x1, Pallas kernels, subspace(): pl.pallas_call(subspace_kernel, out_shape=jax.ShapeDtypeStruct((rank, ord...  31.3 us
    ppermute x4, waiting for transfers between devices, on_halves(): lax.ppermute(piece, 'gx', flip(2, 1))  25.6 us
    all_to_all x1, waiting for transfers between devices, on_device(): lax.all_to_all(projected, 'gy', split_axis=2, concat_axis=3, tiled=True)  14 us
    dot_general x5, matrix products, outer(): jnp.einsum('stxy,stzy->xz', left, right, precision=HIGH_PREC, preferred_e...  13.9 us
    unnamed x21, local copies, waits for them, and re-layouts  12.1 us
    ppermute x3, waiting for transfers between devices, sum_cross(): got = lax.ppermute(total, ('gx', 'sa'), target)  9.15 us
    all_to_all x1, starting transfers between devices, on_device(): lax.all_to_all(projected, 'gy', split_axis=2, concat_axis=3, tiled=True)  6.45 us
    ppermute x3, starting transfers between devices, sum_cross(): lax.ppermute(total, 'gy', turn(size, step))  6.07 us
  transfers between devices with their start and end apart: 27, of which 15 were waited for; matrix products, arithmetic and copies ran while one was open for 19% of the time, Pallas kernels for 0%

profile of v1, /device:TPU:0, one launch (start us, length us, event | category | flops | bytes accessed | tf_op | source)
XLA Modules:
  0.0 188.3 jit_solution(5933290873725259359)
XLA Ops:
  0.6 7.1 %fusion.11 = f32[2,256,512]{2,1,0:T(8,128)S(1)} fusion(f32[2,256,16,128]{3,1,0,2:T(8,128)} %bitcast.144, f32[16,1,512,128]{3,2,1,0:T(8,128)} %param.2), kind=kOutput, calls=%fused_computation.14 | convolution fusion | flops 3221225472 | bytes 9437184 | tf_op jit(solution)/shard_map/stxy,stzy->xz/dot_general | solution.py:214
  7.7 0.9 dynamic-slice_bitcast_fusion.1
  9.1 1.7 constant_dynamic-slice_fusion.2
  10.8 1.0 copy.77
  11.8 2.5 %collective-permute-start.14 = (f32[2,1,512,128]{2,3,0,1:T(8,128)}, f32[2,1,512,128]{2,3,0,1:T(8,128)}, u32[]{:S(2)}, u32[]{:S(2)}) collective-permute-start(f32[2,1,512,128]{2,3,0,1:T(8,128)} %copy.77), channel_id=1, source_target_pairs={{0,16},{16,0},{1,17},{17,1},{2,18},{18,2},{3,19},{19,3},{4,20},{20... | collective-permute-start | bytes 1572872 | tf_op jit(solution)/shard_map/ppermute | solution.py:234
  14.3 1.0 copy.76
  15.3 1.0 copy.75
  16.3 2.0 %collective-permute-start.12 = (f32[2,1,512,128]{2,3,0,1:T(8,128)}, f32[2,1,512,128]{2,3,0,1:T(8,128)}, u32[]{:S(2)}, u32[]{:S(2)}) collective-permute-start(f32[2,1,512,128]{2,3,0,1:T(8,128)} %copy.75), channel_id=1, source_target_pairs={{0,16},{16,0},{1,17},{17,1},{2,18},{18,2},{3,19},{19,3},{4,20},{20... | collective-permute-start | bytes 1572872 | tf_op jit(solution)/shard_map/ppermute | solution.py:234
  18.3 1.0 copy.74
  19.3 1.7 constant_dynamic-slice_fusion.4
  21.0 1.1 fusion.51
  22.2 1.0 copy.81
  23.4 1.2 copy.79
  24.6 2.1 %copy.78 = f32[2,1,512,128]{2,3,0,1:T(8,128)} copy(f32[2,1,512,128]{3,2,1,0:T(8,128)} %get-tuple-element.16) | data formatting | bytes 1048576
  26.7 1.3 bitcast_add_fusion.1
  28.1 2.1 %collective-permute-start.1 = (f32[128,512]{1,0:T(8,128)S(1)}, f32[128,512]{1,0:T(8,128)S(1)}, u32[]{:S(2)}, u32[]{:S(2)}) collective-permute-start(f32[128,512]{1,0:T(8,128)S(1)} %dynamic-slice_bitcast_fusion.2), channel_id=1, source_target_pairs={{0,2},{1,3},{2,0},{3,1},{4,6},{5,7},{6,4},{7,5},{8,10},{9,11},{10,... | collective-permute-start | bytes 786440 | tf_op jit(solution)/shard_map/ppermute | solution.py:137
  30.2 1.7 convolution_bitcast_fusion
  31.9 6.7 %collective-permute-done.13 = f32[2,1,512,128]{2,3,0,1:T(8,128)} collective-permute-done((f32[2,1,512,128]{2,3,0,1:T(8,128)}, f32[2,1,512,128]{2,3,0,1:T(8,128)}, u32[]{:S(2)}, u32[]{:S(2)}) %collective-permute-start.13) | collective-permute-done | bytes 524320 | tf_op jit(solution)/shard_map/ppermute | solution.py:234
  38.6 1.7 convolution_bitcast_fusion.1
  40.3 9.5 %collective-permute-done.12 = f32[2,1,512,128]{2,3,0,1:T(8,128)} collective-permute-done((f32[2,1,512,128]{2,3,0,1:T(8,128)}, f32[2,1,512,128]{2,3,0,1:T(8,128)}, u32[]{:S(2)}, u32[]{:S(2)}) %collective-permute-start.12) | collective-permute-done | bytes 524320 | tf_op jit(solution)/shard_map/ppermute | solution.py:234
  49.8 1.7 convolution_bitcast_fusion.2
  51.5 9.4 %collective-permute-done.11 = f32[2,1,512,128]{2,3,0,1:T(8,128)} collective-permute-done((f32[2,1,512,128]{2,3,0,1:T(8,128)}, f32[2,1,512,128]{2,3,0,1:T(8,128)}, u32[]{:S(2)}, u32[]{:S(2)}) %collective-permute-start.11) | collective-permute-done | bytes 524320 | tf_op jit(solution)/shard_map/ppermute | solution.py:234
  60.9 1.8 fusion.16
  62.8 1.9 collective-permute-start.2
  64.7 2.6 %collective-permute-start.3 = (f32[32,512]{1,0:T(8,128)S(1)}, f32[32,512]{1,0:T(8,128)S(1)}, u32[]{:S(2)}, u32[]{:S(2)}) collective-permute-start(f32[32,512]{1,0:T(8,128)S(1)} %get-tuple-element.33), channel_id=1, source_target_pairs={{0,8},{4,12},{8,0},{12,4},{1,9},{5,13},{9,1},{13,5},{2,10},{6,14},... | collective-permute-start | bytes 196616 | tf_op jit(solution)/shard_map/ppermute | solution.py:155
  67.3 1.3 collective-permute-start.4
  68.6 0.8 dynamic-slice_bitcast_fusion
  69.4 2.3 %collective-permute-done.3 = f32[32,512]{1,0:T(8,128)S(1)} collective-permute-done((f32[32,512]{1,0:T(8,128)S(1)}, f32[32,512]{1,0:T(8,128)S(1)}, u32[]{:S(2)}, u32[]{:S(2)}) %collective-permute-start.3) | collective-permute-done | bytes 65568 | tf_op jit(solution)/shard_map/ppermute | solution.py:155
  71.9 1.7 collective-permute-start.5
  73.6 2.6 %collective-permute-done.5 = f32[32,512]{1,0:T(8,128)S(1)} collective-permute-done((f32[32,512]{1,0:T(8,128)S(1)}, f32[32,512]{1,0:T(8,128)S(1)}, u32[]{:S(2)}, u32[]{:S(2)}) %collective-permute-start.5) | collective-permute-done | bytes 65568 | tf_op jit(solution)/shard_map/ppermute | solution.py:205
  76.2 1.6 collective-permute-start.6
  77.9 2.0 %collective-permute-start.7 = (f32[32,1024]{1,0:T(8,128)S(1)}, f32[32,1024]{1,0:T(8,128)S(1)}, u32[]{:S(2)}, u32[]{:S(2)}) collective-permute-start(f32[32,1024]{1,0:T(8,128)S(1)} %pad_maximum_fusion.2), channel_id=1, source_target_pairs={{0,8},{4,12},{8,0},{12,4},{1,9},{5,13},{9,1},{13,5},{2,10},{6,14},... | collective-permute-start | bytes 393224 | tf_op jit(solution)/shard_map/ppermute | solution.py:165
  80.3 0.8 broadcast_in_dim.32
  81.8 1.1 bitcast_add_fusion
  83.0 1.6 collective-permute-start.16
  84.6 1.5 collective-permute-start.17
  87.2 1.5 collective-permute-done.16
  88.7 1.3 collective-permute-done.17
  90.0 2.0 %collective-permute-done.18 = f32[64,512]{1,0:T(8,128)S(1)} collective-permute-done((f32[64,512]{1,0:T(8,128)S(1)}, f32[64,512]{1,0:T(8,128)S(1)}, u32[]{:S(2)}, u32[]{:S(2)}) %collective-permute-start.18) | collective-permute-done | bytes 131104 | tf_op jit(solution)/shard_map/ppermute | solution.py:187
  92.0 1.7 collective-permute-start.19
  93.6 1.6 collective-permute-start.20
  95.2 2.8 %collective-permute-start.21 = (f32[64,512]{1,0:T(8,128)S(1)}, f32[64,512]{1,0:T(8,128)S(1)}, u32[]{:S(2)}, u32[]{:S(2)}) collective-permute-start(f32[64,512]{1,0:T(8,128)S(1)} %fusion.45), channel_id=1, source_target_pairs={{0,12},{4,0},{8,4},{12,8},{1,13},{5,1},{9,5},{13,9},{2,14},{6,2},{... | collective-permute-start | bytes 393224 | tf_op jit(solution)/shard_map/ppermute | solution.py:191
  99.1 3.2 %collective-permute-done.20 = f32[64,512]{1,0:T(8,128)S(1)} collective-permute-done((f32[64,512]{1,0:T(8,128)S(1)}, f32[64,512]{1,0:T(8,128)S(1)}, u32[]{:S(2)}, u32[]{:S(2)}) %collective-permute-start.20) | collective-permute-done | bytes 131104 | tf_op jit(solution)/shard_map/ppermute | solution.py:191
  102.3 0.9 broadcast_in_dim.37
  103.2 0.7 bitcast_dynamic-update-slice_fusion.3
  104.6 0.8 collective-permute-start.9
  105.4 1.2 collective-permute-start.23
  106.6 2.0 %collective-permute-start.24 = (f32[64,512]{1,0:T(8,128)S(1)}, f32[64,512]{1,0:T(8,128)S(1)}, u32[]{:S(2)}, u32[]{:S(2)}) collective-permute-start(f32[64,512]{1,0:T(8,128)S(1)} %get-tuple-element.11), channel_id=1, source_target_pairs={{0,18},{1,19},{2,16},{3,17},{16,2},{17,3},{18,0},{19,1},{4,22},{5,... | collective-permute-start | bytes 393224 | tf_op jit(solution)/shard_map/ppermute | solution.py:197
  109.5 8.9 %collective-permute-done.23 = f32[64,512]{1,0:T(8,128)S(1)} collective-permute-done((f32[64,512]{1,0:T(8,128)S(1)}, f32[64,512]{1,0:T(8,128)S(1)}, u32[]{:S(2)}, u32[]{:S(2)}) %collective-permute-start.23) | collective-permute-done | bytes 131104 | tf_op jit(solution)/shard_map/ppermute | solution.py:197
  119.1 1.1 broadcast_select_fusion.5
  120.2 0.8 copy-done
  121.0 1.1 pad_maximum_fusion.1
  123.2 1.2 copy.57
  124.5 1.3 collective-permute-done.25
  125.8 1.3 broadcast_select_fusion.3
  127.3 1.5 broadcast_select_fusion.1
  129.1 31.3 %subspace.1 = f32[128,1024]{1,0:T(8,128)S(1)} custom-call(f32[512,512]{1,0:T(8,128)S(1)} %get-tuple-element.21.first_ref, f32[512,512]{1,0:T(8,128)S(1)} %get-tuple-element.20.last_ref, f32[512,512]{1,0:T(8,128)S(1)} %maximum_multiply_fusion.cross_ref, f32[128,1024]{1,0:T(8,128)S(1)} %bitcast.143), custom_call_target="tpu_custom_call" | custom-call | tf_op jit(solution)/shard_map/subspace/pallas_call | solution.py:107
  160.4 1.8 fusion.9
  162.2 2.5 %fusion.18 = f32[8,1,128,128]{2,3,0,1:T(8,128)S(1)} fusion(f32[8,128,128]{2,1,0:T(8,128)S(1)} %fusion.9, f32[2,1,512,128]{2,3,0,1:T(8,128)} %collective-permute-done.14, f32[2,1,512,128]{2,3,0,1:T(8,128)} %collective-permute-done.13, f32[2,1,512,128]{2,3,0,1:T(8,128)} %collective-permute-done.12, f32[2,1,512,128]{2,3,0,1:T(8,128)} %collective-permute-done.11, ...), kind=kOutput, calls=%fused_computation.23 | convolution fusion | flops 404357120 | bytes 3407876 | tf_op jit(solution)/shard_map/kx,stxy->stky/dot_general | solution.py:220
  164.8 1.0 copy.58
  165.8 6.5 %all-to-all-start = ((f32[8,1,128,128]{3,0,1,2:T(8,128)}), f32[8,1,128,128]{3,0,1,2:T(8,128)S(1)}, u32[]{:S(2)}, u32[]{:S(2)}) async-start(f32[8,1,128,128]{3,0,1,2:T(8,128)} %copy.58), calls=%async_computation | async-start | bytes 1048576 | tf_op jit(solution)/shard_map/all_to_all | solution.py:265
  172.3 0.7 copy.62
  173.0 14.0 %all-to-all-done = f32[8,1,128,128]{3,0,1,2:T(8,128)S(1)} async-done(((f32[8,1,128,128]{3,0,1,2:T(8,128)}), f32[8,1,128,128]{3,0,1,2:T(8,128)S(1)}, u32[]{:S(2)}, u32[]{:S(2)}) %all-to-all-start) | async-done | bytes 524320 | tf_op jit(solution)/shard_map/all_to_all | solution.py:265
  187.5 0.8 copy.61
  (53 shorter events, 8.6 us)
Async XLA Ops:
  7.7 3.0 %copy-start.4 = (f32[2,256,512]{2,1,0:T(8,128)}, f32[2,256,512]{2,1,0:T(8,128)S(1)}, u32[]{:S(2)}) copy-start(f32[2,256,512]{2,1,0:T(8,128)S(1)} %fusion.11) | copy-start | bytes 3145732
  8.6 18.1 %collective-permute-start = (f32[256,512]{1,0:T(8,128)}, f32[256,512]{1,0:T(8,128)}, u32[]{:S(2)}, u32[]{:S(2)}) collective-permute-start(f32[256,512]{1,0:T(8,128)} %dynamic-slice_bitcast_fusion.1), channel_id=1, source_target_pairs={{0,1},{1,0},{2,3},{3,2},{4,5},{5,4},{6,7},{7,6},{8,9},{9,8},{10,11... | collective-permute-start | bytes 1572872 | tf_op jit(solution)/shard_map/ppermute | solution.py:137
  11.8 18.4 %collective-permute-start.14 = (f32[2,1,512,128]{2,3,0,1:T(8,128)}, f32[2,1,512,128]{2,3,0,1:T(8,128)}, u32[]{:S(2)}, u32[]{:S(2)}) collective-permute-start(f32[2,1,512,128]{2,3,0,1:T(8,128)} %copy.77), channel_id=1, source_target_pairs={{0,16},{16,0},{1,17},{17,1},{2,18},{18,2},{3,19},{19,3},{4,20},{20... | collective-permute-start | bytes 1572872 | tf_op jit(solution)/shard_map/ppermute | solution.py:234
  15.3 23.3 %collective-permute-start.13 = (f32[2,1,512,128]{2,3,0,1:T(8,128)}, f32[2,1,512,128]{2,3,0,1:T(8,128)}, u32[]{:S(2)}, u32[]{:S(2)}) collective-permute-start(f32[2,1,512,128]{2,3,0,1:T(8,128)} %copy.76), channel_id=1, source_target_pairs={{0,16},{16,0},{1,17},{17,1},{2,18},{18,2},{3,19},{19,3},{4,20},{20... | collective-permute-start | bytes 1572872 | tf_op jit(solution)/shard_map/ppermute | solution.py:234
  16.3 33.5 %collective-permute-start.12 = (f32[2,1,512,128]{2,3,0,1:T(8,128)}, f32[2,1,512,128]{2,3,0,1:T(8,128)}, u32[]{:S(2)}, u32[]{:S(2)}) collective-permute-start(f32[2,1,512,128]{2,3,0,1:T(8,128)} %copy.75), channel_id=1, source_target_pairs={{0,16},{16,0},{1,17},{17,1},{2,18},{18,2},{3,19},{19,3},{4,20},{20... | collective-permute-start | bytes 1572872 | tf_op jit(solution)/shard_map/ppermute | solution.py:234
  19.3 41.6 %collective-permute-start.11 = (f32[2,1,512,128]{2,3,0,1:T(8,128)}, f32[2,1,512,128]{2,3,0,1:T(8,128)}, u32[]{:S(2)}, u32[]{:S(2)}) collective-permute-start(f32[2,1,512,128]{2,3,0,1:T(8,128)} %copy.74), channel_id=1, source_target_pairs={{0,16},{16,0},{1,17},{17,1},{2,18},{18,2},{3,19},{19,3},{4,20},{20... | collective-permute-start | bytes 1572872 | tf_op jit(solution)/shard_map/ppermute | solution.py:234
  26.7 3.5 %copy-start.2 = (f32[2,1,512,128]{2,3,0,1:T(8,128)S(1)}, f32[2,1,512,128]{2,3,0,1:T(8,128)}, u32[]{:S(2)}) copy-start(f32[2,1,512,128]{2,3,0,1:T(8,128)} %copy.81) | copy-start | bytes 1572868
  28.1 34.6 %collective-permute-start.1 = (f32[128,512]{1,0:T(8,128)S(1)}, f32[128,512]{1,0:T(8,128)S(1)}, u32[]{:S(2)}, u32[]{:S(2)}) collective-permute-start(f32[128,512]{1,0:T(8,128)S(1)} %dynamic-slice_bitcast_fusion.2), channel_id=1, source_target_pairs={{0,2},{1,3},{2,0},{3,1},{4,6},{5,7},{6,4},{7,5},{8,10},{9,11},{10,... | collective-permute-start | bytes 786440 | tf_op jit(solution)/shard_map/ppermute | solution.py:137
  40.3 20.6 %copy-start.3 = (f32[2,1,512,128]{2,3,0,1:T(8,128)S(1)}, f32[2,1,512,128]{2,3,0,1:T(8,128)}, u32[]{:S(2)}) copy-start(f32[2,1,512,128]{2,3,0,1:T(8,128)} %copy.78) | copy-start | bytes 1572868
  62.8 6.6 %collective-permute-start.2 = (f32[32,512]{1,0:T(8,128)S(1)}, f32[32,512]{1,0:T(8,128)S(1)}, u32[]{:S(2)}, u32[]{:S(2)}) collective-permute-start(f32[32,512]{1,0:T(8,128)S(1)} %get-tuple-element.31), channel_id=1, source_target_pairs={{0,4},{4,8},{8,12},{12,0},{1,5},{5,9},{9,13},{13,1},{2,6},{6,10},{... | collective-permute-start | bytes 196616 | tf_op jit(solution)/shard_map/ppermute | solution.py:155
  64.7 7.1 %collective-permute-start.3 = (f32[32,512]{1,0:T(8,128)S(1)}, f32[32,512]{1,0:T(8,128)S(1)}, u32[]{:S(2)}, u32[]{:S(2)}) collective-permute-start(f32[32,512]{1,0:T(8,128)S(1)} %get-tuple-element.33), channel_id=1, source_target_pairs={{0,8},{4,12},{8,0},{12,4},{1,9},{5,13},{9,1},{13,5},{2,10},{6,14},... | collective-permute-start | bytes 196616 | tf_op jit(solution)/shard_map/ppermute | solution.py:155
  67.3 4.6 %collective-permute-start.4 = (f32[32,512]{1,0:T(8,128)S(1)}, f32[32,512]{1,0:T(8,128)S(1)}, u32[]{:S(2)}, u32[]{:S(2)}) collective-permute-start(f32[32,512]{1,0:T(8,128)S(1)} %get-tuple-element.32), channel_id=1, source_target_pairs={{0,12},{4,0},{8,4},{12,8},{1,13},{5,1},{9,5},{13,9},{2,14},{6,2},{... | collective-permute-start | bytes 196616 | tf_op jit(solution)/shard_map/ppermute | solution.py:155
  69.4 12.4 %collective-permute-start.15 = (f32[256,512]{1,0:T(8,128)}, f32[256,512]{1,0:T(8,128)}, u32[]{:S(2)}, u32[]{:S(2)}) collective-permute-start(f32[256,512]{1,0:T(8,128)} %dynamic-slice_bitcast_fusion), channel_id=1, source_target_pairs={{0,1},{1,0},{2,3},{3,2},{4,5},{5,4},{6,7},{7,6},{8,9},{9,8},{10,11... | collective-permute-start | bytes 1572872 | tf_op jit(solution)/shard_map/ppermute | solution.py:137
  71.9 4.3 %collective-permute-start.5 = (f32[32,512]{1,0:T(8,128)S(1)}, f32[32,512]{1,0:T(8,128)S(1)}, u32[]{:S(2)}, u32[]{:S(2)}) collective-permute-start(f32[32,512]{1,0:T(8,128)S(1)} %fusion.47), channel_id=1, source_target_pairs={{0,16},{16,0},{1,17},{17,1},{2,18},{18,2},{3,19},{19,3},{4,20},{20... | collective-permute-start | bytes 196616 | tf_op jit(solution)/shard_map/ppermute | solution.py:205
  76.2 9.8 %collective-permute-start.6 = (f32[32,1024]{1,0:T(8,128)S(1)}, f32[32,1024]{1,0:T(8,128)S(1)}, u32[]{:S(2)}, u32[]{:S(2)}) collective-permute-start(f32[32,1024]{1,0:T(8,128)S(1)} %pad_maximum_fusion.2), channel_id=1, source_target_pairs={{0,4},{4,8},{8,12},{12,0},{1,5},{5,9},{9,13},{13,1},{2,6},{6,10},{... | collective-permute-start | bytes 393224 | tf_op jit(solution)/shard_map/ppermute | solution.py:165
  77.9 20.2 %collective-permute-start.7 = (f32[32,1024]{1,0:T(8,128)S(1)}, f32[32,1024]{1,0:T(8,128)S(1)}, u32[]{:S(2)}, u32[]{:S(2)}) collective-permute-start(f32[32,1024]{1,0:T(8,128)S(1)} %pad_maximum_fusion.2), channel_id=1, source_target_pairs={{0,8},{4,12},{8,0},{12,4},{1,9},{5,13},{9,1},{13,5},{2,10},{6,14},... | collective-permute-start | bytes 393224 | tf_op jit(solution)/shard_map/ppermute | solution.py:165
  79.9 24.1 %collective-permute-start.8 = (f32[32,1024]{1,0:T(8,128)S(1)}, f32[32,1024]{1,0:T(8,128)S(1)}, u32[]{:S(2)}, u32[]{:S(2)}) collective-permute-start(f32[32,1024]{1,0:T(8,128)S(1)} %pad_maximum_fusion.2), channel_id=1, source_target_pairs={{0,12},{4,0},{8,4},{12,8},{1,13},{5,1},{9,5},{13,9},{2,14},{6,2},{... | collective-permute-start | bytes 393224 | tf_op jit(solution)/shard_map/ppermute | solution.py:165
  83.0 5.7 %collective-permute-start.16 = (f32[64,512]{1,0:T(8,128)S(1)}, f32[64,512]{1,0:T(8,128)S(1)}, u32[]{:S(2)}, u32[]{:S(2)}) collective-permute-start(f32[64,512]{1,0:T(8,128)S(1)} %get-tuple-element.28), channel_id=1, source_target_pairs={{0,16},{1,17},{2,18},{3,19},{16,0},{17,1},{18,2},{19,3},{4,20},{5,... | collective-permute-start | bytes 393224 | tf_op jit(solution)/shard_map/ppermute | solution.py:187
  84.6 5.4 %collective-permute-start.17 = (f32[64,512]{1,0:T(8,128)S(1)}, f32[64,512]{1,0:T(8,128)S(1)}, u32[]{:S(2)}, u32[]{:S(2)}) collective-permute-start(f32[64,512]{1,0:T(8,128)S(1)} %get-tuple-element.30), channel_id=1, source_target_pairs={{0,2},{1,3},{2,0},{3,1},{16,18},{17,19},{18,16},{19,17},{4,6},{5,7... | collective-permute-start | bytes 393224 | tf_op jit(solution)/shard_map/ppermute | solution.py:187
  86.1 5.9 %collective-permute-start.18 = (f32[64,512]{1,0:T(8,128)S(1)}, f32[64,512]{1,0:T(8,128)S(1)}, u32[]{:S(2)}, u32[]{:S(2)}) collective-permute-start(f32[64,512]{1,0:T(8,128)S(1)} %get-tuple-element.29), channel_id=1, source_target_pairs={{0,18},{1,19},{2,16},{3,17},{16,2},{17,3},{18,0},{19,1},{4,22},{5,... | collective-permute-start | bytes 393224 | tf_op jit(solution)/shard_map/ppermute | solution.py:187
  92.0 7.1 %collective-permute-start.19 = (f32[64,512]{1,0:T(8,128)S(1)}, f32[64,512]{1,0:T(8,128)S(1)}, u32[]{:S(2)}, u32[]{:S(2)}) collective-permute-start(f32[64,512]{1,0:T(8,128)S(1)} %fusion.45), channel_id=1, source_target_pairs={{0,4},{4,8},{8,12},{12,0},{1,5},{5,9},{9,13},{13,1},{2,6},{6,10},{... | collective-permute-start | bytes 393224 | tf_op jit(solution)/shard_map/ppermute | solution.py:191
  93.6 8.7 %collective-permute-start.20 = (f32[64,512]{1,0:T(8,128)S(1)}, f32[64,512]{1,0:T(8,128)S(1)}, u32[]{:S(2)}, u32[]{:S(2)}) collective-permute-start(f32[64,512]{1,0:T(8,128)S(1)} %fusion.45), channel_id=1, source_target_pairs={{0,8},{4,12},{8,0},{12,4},{1,9},{5,13},{9,1},{13,5},{2,10},{6,14},... | collective-permute-start | bytes 393224 | tf_op jit(solution)/shard_map/ppermute | solution.py:191
  95.2 7.1 %collective-permute-start.21 = (f32[64,512]{1,0:T(8,128)S(1)}, f32[64,512]{1,0:T(8,128)S(1)}, u32[]{:S(2)}, u32[]{:S(2)}) collective-permute-start(f32[64,512]{1,0:T(8,128)S(1)} %fusion.45), channel_id=1, source_target_pairs={{0,12},{4,0},{8,4},{12,8},{1,13},{5,1},{9,5},{13,9},{2,14},{6,2},{... | collective-permute-start | bytes 393224 | tf_op jit(solution)/shard_map/ppermute | solution.py:191
  103.9 5.0 %collective-permute-start.22 = (f32[64,512]{1,0:T(8,128)S(1)}, f32[64,512]{1,0:T(8,128)S(1)}, u32[]{:S(2)}, u32[]{:S(2)}) collective-permute-start(f32[64,512]{1,0:T(8,128)S(1)} %get-tuple-element.11), channel_id=1, source_target_pairs={{0,16},{1,17},{2,18},{3,19},{16,0},{17,1},{18,2},{19,3},{4,20},{5,... | collective-permute-start | bytes 393224 | tf_op jit(solution)/shard_map/ppermute | solution.py:197
  104.6 14.5 %collective-permute-start.9 = (f32[128,1024]{1,0:T(8,128)}, f32[128,1024]{1,0:T(8,128)S(1)}, u32[]{:S(2)}, u32[]{:S(2)}) collective-permute-start(f32[128,1024]{1,0:T(8,128)} %bitcast.21), channel_id=1, source_target_pairs={{0,2},{1,3},{2,0},{3,1},{4,6},{5,7},{6,4},{7,5},{8,10},{9,11},{10,... | collective-permute-start | bytes 1572872 | tf_op jit(solution)/shard_map/ppermute | solution.py:143
  105.4 13.0 %collective-permute-start.23 = (f32[64,512]{1,0:T(8,128)S(1)}, f32[64,512]{1,0:T(8,128)S(1)}, u32[]{:S(2)}, u32[]{:S(2)}) collective-permute-start(f32[64,512]{1,0:T(8,128)S(1)} %get-tuple-element.11), channel_id=1, source_target_pairs={{0,2},{1,3},{2,0},{3,1},{16,18},{17,19},{18,16},{19,17},{4,6},{5,7... | collective-permute-start | bytes 393224 | tf_op jit(solution)/shard_map/ppermute | solution.py:197
  106.6 15.4 %collective-permute-start.24 = (f32[64,512]{1,0:T(8,128)S(1)}, f32[64,512]{1,0:T(8,128)S(1)}, u32[]{:S(2)}, u32[]{:S(2)}) collective-permute-start(f32[64,512]{1,0:T(8,128)S(1)} %get-tuple-element.11), channel_id=1, source_target_pairs={{0,18},{1,19},{2,16},{3,17},{16,2},{17,3},{18,0},{19,1},{4,22},{5,... | collective-permute-start | bytes 393224 | tf_op jit(solution)/shard_map/ppermute | solution.py:197
  120.2 0.8 copy-start
  122.1 5.2 %collective-permute-start.10 = (f32[256,1024]{1,0:T(8,128)}, f32[256,1024]{1,0:T(8,128)}, u32[]{:S(2)}, u32[]{:S(2)}) collective-permute-start(f32[256,1024]{1,0:T(8,128)} %pad_maximum_fusion.1), channel_id=1, source_target_pairs={{0,1},{1,0},{2,3},{3,2},{4,5},{5,4},{6,7},{7,6},{8,9},{9,8},{10,11... | collective-permute-start | bytes 3145736 | tf_op jit(solution)/shard_map/ppermute | solution.py:143
  122.7 3.1 %collective-permute-start.25 = (f32[256,512]{1,0:T(8,128)}, f32[256,512]{1,0:T(8,128)}, u32[]{:S(2)}, u32[]{:S(2)}) collective-permute-start(f32[256,512]{1,0:T(8,128)} %bitcast.46), channel_id=1, source_target_pairs={{0,1},{1,0},{2,3},{3,2},{4,5},{5,4},{6,7},{7,6},{8,9},{9,8},{10,11... | collective-permute-start | bytes 1572872 | tf_op jit(solution)/shard_map/ppermute | solution.py:143
  124.5 2.8 %copy-start.1 = (f32[128,1024]{1,0:T(8,128)S(1)}, f32[128,1024]{1,0:T(8,128)}, u32[]{:S(2)}) copy-start(f32[128,1024]{1,0:T(8,128)} %copy-done) | copy-start | bytes 1572868
  165.8 21.2 %all-to-all-start = ((f32[8,1,128,128]{3,0,1,2:T(8,128)}), f32[8,1,128,128]{3,0,1,2:T(8,128)S(1)}, u32[]{:S(2)}, u32[]{:S(2)}) async-start(f32[8,1,128,128]{3,0,1,2:T(8,128)} %copy.58), calls=%async_computation | async-start | bytes 1048576 | tf_op jit(solution)/shard_map/all_to_all | solution.py:265

commit v2 on v1

v2 whole, which is shorter than its diff:
```python
import functools
import math

import jax
import jax.numpy as jnp
from jax import lax
from jax.experimental import pallas as pl
from jax.experimental.pallas import tpu as pltpu
from jax.sharding import PartitionSpec as P

ITERS = 3
PANEL = 8
SMALL = 1e-6
HIGHEST_PREC = lax.Precision.HIGHEST
HIGH_PREC = lax.Precision.HIGH


def mul(left, right):
    return lax.dot_general(
        left, right, (((1,), (0,)), ((), ())), precision=HIGHEST_PREC, preferred_element_type=jnp.float32
    )


def mul_t(left, right):
    return lax.dot_general(
        left, right, (((1,), (1,)), ((), ())), precision=HIGHEST_PREC, preferred_element_type=jnp.float32
    )


def inverse_factor(matrix):
    order = matrix.shape[0]
    panels = order // PANEL
    shape = (PANEL, order)
    sub = lax.broadcasted_iota(jnp.int32, shape, 0)
    lane = lax.broadcasted_iota(jnp.int32, shape, 1)
    rows = [matrix[PANEL * q : PANEL * (q + 1), :] for q in range(panels)]
    inverse = [jnp.where(lane == sub + PANEL * q, 1.0, 0.0).astype(jnp.float32) for q in range(panels)]
    for p in range(panels):
        columns = {
            q: [
                jnp.broadcast_to(rows[q][:, PANEL * p + j : PANEL * p + j + 1], shape)
                for j in range(PANEL)
            ]
            for q in range(p, panels)
        }
        for j in range(PANEL):
            scale = lax.rsqrt(jnp.broadcast_to(columns[p][j][j : j + 1, :], shape))
            factor = {q: columns[q][j] * scale for q in range(p, panels)}
            row = jnp.broadcast_to(rows[p][j : j + 1, :], shape) * scale
            inverse_row = jnp.broadcast_to(inverse[p][j : j + 1, :], shape) * scale
            for k in range(j + 1, PANEL):
                pivot = jnp.broadcast_to(factor[p][k : k + 1, :], shape)
                for q in range(p, panels):
                    columns[q][k] = columns[q][k] - factor[q] * pivot
            below = jnp.where(sub > j, factor[p], 0.0)
            rows[p] = rows[p] - below * row
            inverse[p] = jnp.where(sub == j, inverse_row, inverse[p] - below * inverse_row)
            for q in range(p + 1, panels):
                rows[q] = rows[q] - factor[q] * row
                inverse[q] = inverse[q] - factor[q] * inverse_row
    return jnp.concatenate(inverse, axis=0)


def inverse_factor_near_one(error, row, col):
    def lower(a):
        return jnp.where(row > col, a, jnp.where(row == col, 0.5 * a, 0.0))

    first = lower(error)
    eye = jnp.where(row == col, 1.0, 0.0)
    return eye - first + (lower(mul_t(first, first)) + mul(first, first))


def iterate(start_ref, basis_ref, gram_ref, inverse_ref):
    rank = start_ref.shape[0]
    row = lax.broadcasted_iota(jnp.int32, (rank, rank), 0)
    col = lax.broadcasted_iota(jnp.int32, (rank, rank), 1)
    basis_ref[...] = start_ref[...]

    def iteration(_, carry):
        mapped = mul(basis_ref[...], gram_ref[...])
        once = mul(inverse_factor(mul_t(mapped, mapped)), mapped)
        inner = mul_t(once, once)
        error = inner - jnp.where(row == col, 1.0, 0.0)
        small = jnp.sum(error * error) <= SMALL

        @pl.when(small)
        def _():
            inverse_ref[...] = inverse_factor_near_one(error, row, col)

        @pl.when(jnp.logical_not(small))
        def _():
            inverse_ref[...] = inverse_factor(inner)

        basis_ref[...] = mul(inverse_ref[...], once)
        return carry

    lax.fori_loop(0, ITERS, iteration, 0)


VMEM_SPEC = pl.BlockSpec(memory_space=pltpu.VMEM)
SMEM_SPEC = pl.BlockSpec(memory_space=pltpu.SMEM)


def params(mebibytes):
    return pltpu.CompilerParams(vmem_limit_bytes=mebibytes << 20)


def whole_kernel(gram_ref, start_ref, basis_ref, inverse_ref):
    iterate(start_ref, basis_ref, gram_ref, inverse_ref)


def subspace_whole(gram, start):
    rank, order = start.shape
    return pl.pallas_call(
        whole_kernel,
        out_shape=jax.ShapeDtypeStruct((rank, order), jnp.float32),
        in_specs=[VMEM_SPEC] * 2,
        out_specs=VMEM_SPEC,
        scratch_shapes=[pltpu.VMEM((rank, rank), jnp.float32)],
        compiler_params=params(24),
        name="subspace_whole",
    )(gram, start)


def pieces_kernel(scale, place_ref, *refs):
    own_refs, cross_refs = refs[:8], refs[8:16]
    start_ref, basis_ref, gram_ref, packed_ref, inverse_ref = refs[16:]
    x, y, core = place_ref[0], place_ref[1], place_ref[2]
    half = gram_ref.shape[0] // 2
    side = half // 2
    rows = own_refs[0].shape[0]
    for ref, (dc, dx, dy) in zip(own_refs, PIECES):
        at = pl.multiple_of(((core ^ dc) * 2 + (y ^ dy)) * rows, 8)
        packed_ref[x ^ dx, pl.ds(at, rows), :] = ref[...]
    rows = cross_refs[0].shape[0]
    for ref, (dc, dx, dy) in zip(cross_refs, PIECES):
        at = pl.multiple_of(((core ^ dc) * 4 + (x ^ dx) * 2 + (y ^ dy)) * rows, 8)
        gram_ref[pl.ds(at, rows), half:] = ref[...] * scale
    gram_ref[half:, :half] = gram_ref[:half, half:].T
    for p in range(2):
        base = p * half
        top = side // 2
        low = packed_ref[p, top:, :] * scale
        gram_ref[base : base + top, base : base + side] = packed_ref[p, :top, :side] * scale
        gram_ref[base + top : base + side, base : base + side] = packed_ref[p, :top, side:] * scale
        gram_ref[base + side : base + half, base : base + half] = low
        gram_ref[base : base + side, base + side : base + half] = low[:, :side].T
    iterate(start_ref, basis_ref, gram_ref, inverse_ref)


PIECES = [(dc, dx, dy) for dc in range(2) for dx, dy in ((0, 0), (1, 0), (0, 1), (1, 1))]


def subspace_pieces(place, own, cross, start, scale):
    rank, order = start.shape
    half = order // 2
    return pl.pallas_call(
        functools.partial(pieces_kernel, scale),
        out_shape=jax.ShapeDtypeStruct((rank, order), jnp.float32),
        in_specs=[SMEM_SPEC] + [VMEM_SPEC] * 17,
        out_specs=VMEM_SPEC,
        scratch_shapes=[
            pltpu.VMEM((order, order), jnp.float32),
            pltpu.VMEM((2, 3 * half // 4, half), jnp.float32),
            pltpu.VMEM((rank, rank), jnp.float32),
        ],
        compiler_params=params(56),
        name="subspace",
    )(place, *own, *cross, start)


def split(value):
    high = value.astype(jnp.bfloat16)
    return high, (value - high.astype(jnp.float32)).astype(jnp.bfloat16)


def dot3(left, right, contract):
    (a, b), (c, d) = left, right

    def dot(u, v):
        return lax.dot_general(u, v, (contract, ((), ())), preferred_element_type=jnp.float32)

    return dot(a, c) + (dot(a, d) + dot(b, c))


CORNERS = ((1, 0), (0, 1), (1, 1))
NN = ((1,), (0,))
NT = ((1,), (1,))


def pick(parts, rows):
    return parts[0][rows], parts[1][rows]


def own_kernel(place_ref, field_ref, keep_ref, send_ref, total_ref):
    half = field_ref.shape[2]
    side = half // 2
    top = side // 2
    values = split(jnp.concatenate([field_ref[s, 0] for s in range(field_ref.shape[0])], axis=1))
    upper = pick(values, slice(0, side))
    lower = pick(values, slice(side, half))

    @pl.when(pl.program_id(0) == 0)
    def _():
        total_ref[...] = jnp.zeros_like(total_ref)

    square = dot3(upper, upper, NT)
    total_ref[:top, :side] += square[:top]
    total_ref[:top, side:] += square[top:]
    total_ref[top:, :] += dot3(lower, values, NT)

    @pl.when(pl.program_id(0) == pl.num_programs(0) - 1)
    def _():
        rows = keep_ref.shape[0]
        core = place_ref[2]
        keep_ref[...] = total_ref[pl.ds(pl.multiple_of(core * rows, 8), rows), :]
        send_ref[...] = total_ref[pl.ds(pl.multiple_of((1 - core) * rows, 8), rows), :]


def own_blocks(place, field):
    half = field.shape[2]
    rows = 3 * half // 4
    step = math.gcd(field.shape[0], 4)
    shape = jax.ShapeDtypeStruct((rows // 2, half), jnp.float32)
    return pl.pallas_call(
        own_kernel,
        grid=(field.shape[0] // step,),
        out_shape=[shape, shape],
        in_specs=[SMEM_SPEC, pl.BlockSpec((step, 1, half, field.shape[3]), lambda i: (i, 0, 0, 0))],
        out_specs=[pl.BlockSpec((rows // 2, half), lambda i: (0, 0))] * 2,
        scratch_shapes=[pltpu.VMEM((rows, half), jnp.float32)],
        compiler_params=params(56),
        cost_estimate=pl.CostEstimate(flops=2 * 10**11, bytes_accessed=field.size * 4, transcendentals=0),
        name="own_blocks",
    )(place, field)


def species_pairs(refs):
    slots = [(i, s) for i, ref in enumerate(refs) for s in range(ref.shape[0])]
    return [slots[i : i + 2] for i in range(0, len(slots), 2)]


def cross_kernel(count, last, place_ref, *refs):
    got_refs, kept_refs = refs[:count], refs[count : 2 * count]
    refs = refs[2 * count :]
    x, core = place_ref[0], place_ref[2]
    half = got_refs[0].shape[2]
    rows = half // 2
    in_order = x == 0

    def product(at):
        total = None
        some, every = pl.ds(at, rows), slice(None)
        for pair in species_pairs(got_refs):
            def two(refs, where):
                return jnp.concatenate([refs[i][s, 0, where, :] for i, s in pair], axis=1)

            low = split(jnp.where(in_order, two(kept_refs, some), two(got_refs, some)))
            high = split(jnp.where(in_order, two(got_refs, every), two(kept_refs, every)))
            value = dot3(low, high, NT)
            total = value if total is None else total + value
        return total

    keep_at = pl.multiple_of(core * rows, 8)
    send_at = pl.multiple_of((1 - core) * rows, 8)
    if last:
        so_far_keep, so_far_send, keep_ref, send_ref = refs
        send_ref[...] = so_far_send[...] + product(send_at)
        keep_ref[...] = so_far_keep[...] + product(keep_at)
    else:
        keep_ref, send_ref = refs
        send_ref[...] = product(send_at)
        keep_ref[...] = product(keep_at)


def cross_block(place, got, kept, so_far):
    half = got[0].shape[2]
    shape = jax.ShapeDtypeStruct((half // 2, half), jnp.float32)
    return pl.pallas_call(
        functools.partial(cross_kernel, len(got), bool(so_far)),
        out_shape=[shape, shape],
        in_specs=[SMEM_SPEC] + [VMEM_SPEC] * (2 * len(got) + len(so_far)),
        out_specs=[VMEM_SPEC] * 2,
        compiler_params=params(24),
        name="cross_block",
    )(place, *got, *kept, *so_far)


def quarters_kernel(place_ref, left_ref, right_ref, *out_refs):
    rows = out_refs[0].shape[0]
    x, y = place_ref[0], place_ref[1]
    for ref, (dx, dy) in zip(out_refs, ((0, 0),) + CORNERS):
        some = pl.ds(pl.multiple_of(((x ^ dx) * 2 + (y ^ dy)) * rows, 8), rows)
        ref[...] = left_ref[some, :] + right_ref[some, :]


def sum_quarters(place, left, right):
    shape = jax.ShapeDtypeStruct((left.shape[0] // 4, left.shape[1]), jnp.float32)
    return pl.pallas_call(
        quarters_kernel,
        out_shape=[shape] * 4,
        in_specs=[SMEM_SPEC] + [VMEM_SPEC] * 2,
        out_specs=[VMEM_SPEC] * 4,
        compiler_params=params(24),
        name="quarters",
    )(place, left, right)


def project_kernel(count, place_ref, basis_ref, *refs):
    got_refs, kept_refs = refs[:count], refs[count : 2 * count]
    own_rows_ref, slab_refs, value_ref = refs[2 * count], refs[2 * count + 1 : -1], refs[-1]
    x, z, index = place_ref[0], place_ref[3], place_ref[4]
    half = got_refs[0].shape[2]
    width = got_refs[0].shape[3]
    near = split(basis_ref[:, pl.ds(pl.multiple_of(x * half, 128), half)])
    far = split(basis_ref[:, pl.ds(pl.multiple_of((1 - x) * half, 128), half)])
    slabs = len(slab_refs)
    rows = slab_refs[0].shape[2]
    for number, pair in enumerate(species_pairs(got_refs)):
        def two(refs):
            return split(jnp.concatenate([refs[i][s, 0] for i, s in pair], axis=1))

        value_ref[...] = dot3(near, two(kept_refs), NN) + dot3(far, two(got_refs), NN)
        for step in range(slabs):
            at = pl.multiple_of(lax.rem(z + step, slabs) * rows, 8)
            for j in range(len(pair)):
                slab_refs[step][2 * number + j, 0] = value_ref[
                    pl.ds(at, rows), width * j : width * (j + 1)
                ]
    count_rows = own_rows_ref.shape[0]
    per_tile = 128 // count_rows
    tile = basis_ref[:, pl.ds(pl.multiple_of(index // per_tile * 128, 128), 128)].T
    shift = lax.rem(index, per_tile)
    value_ref[:, :width] = tile
    own_rows_ref[...] = value_ref[pl.ds(pl.multiple_of(shift * count_rows, 8), count_rows), :width]


def project_slabs(place, basis, got, kept, slabs, own_rows):
    rank = basis.shape[0]
    species = sum(piece.shape[0] for piece in got)
    width = got[0].shape[3]
    slab = jax.ShapeDtypeStruct((species, 1, rank // slabs, width), jnp.float32)
    rows = jax.ShapeDtypeStruct((own_rows, rank), jnp.float32)
    return pl.pallas_call(
        functools.partial(project_kernel, len(got)),
        out_shape=[rows] + [slab] * slabs,
        in_specs=[SMEM_SPEC] + [VMEM_SPEC] * (1 + 2 * len(got)),
        out_specs=[VMEM_SPEC] * (1 + slabs),
        scratch_shapes=[pltpu.VMEM((rank, 2 * width), jnp.float32)],
        compiler_params=params(24),
        name="project",
    )(place, basis, *got, *kept)


def join_kernel(place_ref, *refs):
    out_ref = refs[-1]
    slabs = len(refs) - 1
    width = refs[0].shape[3]
    for step in range(slabs):
        source = lax.rem(place_ref[3] + slabs - step, slabs)
        out_ref[:, :, :, pl.ds(pl.multiple_of(source * width, 128), width)] = refs[step][...]


def join_slabs(place, slabs):
    shape = slabs[0].shape[:3] + (slabs[0].shape[3] * len(slabs),)
    return pl.pallas_call(
        join_kernel,
        out_shape=jax.ShapeDtypeStruct(shape, jnp.float32),
        in_specs=[SMEM_SPEC] + [VMEM_SPEC] * len(slabs),
        out_specs=VMEM_SPEC,
        compiler_params=params(24),
        name="join",
    )(place, *slabs)


def blocks(array, count):
    return array.reshape((count, array.shape[0] // count) + array.shape[1:])


def part(array, index):
    return lax.dynamic_index_in_dim(array, index, 0, keepdims=False)


def flip(size, bit):
    return [(i, i ^ bit) for i in range(size)]


def turn(size, step):
    return [(i, (i + step) % size) for i in range(size)]


def after(value, *others):
    return lax.optimization_barrier((value, others))[0]


def send_core(array):
    return lax.ppermute(array, "sa", flip(lax.axis_size("sa"), 1))


def send_corner(array, dx, dy):
    size = lax.axis_size("sa")
    pairs = [(x * size + s, (x ^ dx) * size + (s ^ (2 * dy))) for x in range(2) for s in range(size)]
    return lax.ppermute(array, ("gx", "sa"), pairs)


def sum_z(array):
    size = lax.axis_size("gy")
    shares = [lax.ppermute(array, "gy", turn(size, step)) for step in range(1, size)]
    return sum(shares, array)


def gather_pieces(array):
    near = [array] + [send_corner(array, dx, dy) for dx, dy in CORNERS]
    return near + [send_core(piece) for piece in near]


def chunk_sizes(species):
    return [3, species - 5, 2]


def on_halves(field, start):
    x = lax.axis_index("gx")
    y = lax.axis_index("sa") // 2
    core = lax.axis_index("sa") % 2
    z = lax.axis_index("gy")
    place = jnp.stack([x, y, core, z, lax.axis_index(("gx", "gy", "sa"))]).astype(jnp.int32)
    species = field.shape[0] // 2
    columns = field.shape[0] * field.shape[1] * field.shape[3]
    columns = columns * lax.axis_size("gy") * lax.axis_size("sa")
    sizes = chunk_sizes(species)
    starts = [sum(sizes[:i]) for i in range(len(sizes))]

    def chunk(source, owner, i):
        return lax.dynamic_slice_in_dim(source, owner * species + starts[i], sizes[i], 0)

    sent = [chunk(field, 1 - x, 0)]
    rest = after(field, sent[0])
    sent = sent + [chunk(rest, 1 - x, i) for i in range(1, len(sizes))]
    got = [lax.ppermute(piece, "gx", flip(2, 1)) for piece in sent]

    own_field = after(rest, sent)
    own_keep, own_send = own_blocks(place, own_field)
    own = blocks(own_keep + send_core(after(own_send, got[0])), 2)
    own = sum_z(part(own, y) + send_corner(part(own, 1 - y), 0, 1))

    kept = [chunk(own_field, x, i) for i in range(len(sizes))]
    start_t = start.T
    *early_got, final_got = got
    kept[0] = after(kept[0], start_t)
    so_far = cross_block(place, early_got, kept[:-1], ())
    final_got = after(final_got, own, so_far)
    cross_keep, cross_send = cross_block(place, [final_got], kept[-1:], so_far)
    cross, *shares = sum_quarters(place, cross_keep, send_core(cross_send))
    shares = [send_corner(share, dx, dy) for share, (dx, dy) in zip(shares, CORNERS)]
    cross = sum(shares, cross)
    own_pieces = gather_pieces(after(own, cross))
    cross_pieces = gather_pieces(sum_z(cross))

    basis = subspace_pieces(place, own_pieces, cross_pieces, start_t, 1.0 / columns)
    devices = lax.axis_size(("gx", "gy", "sa"))
    slabs = lax.axis_size("gy")
    own_rows, *projected = project_slabs(
        place, basis, early_got + [final_got], kept, slabs, start.shape[0] // devices
    )
    arrived = [projected[0]] + [
        lax.ppermute(projected[i], "gy", turn(slabs, i)) for i in range(1, slabs)
    ]
    return join_slabs(place, arrived), own_rows


def outer(left, right):
    return jnp.einsum(
        "stxy,stzy->xz", left, right, precision=HIGH_PREC, preferred_element_type=jnp.float32
    )


def on_fibres(field, start):
    axes = ("gx", "gy", "sa")
    fibres = lax.all_to_all(field, "gx", split_axis=0, concat_axis=2, tiled=True)
    columns = fibres.shape[0] * fibres.shape[1] * fibres.shape[3] * lax.axis_size(axes)
    gram = lax.psum(outer(fibres, fibres), axes) / columns
    basis = subspace_whole(gram, start.T)
    projected = jnp.einsum(
        "kx,stxy->stky", basis, fibres, precision=HIGH_PREC, preferred_element_type=jnp.float32
    )
    rows_dev = start.shape[0] // lax.axis_size(axes)
    own_rows = lax.dynamic_slice_in_dim(basis.T, lax.axis_index(axes) * rows_dev, rows_dev, 0)
    return lax.all_to_all(projected, "gy", split_axis=2, concat_axis=3, tiled=True), own_rows


def on_device(scalar_field, start_basis):
    if lax.axis_size("gx") == 2 and lax.axis_size("sa") == 4:
        return on_halves(scalar_field, start_basis)
    return on_fibres(scalar_field, start_basis)


def solution(mesh):
    placed = (P("sa", None, "gx", "gy"), P())
    return jax.shard_map(
        on_device,
        mesh=mesh,
        in_specs=placed,
        out_specs=(P(("sa", "gx"), None, "gy", None), P(("gx", "gy", "sa"), None)),
        check_vma=False,
    )
```

time: 189 us -> 152 us (0.80)
  matrix products: 18.3 us -> 0 us
  Pallas kernels: 31.3 us -> 49.5 us
  waiting for transfers between devices: 63.5 us -> 50.9 us
  local copies, waits for them, and re-layouts: 25.6 us -> 13.7 us
  other arithmetic: 9.31 us -> 2.14 us
  starting transfers between devices: 39.4 us -> 34.2 us
    dot_general x7 -> x0, matrix products: 18.3 us -> none  [the longest x5 13.9 us: outer(): jnp.einsum('stxy,stzy->xz', left, right, precision=HIGH_PREC, preferred_e...]
    pallas_call x1 -> x7, Pallas kernels: 31.3 us -> 49.5 us  [the longest x1 34 us: subspace_pieces(): pl.pallas_call(functools.partial(pieces_kernel, scale), out_shape=jax.Sha...]
    all_to_all x1 -> x0, waiting for transfers between devices: 14 us -> none  [on_device(): lax.all_to_all(projected, 'gy', split_axis=2, concat_axis=3, tiled=True)]
    unnamed x21 -> x39, local copies, waits for them, and re-layouts: 12.1 us -> 4.47 us
    dynamic_slice x2 -> x5, local copies, waits for them, and re-layouts: 1.82 us -> 8.55 us  [chunk(): lax.dynamic_slice_in_dim(source, owner * species + starts[i], sizes[i], 0)]
    all_to_all x1 -> x0, starting transfers between devices: 6.45 us -> none  [on_device(): lax.all_to_all(projected, 'gy', split_axis=2, concat_axis=3, tiled=True)]
    dynamic_update_slice x6 -> x0, local copies, waits for them, and re-layouts: 3.95 us -> none  [the longest x3 1.99 us: gather_turn(): out = lax.dynamic_update_index_in_dim(out, got, (mine - step) % size, 0)]
    select_n x3 -> x0, other arithmetic: 3.95 us -> none  [gather_flip(): low = jnp.where(mine == 0, array, got)]
  transfers between devices with their start and end apart: 27 -> 32, of which waited for: 15 -> 17; matrix products, arithmetic and copies ran while one was open for 19% -> 7% of each run, Pallas kernels for 0% -> 6%
where the time goes in v2:
time: 152 us; the launch traced here: 151 us
  waiting for transfers between devices  50.9 us (33%)
  Pallas kernels  49.5 us (33%)
  starting transfers between devices  34.2 us (23%)
  local copies, waits for them, and re-layouts  13.7 us (9%)
  other arithmetic  2.14 us (1%)
    pallas_call x1, Pallas kernels, subspace_pieces(): pl.pallas_call(functools.partial(pieces_kernel, scale), out_shape=jax.Sha...  34 us
    ppermute x10, waiting for transfers between devices, send_corner(): return lax.ppermute(array, ('gx', 'sa'), pairs)  16.5 us
    ppermute x6, waiting for transfers between devices, sum_z(): lax.ppermute(array, 'gy', turn(size, step))  13.8 us
    ppermute x10, starting transfers between devices, send_corner(): return lax.ppermute(array, ('gx', 'sa'), pairs)  13.3 us
    ppermute x6, starting transfers between devices, sum_z(): lax.ppermute(array, 'gy', turn(size, step))  9.55 us
    ppermute x3, waiting for transfers between devices, on_halves(): lax.ppermute(projected[i], 'gy', turn(slabs, i))  9.33 us
    dynamic_slice x5, local copies, waits for them, and re-layouts, chunk(): lax.dynamic_slice_in_dim(source, owner * species + starts[i], sizes[i], 0)  8.55 us
    ppermute x3, waiting for transfers between devices, on_halves(): got = [lax.ppermute(piece, 'gx', flip(2, 1)) for piece in sent]  7.87 us
  transfers between devices with their start and end apart: 32, of which 17 were waited for; matrix products, arithmetic and copies ran while one was open for 7% of the time, Pallas kernels for 6%

profile of v2, /device:TPU:0, one launch (start us, length us, event | category | flops | bytes accessed | tf_op | source)
XLA Modules:
  0.0 151.3 jit_solution(15437012876484744861)
XLA Ops:
  0.6 2.1 %constant_dynamic-slice_fusion.5 = f32[3,1,512,128]{3,2,1,0:T(8,128)} fusion(f32[16,1,512,128]{3,2,1,0:T(8,128)} %field_ref, s32[]{:T(128)S(6)} %select_n.38), kind=kLoop, calls=%fused_computation.10 | loop fusion | bytes 1572868 | tf_op jit(solution)/shard_map/dynamic_slice | solution.py:434
  2.7 2.9 %collective-permute-start = (f32[3,1,512,128]{3,2,1,0:T(8,128)}, f32[3,1,512,128]{3,2,1,0:T(8,128)}, u32[]{:S(2)}, u32[]{:S(2)}) collective-permute-start(f32[3,1,512,128]{3,2,1,0:T(8,128)} %constant_dynamic-slice_fusion.5), channel_id=1, source_target_pairs={{0,16},{16,0},{1,17},{17,1},{2,18},{18,2},{3,19},{19,3},{4,20},{20... | collective-permute-start | bytes 2359304 | tf_op jit(solution)/shard_map/ppermute | solution.py:439
  5.6 1.9 %constant_dynamic-slice_fusion.3 = f32[2,1,512,128]{3,2,1,0:T(8,128)} fusion(f32[16,1,512,128]{3,2,1,0:T(8,128)} %field_ref, s32[]{:T(128)S(6)} %select_n.40), kind=kLoop, calls=%fused_computation.8 | loop fusion | bytes 1048580 | tf_op jit(solution)/shard_map/dynamic_slice | solution.py:434
  7.5 2.1 %constant_dynamic-slice_fusion.4 = f32[3,1,512,128]{3,2,1,0:T(8,128)} fusion(f32[16,1,512,128]{3,2,1,0:T(8,128)} %field_ref, s32[]{:T(128)S(6)} %select_n.39), kind=kLoop, calls=%fused_computation.9 | loop fusion | bytes 1572868 | tf_op jit(solution)/shard_map/dynamic_slice | solution.py:434
  9.6 0.7 stack.23.place_ref
  10.3 6.6 %own_blocks.1 = (f32[192,512]{1,0:T(8,128)}, f32[192,512]{1,0:T(8,128)}) custom-call(s32[5]{0:T(128)} %stack.23.place_ref, f32[16,1,512,128]{3,2,1,0:T(8,128)} %field_ref), custom_call_target="tpu_custom_call" | custom-call | flops 199999995904 | bytes 4194304 | tf_op jit(solution)/shard_map/own_blocks/pallas_call | solution.py:225
  16.9 6.6 %collective-permute-done.refs_0_ = f32[3,1,512,128]{3,2,1,0:T(8,128)} collective-permute-done((f32[3,1,512,128]{3,2,1,0:T(8,128)}, f32[3,1,512,128]{3,2,1,0:T(8,128)}, u32[]{:S(2)}, u32[]{:S(2)}) %collective-permute-start) | collective-permute-done | bytes 786464 | tf_op jit(solution)/shard_map/ppermute | solution.py:439
  23.5 1.7 %collective-permute-start.7 = (f32[3,1,512,128]{3,2,1,0:T(8,128)}, f32[3,1,512,128]{3,2,1,0:T(8,128)S(1)}, u32[]{:S(2)}, u32[]{:S(2)}) collective-permute-start(f32[3,1,512,128]{3,2,1,0:T(8,128)} %constant_dynamic-slice_fusion.4), channel_id=1, source_target_pairs={{0,16},{16,0},{1,17},{17,1},{2,18},{18,2},{3,19},{19,3},{4,20},{20... | collective-permute-start | bytes 2359304 | tf_op jit(solution)/shard_map/ppermute | solution.py:439
  25.2 0.2 collective-permute-done.1
  25.4 1.1 add.98
  26.5 1.8 %collective-permute-start.2 = (f32[96,512]{1,0:T(8,128)S(1)}, f32[96,512]{1,0:T(8,128)S(1)}, u32[]{:S(2)}, u32[]{:S(2)}) collective-permute-start(f32[96,512]{1,0:T(8,128)S(1)} %dynamic-slice_bitcast_fusion), channel_id=1, source_target_pairs={{0,2},{1,3},{2,0},{3,1},{16,18},{17,19},{18,16},{19,17},{4,6},{5,7... | collective-permute-start | bytes 589832 | tf_op jit(solution)/shard_map/ppermute | solution.py:403
  28.4 1.5 collective-permute-start.6
  29.8 3.7 %collective-permute-done.2 = f32[96,512]{1,0:T(8,128)S(1)} collective-permute-done((f32[96,512]{1,0:T(8,128)S(1)}, f32[96,512]{1,0:T(8,128)S(1)}, u32[]{:S(2)}, u32[]{:S(2)}) %collective-permute-start.2) | collective-permute-done | bytes 196640 | tf_op jit(solution)/shard_map/ppermute | solution.py:403
  33.6 3.9 %collective-permute-start.5 = (f32[96,512]{1,0:T(8,128)S(1)}, f32[96,512]{1,0:T(8,128)S(1)}, u32[]{:S(2)}, u32[]{:S(2)}) collective-permute-start(f32[96,512]{1,0:T(8,128)S(1)} %bitcast_add_fusion), channel_id=1, source_target_pairs={{0,12},{4,0},{8,4},{12,8},{1,13},{5,1},{9,5},{13,9},{2,14},{6,2},{... | collective-permute-start | bytes 589832 | tf_op jit(solution)/shard_map/ppermute | solution.py:408
  37.5 1.0 collective-permute-start.3
  38.5 1.5 constant_dynamic-slice_fusion.1
  39.9 2.0 %copy.4 = f32[1024,128]{0,1:T(8,128)} copy(f32[1024,128]{1,0:T(8,128)} %param.3) | data formatting | bytes 1048576 | tf_op args[1]
  42.0 1.1 constant_dynamic-slice_fusion.refs_1_.refs_5_
  43.1 1.0 collective-permute-done.7.refs_1_
  44.1 2.6 %cross_block.2 = (f32[256,512]{1,0:T(8,128)S(1)}, f32[256,512]{1,0:T(8,128)S(1)}) custom-call(s32[5]{0:T(128)S(1)} %copy-done.1, f32[3,1,512,128]{3,2,1,0:T(8,128)} %collective-permute-done.refs_0_, f32[3,1,512,128]{3,2,1,0:T(8,128)S(1)} %collective-permute-done.7.refs_1_, f32[3,1,512,128]{3,2,1,0:T(8,128)S(1)} %get-tuple-element.28.refs_2_.refs_3_, ...), custom_call_target="tpu_custom_call" | custom-call | tf_op jit(solution)/shard_map/cross_block/pallas_call | solution.py:279
  46.7 7.0 %collective-permute-done.4 = f32[96,512]{1,0:T(8,128)S(1)} collective-permute-done((f32[96,512]{1,0:T(8,128)S(1)}, f32[96,512]{1,0:T(8,128)S(1)}, u32[]{:S(2)}, u32[]{:S(2)}) %collective-permute-start.4) | collective-permute-done | bytes 196640 | tf_op jit(solution)/shard_map/ppermute | solution.py:408
  53.6 1.0 add_add_fusion.refs_0_
  54.6 0.3 collective-permute-done.6.refs_0_.refs_2_
  54.9 1.2 cross_block.3
  56.2 0.1 collective-permute-start.8
  56.2 1.9 %collective-permute-done.8.right_ref = f32[256,512]{1,0:T(8,128)S(1)} collective-permute-done((f32[256,512]{1,0:T(8,128)S(1)}, f32[256,512]{1,0:T(8,128)S(1)}, u32[]{:S(2)}, u32[]{:S(2)}) %collective-permute-start.8) | collective-permute-done | bytes 524320 | tf_op jit(solution)/shard_map/ppermute | solution.py:397
  58.1 0.6 quarters.1
  58.7 1.8 %collective-permute-start.9 = (f32[64,512]{1,0:T(8,128)S(1)}, f32[64,512]{1,0:T(8,128)S(1)}, u32[]{:S(2)}, u32[]{:S(2)}) collective-permute-start(f32[64,512]{1,0:T(8,128)S(1)} %get-tuple-element.35), channel_id=1, source_target_pairs={{0,16},{1,17},{2,18},{3,19},{16,0},{17,1},{18,2},{19,3},{4,20},{5,... | collective-permute-start | bytes 393224 | tf_op jit(solution)/shard_map/ppermute | solution.py:403
  60.6 1.5 %collective-permute-start.10 = (f32[64,512]{1,0:T(8,128)S(1)}, f32[64,512]{1,0:T(8,128)S(1)}, u32[]{:S(2)}, u32[]{:S(2)}) collective-permute-start(f32[64,512]{1,0:T(8,128)S(1)} %get-tuple-element.36), channel_id=1, source_target_pairs={{0,2},{1,3},{2,0},{3,1},{16,18},{17,19},{18,16},{19,17},{4,6},{5,7... | collective-permute-start | bytes 393224 | tf_op jit(solution)/shard_map/ppermute | solution.py:403
  62.1 0.2 collective-permute-start.11
  62.3 2.2 %collective-permute-done.9 = f32[64,512]{1,0:T(8,128)S(1)} collective-permute-done((f32[64,512]{1,0:T(8,128)S(1)}, f32[64,512]{1,0:T(8,128)S(1)}, u32[]{:S(2)}, u32[]{:S(2)}) %collective-permute-start.9) | collective-permute-done | bytes 131104 | tf_op jit(solution)/shard_map/ppermute | solution.py:403
  64.5 4.2 %collective-permute-done.10 = f32[64,512]{1,0:T(8,128)S(1)} collective-permute-done((f32[64,512]{1,0:T(8,128)S(1)}, f32[64,512]{1,0:T(8,128)S(1)}, u32[]{:S(2)}, u32[]{:S(2)}) %collective-permute-start.10) | collective-permute-done | bytes 131104 | tf_op jit(solution)/shard_map/ppermute | solution.py:403
  68.7 3.7 %collective-permute-start.21 = (f32[64,512]{1,0:T(8,128)S(1)}, f32[64,512]{1,0:T(8,128)S(1)}, u32[]{:S(2)}, u32[]{:S(2)}) collective-permute-start(f32[64,512]{1,0:T(8,128)S(1)} %add_add_fusion.2), channel_id=1, source_target_pairs={{0,12},{4,0},{8,4},{12,8},{1,13},{5,1},{9,5},{13,9},{2,14},{6,2},{... | collective-permute-start | bytes 393224 | tf_op jit(solution)/shard_map/ppermute | solution.py:408
  72.3 1.0 collective-permute-start.19
  73.3 1.5 collective-permute-start.14
  74.8 1.4 collective-permute-done.21
  76.3 1.5 %collective-permute-start.13 = (f32[96,512]{1,0:T(8,128)S(1)}, f32[96,512]{1,0:T(8,128)S(1)}, u32[]{:S(2)}, u32[]{:S(2)}) collective-permute-start(f32[96,512]{1,0:T(8,128)S(1)} %add_add_fusion.refs_0_), channel_id=1, source_target_pairs={{0,2},{1,3},{2,0},{3,1},{16,18},{17,19},{18,16},{19,17},{4,6},{5,7... | collective-permute-start | bytes 589832 | tf_op jit(solution)/shard_map/ppermute | solution.py:403
  77.8 5.3 %collective-permute-done.20 = f32[64,512]{1,0:T(8,128)S(1)} collective-permute-done((f32[64,512]{1,0:T(8,128)S(1)}, f32[64,512]{1,0:T(8,128)S(1)}, u32[]{:S(2)}, u32[]{:S(2)}) %collective-permute-start.20) | collective-permute-done | bytes 131104 | tf_op jit(solution)/shard_map/ppermute | solution.py:408
  83.1 1.2 collective-permute-start.12
  84.4 1.8 %collective-permute-start.24 = (f32[64,512]{1,0:T(8,128)S(1)}, f32[64,512]{1,0:T(8,128)S(1)}, u32[]{:S(2)}, u32[]{:S(2)}) collective-permute-start(f32[64,512]{1,0:T(8,128)S(1)} %add_add_fusion.1.refs_8_), channel_id=1, source_target_pairs={{0,18},{1,19},{2,16},{3,17},{16,2},{17,3},{18,0},{19,1},{4,22},{5,... | collective-permute-start | bytes 393224 | tf_op jit(solution)/shard_map/ppermute | solution.py:403
  86.3 0.6 collective-permute-start.23
  86.8 1.2 collective-permute-start.22
  88.1 6.4 %collective-permute-done.24.refs_11_ = f32[64,512]{1,0:T(8,128)S(1)} collective-permute-done((f32[64,512]{1,0:T(8,128)S(1)}, f32[64,512]{1,0:T(8,128)S(1)}, u32[]{:S(2)}, u32[]{:S(2)}) %collective-permute-start.24) | collective-permute-done | bytes 131104 | tf_op jit(solution)/shard_map/ppermute | solution.py:403
  94.5 0.5 collective-permute-start.18
  95.0 0.1 collective-permute-start.17
  95.1 0.4 collective-permute-start.16
  95.5 0.1 collective-permute-start.27
  95.6 0.2 collective-permute-done.28.refs_15_
  95.8 0.2 collective-permute-start.26
  96.0 0.9 collective-permute-done.27.refs_14_
  96.9 0.3 collective-permute-done.26.refs_13_
  97.3 0.2 copy-done.17
  97.6 0.3 copy-done.18
  97.8 0.1 copy-done.9
  97.9 0.1 copy-done.10
  98.0 0.7 copy-done.11
  98.7 34.0 %subspace.1.basis_ref = f32[128,1024]{1,0:T(8,128)} custom-call(s32[5]{0:T(128)} %stack.23.place_ref, f32[96,512]{1,0:T(8,128)} %copy-done.3, f32[96,512]{1,0:T(8,128)} %copy-done.8, f32[96,512]{1,0:T(8,128)} %copy-done.7, f32[96,512]{1,0:T(8,128)} %copy-done.6, f32[96,512]{1,0:T(8,128)} %copy-done.5, f32[96,512]{1,0:T(8,128)} %copy-done.11, ...), custom_call_target="tpu_custom_call" | custom-call | tf_op jit(solution)/shard_map/subspace/pallas_call | solution.py:157
  132.7 1.0 copy-done
  133.7 3.0 %project.1 = (f32[32,128]{1,0:T(8,128)}, f32[8,1,32,128]{3,2,1,0:T(8,128)S(1)}, f32[8,1,32,128]{3,2,1,0:T(8,128)S(1)}, f32[8,1,32,128]{3,2,1,0:T(8,128)S(1)}, f32[8,1,32,128]{3,2,1,0:T(8,128)S(1)}) custom-call(s32[5]{0:T(128)S(1)} %copy-done.2, f32[128,1024]{1,0:T(8,128)S(1)} %copy-done, f32[3,1,512,128]{3,2,1,0:T(8,128)} %collective-permute-done.refs_0_, ...), custom_call_target="tpu_custom_call" | custom-call | tf_op jit(solution)/shard_map/project/pallas_call | solution.py:344
  136.8 1.4 collective-permute-start.29
  138.1 2.5 %collective-permute-start.31 = (f32[8,1,32,128]{3,2,1,0:T(8,128)S(1)}, f32[8,1,32,128]{3,2,1,0:T(8,128)S(1)}, u32[]{:S(2)}, u32[]{:S(2)}) collective-permute-start(f32[8,1,32,128]{3,2,1,0:T(8,128)S(1)} %get-tuple-element.42), channel_id=1, source_target_pairs={{0,12},{4,0},{8,4},{12,8},{1,13},{5,1},{9,5},{13,9},{2,14},{6,2},{... | collective-permute-start | bytes 393224 | tf_op jit(solution)/shard_map/ppermute | solution.py:466
  140.6 4.4 %collective-permute-done.29.refs_1_ = f32[8,1,32,128]{3,2,1,0:T(8,128)S(1)} collective-permute-done((f32[8,1,32,128]{3,2,1,0:T(8,128)S(1)}, f32[8,1,32,128]{3,2,1,0:T(8,128)S(1)}, u32[]{:S(2)}, u32[]{:S(2)}) %collective-permute-start.29) | collective-permute-done | bytes 131104 | tf_op jit(solution)/shard_map/ppermute | solution.py:466
  145.0 4.9 %collective-permute-done.30.refs_2_ = f32[8,1,32,128]{3,2,1,0:T(8,128)S(1)} collective-permute-done((f32[8,1,32,128]{3,2,1,0:T(8,128)S(1)}, f32[8,1,32,128]{3,2,1,0:T(8,128)S(1)}, u32[]{:S(2)}, u32[]{:S(2)}) %collective-permute-start.30) | collective-permute-done | bytes 131104 | tf_op jit(solution)/shard_map/ppermute | solution.py:466
  149.9 1.4 join.1
  (58 shorter events, 0.2 us)
Async XLA Ops:
  2.7 20.8 %collective-permute-start = (f32[3,1,512,128]{3,2,1,0:T(8,128)}, f32[3,1,512,128]{3,2,1,0:T(8,128)}, u32[]{:S(2)}, u32[]{:S(2)}) collective-permute-start(f32[3,1,512,128]{3,2,1,0:T(8,128)} %constant_dynamic-slice_fusion.5), channel_id=1, source_target_pairs={{0,16},{16,0},{1,17},{17,1},{2,18},{18,2},{3,19},{19,3},{4,20},{20... | collective-permute-start | bytes 2359304 | tf_op jit(solution)/shard_map/ppermute | solution.py:439
  16.9 27.2 %copy-start.1 = (s32[5]{0:T(128)S(1)}, s32[5]{0:T(128)}, u32[]{:S(2)}) copy-start(s32[5]{0:T(128)} %stack.23.place_ref) | copy-start | bytes 64
  23.5 1.9 %collective-permute-start.1 = (f32[192,512]{1,0:T(8,128)}, f32[192,512]{1,0:T(8,128)S(1)}, u32[]{:S(2)}, u32[]{:S(2)}) collective-permute-start(f32[192,512]{1,0:T(8,128)} %get-tuple-element.27), channel_id=1, source_target_pairs={{0,1},{1,0},{2,3},{3,2},{4,5},{5,4},{6,7},{7,6},{8,9},{9,8},{10,11... | collective-permute-start | bytes 1179656 | tf_op jit(solution)/shard_map/ppermute | solution.py:397
  23.5 20.5 %collective-permute-start.7 = (f32[3,1,512,128]{3,2,1,0:T(8,128)}, f32[3,1,512,128]{3,2,1,0:T(8,128)S(1)}, u32[]{:S(2)}, u32[]{:S(2)}) collective-permute-start(f32[3,1,512,128]{3,2,1,0:T(8,128)} %constant_dynamic-slice_fusion.4), channel_id=1, source_target_pairs={{0,16},{16,0},{1,17},{17,1},{2,18},{18,2},{3,19},{19,3},{4,20},{20... | collective-permute-start | bytes 2359304 | tf_op jit(solution)/shard_map/ppermute | solution.py:439
  26.5 7.0 %collective-permute-start.2 = (f32[96,512]{1,0:T(8,128)S(1)}, f32[96,512]{1,0:T(8,128)S(1)}, u32[]{:S(2)}, u32[]{:S(2)}) collective-permute-start(f32[96,512]{1,0:T(8,128)S(1)} %dynamic-slice_bitcast_fusion), channel_id=1, source_target_pairs={{0,2},{1,3},{2,0},{3,1},{16,18},{17,19},{18,16},{19,17},{4,6},{5,7... | collective-permute-start | bytes 589832 | tf_op jit(solution)/shard_map/ppermute | solution.py:403
  28.4 26.5 %collective-permute-start.6 = (f32[2,1,512,128]{3,2,1,0:T(8,128)}, f32[2,1,512,128]{3,2,1,0:T(8,128)S(1)}, u32[]{:S(2)}, u32[]{:S(2)}) collective-permute-start(f32[2,1,512,128]{3,2,1,0:T(8,128)} %constant_dynamic-slice_fusion.3), channel_id=1, source_target_pairs={{0,16},{16,0},{1,17},{17,1},{2,18},{18,2},{3,19},{19,3},{4,20},{20... | collective-permute-start | bytes 1572872 | tf_op jit(solution)/shard_map/ppermute | solution.py:439
  33.6 13.1 %collective-permute-start.5 = (f32[96,512]{1,0:T(8,128)S(1)}, f32[96,512]{1,0:T(8,128)S(1)}, u32[]{:S(2)}, u32[]{:S(2)}) collective-permute-start(f32[96,512]{1,0:T(8,128)S(1)} %bitcast_add_fusion), channel_id=1, source_target_pairs={{0,12},{4,0},{8,4},{12,8},{1,13},{5,1},{9,5},{13,9},{2,14},{6,2},{... | collective-permute-start | bytes 589832 | tf_op jit(solution)/shard_map/ppermute | solution.py:408
  37.5 16.2 %collective-permute-start.4 = (f32[96,512]{1,0:T(8,128)S(1)}, f32[96,512]{1,0:T(8,128)S(1)}, u32[]{:S(2)}, u32[]{:S(2)}) collective-permute-start(f32[96,512]{1,0:T(8,128)S(1)} %bitcast_add_fusion), channel_id=1, source_target_pairs={{0,8},{4,12},{8,0},{12,4},{1,9},{5,13},{9,1},{13,5},{2,10},{6,14},... | collective-permute-start | bytes 589832 | tf_op jit(solution)/shard_map/ppermute | solution.py:408
  37.5 16.2 %collective-permute-start.3 = (f32[96,512]{1,0:T(8,128)S(1)}, f32[96,512]{1,0:T(8,128)}, u32[]{:S(2)}, u32[]{:S(2)}) collective-permute-start(f32[96,512]{1,0:T(8,128)S(1)} %bitcast_add_fusion), channel_id=1, source_target_pairs={{0,4},{4,8},{8,12},{12,0},{1,5},{5,9},{9,13},{13,1},{2,6},{6,10},{... | collective-permute-start | bytes 589832 | tf_op jit(solution)/shard_map/ppermute | solution.py:408
  54.6 42.6 %copy-start.3 = (f32[96,512]{1,0:T(8,128)}, f32[96,512]{1,0:T(8,128)S(1)}, u32[]{:S(2)}) copy-start(f32[96,512]{1,0:T(8,128)S(1)} %add_add_fusion.refs_0_) | copy-start | bytes 589828
  54.6 78.0 %copy-start.2 = (s32[5]{0:T(128)S(1)}, s32[5]{0:T(128)}, u32[]{:S(2)}) copy-start(s32[5]{0:T(128)} %stack.23.place_ref) | copy-start | bytes 64
  56.2 2.0 %collective-permute-start.8 = (f32[256,512]{1,0:T(8,128)S(1)}, f32[256,512]{1,0:T(8,128)S(1)}, u32[]{:S(2)}, u32[]{:S(2)}) collective-permute-start(f32[256,512]{1,0:T(8,128)S(1)} %get-tuple-element.33), channel_id=1, source_target_pairs={{0,1},{1,0},{2,3},{3,2},{4,5},{5,4},{6,7},{7,6},{8,9},{9,8},{10,11... | collective-permute-start | bytes 1572872 | tf_op jit(solution)/shard_map/ppermute | solution.py:397
  58.7 5.7 %collective-permute-start.9 = (f32[64,512]{1,0:T(8,128)S(1)}, f32[64,512]{1,0:T(8,128)S(1)}, u32[]{:S(2)}, u32[]{:S(2)}) collective-permute-start(f32[64,512]{1,0:T(8,128)S(1)} %get-tuple-element.35), channel_id=1, source_target_pairs={{0,16},{1,17},{2,18},{3,19},{16,0},{17,1},{18,2},{19,3},{4,20},{5,... | collective-permute-start | bytes 393224 | tf_op jit(solution)/shard_map/ppermute | solution.py:403
  60.6 8.1 %collective-permute-start.10 = (f32[64,512]{1,0:T(8,128)S(1)}, f32[64,512]{1,0:T(8,128)S(1)}, u32[]{:S(2)}, u32[]{:S(2)}) collective-permute-start(f32[64,512]{1,0:T(8,128)S(1)} %get-tuple-element.36), channel_id=1, source_target_pairs={{0,2},{1,3},{2,0},{3,1},{16,18},{17,19},{18,16},{19,17},{4,6},{5,7... | collective-permute-start | bytes 393224 | tf_op jit(solution)/shard_map/ppermute | solution.py:403
  62.1 6.6 %collective-permute-start.11 = (f32[64,512]{1,0:T(8,128)S(1)}, f32[64,512]{1,0:T(8,128)S(1)}, u32[]{:S(2)}, u32[]{:S(2)}) collective-permute-start(f32[64,512]{1,0:T(8,128)S(1)} %get-tuple-element.37), channel_id=1, source_target_pairs={{0,18},{1,19},{2,16},{3,17},{16,2},{17,3},{18,0},{19,1},{4,22},{5,... | collective-permute-start | bytes 393224 | tf_op jit(solution)/shard_map/ppermute | solution.py:403
  68.7 7.6 %collective-permute-start.21 = (f32[64,512]{1,0:T(8,128)S(1)}, f32[64,512]{1,0:T(8,128)S(1)}, u32[]{:S(2)}, u32[]{:S(2)}) collective-permute-start(f32[64,512]{1,0:T(8,128)S(1)} %add_add_fusion.2), channel_id=1, source_target_pairs={{0,12},{4,0},{8,4},{12,8},{1,13},{5,1},{9,5},{13,9},{2,14},{6,2},{... | collective-permute-start | bytes 393224 | tf_op jit(solution)/shard_map/ppermute | solution.py:408
  72.3 10.8 %collective-permute-start.20 = (f32[64,512]{1,0:T(8,128)S(1)}, f32[64,512]{1,0:T(8,128)S(1)}, u32[]{:S(2)}, u32[]{:S(2)}) collective-permute-start(f32[64,512]{1,0:T(8,128)S(1)} %add_add_fusion.2), channel_id=1, source_target_pairs={{0,8},{4,12},{8,0},{12,4},{1,9},{5,13},{9,1},{13,5},{2,10},{6,14},... | collective-permute-start | bytes 393224 | tf_op jit(solution)/shard_map/ppermute | solution.py:408
  72.3 12.0 %collective-permute-start.19 = (f32[64,512]{1,0:T(8,128)S(1)}, f32[64,512]{1,0:T(8,128)S(1)}, u32[]{:S(2)}, u32[]{:S(2)}) collective-permute-start(f32[64,512]{1,0:T(8,128)S(1)} %add_add_fusion.2), channel_id=1, source_target_pairs={{0,4},{4,8},{8,12},{12,0},{1,5},{5,9},{9,13},{13,1},{2,6},{6,10},{... | collective-permute-start | bytes 393224 | tf_op jit(solution)/shard_map/ppermute | solution.py:408
  73.3 12.9 %collective-permute-start.15 = (f32[96,512]{1,0:T(8,128)S(1)}, f32[96,512]{1,0:T(8,128)S(1)}, u32[]{:S(2)}, u32[]{:S(2)}) collective-permute-start(f32[96,512]{1,0:T(8,128)S(1)} %add_add_fusion.refs_0_), channel_id=1, source_target_pairs={{0,1},{1,0},{2,3},{3,2},{4,5},{5,4},{6,7},{7,6},{8,9},{9,8},{10,11... | collective-permute-start | bytes 589832 | tf_op jit(solution)/shard_map/ppermute | solution.py:397
  73.3 12.9 %collective-permute-start.14 = (f32[96,512]{1,0:T(8,128)S(1)}, f32[96,512]{1,0:T(8,128)S(1)}, u32[]{:S(2)}, u32[]{:S(2)}) collective-permute-start(f32[96,512]{1,0:T(8,128)S(1)} %add_add_fusion.refs_0_), channel_id=1, source_target_pairs={{0,18},{1,19},{2,16},{3,17},{16,2},{17,3},{18,0},{19,1},{4,22},{5,... | collective-permute-start | bytes 589832 | tf_op jit(solution)/shard_map/ppermute | solution.py:403
  76.3 10.6 %collective-permute-start.13 = (f32[96,512]{1,0:T(8,128)S(1)}, f32[96,512]{1,0:T(8,128)S(1)}, u32[]{:S(2)}, u32[]{:S(2)}) collective-permute-start(f32[96,512]{1,0:T(8,128)S(1)} %add_add_fusion.refs_0_), channel_id=1, source_target_pairs={{0,2},{1,3},{2,0},{3,1},{16,18},{17,19},{18,16},{19,17},{4,6},{5,7... | collective-permute-start | bytes 589832 | tf_op jit(solution)/shard_map/ppermute | solution.py:403
  83.1 11.4 %collective-permute-start.12 = (f32[96,512]{1,0:T(8,128)S(1)}, f32[96,512]{1,0:T(8,128)S(1)}, u32[]{:S(2)}, u32[]{:S(2)}) collective-permute-start(f32[96,512]{1,0:T(8,128)S(1)} %add_add_fusion.refs_0_), channel_id=1, source_target_pairs={{0,16},{1,17},{2,18},{3,19},{16,0},{17,1},{18,2},{19,3},{4,20},{5,... | collective-permute-start | bytes 589832 | tf_op jit(solution)/shard_map/ppermute | solution.py:403
  84.4 12.8 %copy-start.4 = (f32[64,512]{1,0:T(8,128)}, f32[64,512]{1,0:T(8,128)S(1)}, u32[]{:S(2)}) copy-start(f32[64,512]{1,0:T(8,128)S(1)} %add_add_fusion.1.refs_8_) | copy-start | bytes 393220
  84.4 10.1 %collective-permute-start.24 = (f32[64,512]{1,0:T(8,128)S(1)}, f32[64,512]{1,0:T(8,128)S(1)}, u32[]{:S(2)}, u32[]{:S(2)}) collective-permute-start(f32[64,512]{1,0:T(8,128)S(1)} %add_add_fusion.1.refs_8_), channel_id=1, source_target_pairs={{0,18},{1,19},{2,16},{3,17},{16,2},{17,3},{18,0},{19,1},{4,22},{5,... | collective-permute-start | bytes 393224 | tf_op jit(solution)/shard_map/ppermute | solution.py:403
  86.2 11.0 %copy-start.5 = (f32[96,512]{1,0:T(8,128)}, f32[96,512]{1,0:T(8,128)S(1)}, u32[]{:S(2)}) copy-start(f32[96,512]{1,0:T(8,128)S(1)} %collective-permute-done.15.refs_4_) | copy-start | bytes 589828
  86.2 8.8 %collective-permute-start.25 = (f32[64,512]{1,0:T(8,128)S(1)}, f32[64,512]{1,0:T(8,128)S(1)}, u32[]{:S(2)}, u32[]{:S(2)}) collective-permute-start(f32[64,512]{1,0:T(8,128)S(1)} %add_add_fusion.1.refs_8_), channel_id=1, source_target_pairs={{0,1},{1,0},{2,3},{3,2},{4,5},{5,4},{6,7},{7,6},{8,9},{9,8},{10,11... | collective-permute-start | bytes 393224 | tf_op jit(solution)/shard_map/ppermute | solution.py:397
  86.2 11.0 %copy-start.6 = (f32[96,512]{1,0:T(8,128)}, f32[96,512]{1,0:T(8,128)S(1)}, u32[]{:S(2)}) copy-start(f32[96,512]{1,0:T(8,128)S(1)} %collective-permute-done.14.refs_3_) | copy-start | bytes 589828
  86.3 8.8 %collective-permute-start.23 = (f32[64,512]{1,0:T(8,128)S(1)}, f32[64,512]{1,0:T(8,128)S(1)}, u32[]{:S(2)}, u32[]{:S(2)}) collective-permute-start(f32[64,512]{1,0:T(8,128)S(1)} %add_add_fusion.1.refs_8_), channel_id=1, source_target_pairs={{0,2},{1,3},{2,0},{3,1},{16,18},{17,19},{18,16},{19,17},{4,6},{5,7... | collective-permute-start | bytes 393224 | tf_op jit(solution)/shard_map/ppermute | solution.py:403
  86.8 10.4 %copy-start.7 = (f32[96,512]{1,0:T(8,128)}, f32[96,512]{1,0:T(8,128)S(1)}, u32[]{:S(2)}) copy-start(f32[96,512]{1,0:T(8,128)S(1)} %collective-permute-done.13.refs_2_) | copy-start | bytes 589828
  86.8 8.7 %collective-permute-start.22 = (f32[64,512]{1,0:T(8,128)S(1)}, f32[64,512]{1,0:T(8,128)S(1)}, u32[]{:S(2)}, u32[]{:S(2)}) collective-permute-start(f32[64,512]{1,0:T(8,128)S(1)} %add_add_fusion.1.refs_8_), channel_id=1, source_target_pairs={{0,16},{1,17},{2,18},{3,19},{16,0},{17,1},{18,2},{19,3},{4,20},{5,... | collective-permute-start | bytes 393224 | tf_op jit(solution)/shard_map/ppermute | solution.py:403
  94.5 2.8 %copy-start.12 = (f32[64,512]{1,0:T(8,128)}, f32[64,512]{1,0:T(8,128)S(1)}, u32[]{:S(2)}) copy-start(f32[64,512]{1,0:T(8,128)S(1)} %collective-permute-done.24.refs_11_) | copy-start | bytes 393220
  94.5 1.3 collective-permute-start.28
  94.5 2.8 %copy-start.8 = (f32[96,512]{1,0:T(8,128)}, f32[96,512]{1,0:T(8,128)S(1)}, u32[]{:S(2)}) copy-start(f32[96,512]{1,0:T(8,128)S(1)} %collective-permute-done.12.refs_1_) | copy-start | bytes 589828
  94.5 2.7 %collective-permute-start.18 = (f32[96,512]{1,0:T(8,128)S(1)}, f32[96,512]{1,0:T(8,128)S(1)}, u32[]{:S(2)}, u32[]{:S(2)}) collective-permute-start(f32[96,512]{1,0:T(8,128)S(1)} %collective-permute-done.14.refs_3_), channel_id=1, source_target_pairs={{0,1},{1,0},{2,3},{3,2},{4,5},{5,4},{6,7},{7,6},{8,9},{9,8},{10,11... | collective-permute-start | bytes 589832 | tf_op jit(solution)/shard_map/ppermute | solution.py:397
  95.0 2.3 %copy-start.13 = (f32[64,512]{1,0:T(8,128)}, f32[64,512]{1,0:T(8,128)S(1)}, u32[]{:S(2)}) copy-start(f32[64,512]{1,0:T(8,128)S(1)} %collective-permute-done.25.refs_12_) | copy-start | bytes 393220
  95.0 2.2 %collective-permute-start.17 = (f32[96,512]{1,0:T(8,128)S(1)}, f32[96,512]{1,0:T(8,128)S(1)}, u32[]{:S(2)}, u32[]{:S(2)}) collective-permute-start(f32[96,512]{1,0:T(8,128)S(1)} %collective-permute-done.13.refs_2_), channel_id=1, source_target_pairs={{0,1},{1,0},{2,3},{3,2},{4,5},{5,4},{6,7},{7,6},{8,9},{9,8},{10,11... | collective-permute-start | bytes 589832 | tf_op jit(solution)/shard_map/ppermute | solution.py:397
  95.1 2.2 %copy-start.14 = (f32[64,512]{1,0:T(8,128)}, f32[64,512]{1,0:T(8,128)S(1)}, u32[]{:S(2)}) copy-start(f32[64,512]{1,0:T(8,128)S(1)} %collective-permute-done.23.refs_10_) | copy-start | bytes 393220
  95.1 2.1 %collective-permute-start.16 = (f32[96,512]{1,0:T(8,128)S(1)}, f32[96,512]{1,0:T(8,128)S(1)}, u32[]{:S(2)}, u32[]{:S(2)}) collective-permute-start(f32[96,512]{1,0:T(8,128)S(1)} %collective-permute-done.12.refs_1_), channel_id=1, source_target_pairs={{0,1},{1,0},{2,3},{3,2},{4,5},{5,4},{6,7},{7,6},{8,9},{9,8},{10,11... | collective-permute-start | bytes 589832 | tf_op jit(solution)/shard_map/ppermute | solution.py:397
  95.5 1.8 %copy-start.15 = (f32[64,512]{1,0:T(8,128)}, f32[64,512]{1,0:T(8,128)S(1)}, u32[]{:S(2)}) copy-start(f32[64,512]{1,0:T(8,128)S(1)} %collective-permute-done.22.refs_9_) | copy-start | bytes 393220
  95.5 1.4 collective-permute-start.27
  95.8 1.5 copy-start.16
  95.8 1.3 collective-permute-start.26
  96.9 0.7 copy-start.17
  97.2 0.7 copy-start.18
  97.2 0.7 copy-start.9
  97.2 0.8 copy-start.10
  98.0 0.7 copy-start.11
  132.7 1.0 copy-start
  136.8 8.3 %collective-permute-start.29 = (f32[8,1,32,128]{3,2,1,0:T(8,128)S(1)}, f32[8,1,32,128]{3,2,1,0:T(8,128)S(1)}, u32[]{:S(2)}, u32[]{:S(2)}) collective-permute-start(f32[8,1,32,128]{3,2,1,0:T(8,128)S(1)} %get-tuple-element.40), channel_id=1, source_target_pairs={{0,4},{4,8},{8,12},{12,0},{1,5},{5,9},{9,13},{13,1},{2,6},{6,10},{... | collective-permute-start | bytes 393224 | tf_op jit(solution)/shard_map/ppermute | solution.py:466
  138.1 11.8 %collective-permute-start.30 = (f32[8,1,32,128]{3,2,1,0:T(8,128)S(1)}, f32[8,1,32,128]{3,2,1,0:T(8,128)S(1)}, u32[]{:S(2)}, u32[]{:S(2)}) collective-permute-start(f32[8,1,32,128]{3,2,1,0:T(8,128)S(1)} %get-tuple-element.41), channel_id=1, source_target_pairs={{0,8},{4,12},{8,0},{12,4},{1,9},{5,13},{9,1},{13,5},{2,10},{6,14},... | collective-permute-start | bytes 393224 | tf_op jit(solution)/shard_map/ppermute | solution.py:466
  138.1 11.8 %collective-permute-start.31 = (f32[8,1,32,128]{3,2,1,0:T(8,128)S(1)}, f32[8,1,32,128]{3,2,1,0:T(8,128)S(1)}, u32[]{:S(2)}, u32[]{:S(2)}) collective-permute-start(f32[8,1,32,128]{3,2,1,0:T(8,128)S(1)} %get-tuple-element.42), channel_id=1, source_target_pairs={{0,12},{4,0},{8,4},{12,8},{1,13},{5,1},{9,5},{13,9},{2,14},{6,2},{... | collective-permute-start | bytes 393224 | tf_op jit(solution)/shard_map/ppermute | solution.py:466

commit v3 on v2

--- a/solution.py
+++ b/solution.py
@@ -9,8 +9,13 @@
 from jax.sharding import PartitionSpec as P
 
 ITERS = 3
+CORNERS = ((1, 0), (0, 1), (1, 1))
 PANEL = 8
+AHEAD = 3
 SMALL = 1e-6
+MEDIUM = 4e-4
+NN = ((1,), (0,))
+NT = ((1,), (1,))
 HIGHEST_PREC = lax.Precision.HIGHEST
 HIGH_PREC = lax.Precision.HIGH
 
@@ -25,6 +30,13 @@
     return lax.dot_general(
         left, right, (((1,), (1,)), ((), ())), precision=HIGHEST_PREC, preferred_element_type=jnp.float32
     )
+
+
+def three_parts(value):
+    high = value.astype(jnp.bfloat16)
+    rest = value - high.astype(jnp.float32)
+    middle = rest.astype(jnp.bfloat16)
+    return high, middle, (rest - middle.astype(jnp.float32)).astype(jnp.bfloat16)
 
 
 def inverse_factor(matrix):
@@ -34,64 +46,122 @@
     sub = lax.broadcasted_iota(jnp.int32, shape, 0)
     lane = lax.broadcasted_iota(jnp.int32, shape, 1)
     rows = [matrix[PANEL * q : PANEL * (q + 1), :] for q in range(panels)]
-    inverse = [jnp.where(lane == sub + PANEL * q, 1.0, 0.0).astype(jnp.float32) for q in range(panels)]
+
+    def spread(q, p):
+        return [
+            jnp.broadcast_to(rows[q][:, PANEL * p + j : PANEL * p + j + 1], shape) for j in range(PANEL)
+        ]
+
+    def sublane(value, k):
+        return jnp.broadcast_to(value[k : k + 1, :], shape)
+
+    following = spread(0, 0)
     for p in range(panels):
-        columns = {
-            q: [
-                jnp.broadcast_to(rows[q][:, PANEL * p + j : PANEL * p + j + 1], shape)
-                for j in range(PANEL)
-            ]
-            for q in range(p, panels)
-        }
+        near = list(range(p + 1, min(p + 1 + AHEAD, panels)))
+        columns = {q: spread(q, p) for q in near}
+        columns[p] = following
+        following = spread(p + 1, p + 1) if near else []
+        inside = (lane >= PANEL * p) & (lane < PANEL * (p + 1))
+        rows[p] = jnp.where(inside, jnp.where(lane == sub + PANEL * p, 1.0, 0.0), rows[p])
+        for q in range(p + 1, panels):
+            rows[q] = jnp.where(inside, 0.0, rows[q])
         for j in range(PANEL):
-            scale = lax.rsqrt(jnp.broadcast_to(columns[p][j][j : j + 1, :], shape))
-            factor = {q: columns[q][j] * scale for q in range(p, panels)}
-            row = jnp.broadcast_to(rows[p][j : j + 1, :], shape) * scale
-            inverse_row = jnp.broadcast_to(inverse[p][j : j + 1, :], shape) * scale
+            scale = lax.rsqrt(sublane(columns[p][j], j))
+            factor = {q: columns[q][j] * scale for q in [p] + near}
+            row = sublane(rows[p], j) * scale
             for k in range(j + 1, PANEL):
-                pivot = jnp.broadcast_to(factor[p][k : k + 1, :], shape)
-                for q in range(p, panels):
+                pivot = sublane(factor[p], k)
+                for q in [p] + near:
                     columns[q][k] = columns[q][k] - factor[q] * pivot
+            for k in range(len(following)):
+                following[k] = following[k] - factor[p + 1] * sublane(factor[p + 1], k)
             below = jnp.where(sub > j, factor[p], 0.0)
-            rows[p] = rows[p] - below * row
-            inverse[p] = jnp.where(sub == j, inverse_row, inverse[p] - below * inverse_row)
-            for q in range(p + 1, panels):
+            rows[p] = jnp.where(sub == j, row, rows[p] - below * row)
+            for q in near:
                 rows[q] = rows[q] - factor[q] * row
-                inverse[q] = inverse[q] - factor[q] * inverse_row
-    return jnp.concatenate(inverse, axis=0)
+        if p + 1 + AHEAD < panels:
+            high, middle, low = (part.astype(jnp.float32) for part in three_parts(rows[p]))
+            left = jnp.concatenate([high, high, high, middle, middle, low], axis=0)
+            right = jnp.concatenate([high, middle, low, high, middle, high], axis=0)
+            update = lax.dot_general(
+                left.astype(jnp.bfloat16),
+                right.astype(jnp.bfloat16),
+                (((0,), (0,)), ((), ())),
+                preferred_element_type=jnp.float32,
+            )
+            for q in range(p + 1 + AHEAD, panels):
+                rows[q] = rows[q] - update[PANEL * q : PANEL * (q + 1), :]
+    return jnp.concatenate(
+        [jnp.where(lane <= sub + PANEL * q, rows[q], 0.0) for q in range(panels)], axis=0
+    )
+
+
+def lower(matrix, row, col):
+    return jnp.where(row > col, matrix, jnp.where(row == col, 0.5 * matrix, 0.0))
 
 
 def inverse_factor_near_one(error, row, col):
-    def lower(a):
-        return jnp.where(row > col, a, jnp.where(row == col, 0.5 * a, 0.0))
-
-    first = lower(error)
+    first = lower(error, row, col)
     eye = jnp.where(row == col, 1.0, 0.0)
-    return eye - first + (lower(mul_t(first, first)) + mul(first, first))
-
-
-def iterate(start_ref, basis_ref, gram_ref, inverse_ref):
+    return eye - first + (lower(mul_t(first, first), row, col) + mul(first, first))
+
+
+def dot_t(left, right):
+    return lax.dot_general(left, right, (NT, ((), ())), preferred_element_type=jnp.float32)
+
+
+def inner_products(value):
+    high, middle, low = three_parts(value)
+    mixed = dot_t(high, middle) + dot_t(high, low)
+    return dot_t(high, high) + ((mixed + mixed.T) + dot_t(middle, middle))
+
+
+def apply(factor, value):
+    a, b, c = three_parts(factor)
+    high, middle, low = three_parts(value)
+
+    def pass_of(left, right):
+        return lax.dot_general(
+            jnp.concatenate(left, axis=1),
+            jnp.concatenate(right, axis=0),
+            (NN, ((), ())),
+            preferred_element_type=jnp.float32,
+        )
+
+    return pass_of([a, b], [high, middle]) + (
+        pass_of([a, b], [middle, high]) + pass_of([a, c], [low, high])
+    )
+
+
+def iterate(scale, start_ref, basis_ref, gram_ref, inverse_ref):
     rank = start_ref.shape[0]
     row = lax.broadcasted_iota(jnp.int32, (rank, rank), 0)
     col = lax.broadcasted_iota(jnp.int32, (rank, rank), 1)
+    eye = jnp.where(row == col, 1.0, 0.0)
     basis_ref[...] = start_ref[...]
 
     def iteration(_, carry):
-        mapped = mul(basis_ref[...], gram_ref[...])
-        once = mul(inverse_factor(mul_t(mapped, mapped)), mapped)
-        inner = mul_t(once, once)
-        error = inner - jnp.where(row == col, 1.0, 0.0)
-        small = jnp.sum(error * error) <= SMALL
-
-        @pl.when(small)
+        mapped = mul(basis_ref[...], gram_ref[...]) * scale
+        once = apply(inverse_factor(inner_products(mapped)), mapped)
+        inner = inner_products(once)
+        error = inner - eye
+        size = jnp.sum(error * error)
+
+        @pl.when(size <= MEDIUM)
         def _():
             inverse_ref[...] = inverse_factor_near_one(error, row, col)
 
-        @pl.when(jnp.logical_not(small))
+        @pl.when(jnp.logical_and(size > SMALL, size <= MEDIUM))
+        def _():
+            about = inverse_ref[...]
+            rest = mul_t(mul(about, inner), about) - eye
+            inverse_ref[...] = about - mul(lower(rest, row, col), about)
+
+        @pl.when(jnp.logical_not(size <= MEDIUM))
         def _():
             inverse_ref[...] = inverse_factor(inner)
 
-        basis_ref[...] = mul(inverse_ref[...], once)
+        basis_ref[...] = apply(inverse_ref[...], once)
         return carry
 
     lax.fori_loop(0, ITERS, iteration, 0)
@@ -99,6 +169,7 @@
 
 VMEM_SPEC = pl.BlockSpec(memory_space=pltpu.VMEM)
 SMEM_SPEC = pl.BlockSpec(memory_space=pltpu.SMEM)
+ANY_SPEC = pl.BlockSpec(memory_space=pl.ANY)
 
 
 def params(mebibytes):
@@ -106,7 +177,7 @@
 
 
 def whole_kernel(gram_ref, start_ref, basis_ref, inverse_ref):
-    iterate(start_ref, basis_ref, gram_ref, inverse_ref)
+    iterate(1.0, start_ref, basis_ref, gram_ref, inverse_ref)
 
 
 def subspace_whole(gram, start):
@@ -124,28 +195,47 @@
 
 def pieces_kernel(scale, place_ref, *refs):
     own_refs, cross_refs = refs[:8], refs[8:16]
-    start_ref, basis_ref, gram_ref, packed_ref, inverse_ref = refs[16:]
+    start_ref, basis_ref, gram_ref, packed_ref, inverse_ref, sems = refs[16:]
     x, y, core = place_ref[0], place_ref[1], place_ref[2]
     half = gram_ref.shape[0] // 2
-    side = half // 2
-    rows = own_refs[0].shape[0]
-    for ref, (dc, dx, dy) in zip(own_refs, PIECES):
+    own_copies, cross_copies = [], []
+    for index, (dc, dx, dy) in enumerate(PIECES):
+        rows = own_refs[index].shape[0]
         at = pl.multiple_of(((core ^ dc) * 2 + (y ^ dy)) * rows, 8)
-        packed_ref[x ^ dx, pl.ds(at, rows), :] = ref[...]
-    rows = cross_refs[0].shape[0]
-    for ref, (dc, dx, dy) in zip(cross_refs, PIECES):
+        own_copies.append(
+            pltpu.make_async_copy(
+                own_refs[index], packed_ref.at[x ^ dx, pl.ds(at, rows), :], sems.at[index]
+            )
+        )
+        rows = cross_refs[index].shape[0]
         at = pl.multiple_of(((core ^ dc) * 4 + (x ^ dx) * 2 + (y ^ dy)) * rows, 8)
-        gram_ref[pl.ds(at, rows), half:] = ref[...] * scale
+        cross_copies.append(
+            pltpu.make_async_copy(
+                cross_refs[index], gram_ref.at[pl.ds(at, rows), half:], sems.at[8 + index]
+            )
+        )
+    for copy in own_copies + cross_copies:
+        copy.start()
+    for copy in own_copies:
+        copy.wait()
+    side = half // 4
+    for p in range(2):
+        at = [p * half + side * i for i in range(5)]
+        last = packed_ref[p, :side, :]
+        third = packed_ref[p, side : 2 * side, :]
+        gram_ref[at[3] : at[4], at[0] : at[4]] = last
+        gram_ref[at[0] : at[3], at[3] : at[4]] = last[:, : 3 * side].T
+        gram_ref[at[2] : at[3], at[0] : at[3]] = third[:, : 3 * side]
+        gram_ref[at[0] : at[2], at[2] : at[3]] = third[:, : 2 * side].T
+        gram_ref[at[0] : at[1], at[0] : at[1]] = third[:, 3 * side :]
+        second = packed_ref[p, 2 * side :, :]
+        second = jnp.concatenate([second[:, : 2 * side], second[:, 2 * side :]], axis=0)
+        gram_ref[at[1] : at[2], at[0] : at[2]] = second
+        gram_ref[at[0] : at[1], at[1] : at[2]] = second[:, :side].T
+    for copy in cross_copies:
+        copy.wait()
     gram_ref[half:, :half] = gram_ref[:half, half:].T
-    for p in range(2):
-        base = p * half
-        top = side // 2
-        low = packed_ref[p, top:, :] * scale
-        gram_ref[base : base + top, base : base + side] = packed_ref[p, :top, :side] * scale
-        gram_ref[base + top : base + side, base : base + side] = packed_ref[p, :top, side:] * scale
-        gram_ref[base + side : base + half, base : base + half] = low
-        gram_ref[base : base + side, base + side : base + half] = low[:, :side].T
-    iterate(start_ref, basis_ref, gram_ref, inverse_ref)
+    iterate(scale, start_ref, basis_ref, gram_ref, inverse_ref)
 
 
 PIECES = [(dc, dx, dy) for dc in range(2) for dx, dy in ((0, 0), (1, 0), (0, 1), (1, 1))]
@@ -157,14 +247,15 @@
     return pl.pallas_call(
         functools.partial(pieces_kernel, scale),
         out_shape=jax.ShapeDtypeStruct((rank, order), jnp.float32),
-        in_specs=[SMEM_SPEC] + [VMEM_SPEC] * 17,
+        in_specs=[SMEM_SPEC] + [ANY_SPEC] * 16 + [VMEM_SPEC],
         out_specs=VMEM_SPEC,
         scratch_shapes=[
             pltpu.VMEM((order, order), jnp.float32),
-            pltpu.VMEM((2, 3 * half // 4, half), jnp.float32),
+            pltpu.VMEM((2, 5 * half // 8, half), jnp.float32),
             pltpu.VMEM((rank, rank), jnp.float32),
+            pltpu.SemaphoreType.DMA((16,)),
         ],
-        compiler_params=params(56),
+        compiler_params=params(16),
         name="subspace",
     )(place, *own, *cross, start)
 
@@ -183,31 +274,26 @@
     return dot(a, c) + (dot(a, d) + dot(b, c))
 
 
-CORNERS = ((1, 0), (0, 1), (1, 1))
-NN = ((1,), (0,))
-NT = ((1,), (1,))
-
-
 def pick(parts, rows):
     return parts[0][rows], parts[1][rows]
 
 
 def own_kernel(place_ref, field_ref, keep_ref, send_ref, total_ref):
     half = field_ref.shape[2]
-    side = half // 2
-    top = side // 2
+    side = half // 4
     values = split(jnp.concatenate([field_ref[s, 0] for s in range(field_ref.shape[0])], axis=1))
-    upper = pick(values, slice(0, side))
-    lower = pick(values, slice(side, half))
 
     @pl.when(pl.program_id(0) == 0)
     def _():
         total_ref[...] = jnp.zeros_like(total_ref)
 
-    square = dot3(upper, upper, NT)
-    total_ref[:top, :side] += square[:top]
-    total_ref[:top, side:] += square[top:]
-    total_ref[top:, :] += dot3(lower, values, NT)
+    upper = dot3(pick(values, slice(0, 2 * side)), pick(values, slice(0, 2 * side)), NT)
+    below = dot3(pick(values, slice(2 * side, half)), values, NT)
+    total_ref[:side, :] += below[side:]
+    total_ref[side : 2 * side, : 3 * side] += below[:side, : 3 * side]
+    total_ref[side : 2 * side, 3 * side :] += upper[:side, :side]
+    total_ref[2 * side :, : 2 * side] += upper[side : side + side // 2]
+    total_ref[2 * side :, 2 * side :] += upper[side + side // 2 :]
 
     @pl.when(pl.program_id(0) == pl.num_programs(0) - 1)
     def _():
@@ -219,7 +305,7 @@
 
 def own_blocks(place, field):
     half = field.shape[2]
-    rows = 3 * half // 4
+    rows = 5 * half // 8
     step = math.gcd(field.shape[0], 4)
     shape = jax.ShapeDtypeStruct((rows // 2, half), jnp.float32)
     return pl.pallas_call(
@@ -403,10 +489,10 @@
     return lax.ppermute(array, ("gx", "sa"), pairs)
 
 
-def sum_z(array):
+def sum_z(array, *others):
     size = lax.axis_size("gy")
     shares = [lax.ppermute(array, "gy", turn(size, step)) for step in range(1, size)]
-    return sum(shares, array)
+    return sum(after(shares, others), array)
 
 
 def gather_pieces(array):
@@ -440,21 +526,25 @@
 
     own_field = after(rest, sent)
     own_keep, own_send = own_blocks(place, own_field)
-    own = blocks(own_keep + send_core(after(own_send, got[0])), 2)
-    own = sum_z(part(own, y) + send_corner(part(own, 1 - y), 0, 1))
-
+    own = blocks(after(own_keep + send_core(own_send), got[0]), 2)
+    own = part(own, y) + send_corner(part(own, 1 - y), 0, 1)
     kept = [chunk(own_field, x, i) for i in range(len(sizes))]
     start_t = start.T
     *early_got, final_got = got
-    kept[0] = after(kept[0], start_t)
     so_far = cross_block(place, early_got, kept[:-1], ())
-    final_got = after(final_got, own, so_far)
+    own = sum_z(own, so_far, kept, start_t)
+    beside = send_corner(own, 0, 1)
+
+    final_got = after(final_got, beside)
     cross_keep, cross_send = cross_block(place, [final_got], kept[-1:], so_far)
     cross, *shares = sum_quarters(place, cross_keep, send_core(cross_send))
     shares = [send_corner(share, dx, dy) for share, (dx, dy) in zip(shares, CORNERS)]
+    own, beside = after((own, beside), shares[0])
     cross = sum(shares, cross)
-    own_pieces = gather_pieces(after(own, cross))
-    cross_pieces = gather_pieces(sum_z(cross))
+    far, far_beside = send_corner(own, 1, 0), send_corner(beside, 1, 0)
+    own_pieces = [own, far, beside, far_beside]
+    own_pieces = own_pieces + [send_core(piece) for piece in own_pieces]
+    cross_pieces = gather_pieces(sum_z(cross, far, far_beside))
 
     basis = subspace_pieces(place, own_pieces, cross_pieces, start_t, 1.0 / columns)
     devices = lax.axis_size(("gx", "gy", "sa"))

time: 152 us -> 134 us (0.88)
  Pallas kernels: 49.5 us -> 39.4 us
  waiting for transfers between devices: 50.9 us -> 47 us
  local copies, waits for them, and re-layouts: 13.7 us -> 10.5 us
  starting transfers between devices: 34.2 us -> 32.5 us
    pallas_call x1, Pallas kernels: 34 us -> 23.7 us  [subspace_pieces(): pl.pallas_call(functools.partial(pieces_kernel, scale), out_shape=jax.Sha...]
    unnamed x39 -> x3, local copies, waits for them, and re-layouts: 4.47 us -> 1.24 us
    ppermute x10, waiting for transfers between devices: 16.5 us -> 13.8 us  [send_corner(): return lax.ppermute(array, ('gx', 'sa'), pairs)]
    ppermute x3, starting transfers between devices: 6.17 us -> 4.47 us  [on_halves(): got = [lax.ppermute(piece, 'gx', flip(2, 1)) for piece in sent]]
    ppermute x6, waiting for transfers between devices: 13.8 us -> 12.2 us  [sum_z(): lax.ppermute(array, 'gy', turn(size, step))]
  transfers between devices with their start and end apart: 32 -> 32, of which waited for: 17 -> 19; matrix products, arithmetic and copies ran while one was open for 7% -> 9% of each run, Pallas kernels for 6% -> 7%
where the time goes in v3:
time: 134 us; the launch traced here: 133 us
  waiting for transfers between devices  47 us (35%)
  Pallas kernels  39.4 us (29%)
  starting transfers between devices  32.5 us (24%)
  local copies, waits for them, and re-layouts  10.5 us (8%)
  other arithmetic  3 us (2%)
    pallas_call x1, Pallas kernels, subspace_pieces(): pl.pallas_call(functools.partial(pieces_kernel, scale), out_shape=jax.Sha...  23.7 us
    ppermute x10, waiting for transfers between devices, send_corner(): return lax.ppermute(array, ('gx', 'sa'), pairs)  13.8 us
    ppermute x10, starting transfers between devices, send_corner(): return lax.ppermute(array, ('gx', 'sa'), pairs)  12.8 us
    ppermute x6, waiting for transfers between devices, sum_z(): lax.ppermute(array, 'gy', turn(size, step))  12.2 us
    ppermute x6, starting transfers between devices, sum_z(): lax.ppermute(array, 'gy', turn(size, step))  8.99 us
    dynamic_slice x5, local copies, waits for them, and re-layouts, chunk(): lax.dynamic_slice_in_dim(source, owner * species + starts[i], sizes[i], 0)  8.59 us
    ppermute x3, waiting for transfers between devices, on_halves(): lax.ppermute(projected[i], 'gy', turn(slabs, i))  8.3 us
    ppermute x3, waiting for transfers between devices, on_halves(): got = [lax.ppermute(piece, 'gx', flip(2, 1)) for piece in sent]  8.05 us
  transfers between devices with their start and end apart: 32, of which 19 were waited for; matrix products, arithmetic and copies ran while one was open for 9% of the time, Pallas kernels for 7%

profile of v3, /device:TPU:0, one launch (start us, length us, event | category | flops | bytes accessed | tf_op | source)
XLA Modules:
  0.0 133.3 jit_solution(17554825695924376882)
XLA Ops:
  0.6 2.1 %constant_dynamic-slice_fusion.5 = f32[3,1,512,128]{3,2,1,0:T(8,128)} fusion(f32[16,1,512,128]{3,2,1,0:T(8,128)} %field_ref, s32[]{:T(128)S(6)} %select_n.38), kind=kLoop, calls=%fused_computation.10 | loop fusion | bytes 1572868 | tf_op jit(solution)/shard_map/dynamic_slice | solution.py:520
  2.7 2.9 %collective-permute-start.1 = (f32[3,1,512,128]{3,2,1,0:T(8,128)}, f32[3,1,512,128]{3,2,1,0:T(8,128)}, u32[]{:S(2)}, u32[]{:S(2)}) collective-permute-start(f32[3,1,512,128]{3,2,1,0:T(8,128)} %constant_dynamic-slice_fusion.5), channel_id=1, source_target_pairs={{0,16},{16,0},{1,17},{17,1},{2,18},{18,2},{3,19},{19,3},{4,20},{20... | collective-permute-start | bytes 2359304 | tf_op jit(solution)/shard_map/ppermute | solution.py:525
  5.6 1.9 %constant_dynamic-slice_fusion.3 = f32[2,1,512,128]{3,2,1,0:T(8,128)} fusion(f32[16,1,512,128]{3,2,1,0:T(8,128)} %field_ref, s32[]{:T(128)S(6)} %select_n.40), kind=kLoop, calls=%fused_computation.8 | loop fusion | bytes 1048580 | tf_op jit(solution)/shard_map/dynamic_slice | solution.py:520
  7.5 2.1 %constant_dynamic-slice_fusion.4 = f32[3,1,512,128]{3,2,1,0:T(8,128)} fusion(f32[16,1,512,128]{3,2,1,0:T(8,128)} %field_ref, s32[]{:T(128)S(6)} %select_n.39), kind=kLoop, calls=%fused_computation.9 | loop fusion | bytes 1572868 | tf_op jit(solution)/shard_map/dynamic_slice | solution.py:520
  9.6 0.7 stack.23.place_ref
  10.3 6.5 %own_blocks.1 = (f32[160,512]{1,0:T(8,128)}, f32[160,512]{1,0:T(8,128)}) custom-call(s32[5]{0:T(128)} %stack.23.place_ref, f32[16,1,512,128]{3,2,1,0:T(8,128)} %field_ref), custom_call_target="tpu_custom_call" | custom-call | flops 199999995904 | bytes 4194304 | tf_op jit(solution)/shard_map/own_blocks/pallas_call | solution.py:311
  16.8 0.0 collective-permute-start.6
  16.9 1.8 %collective-permute-done = f32[160,512]{1,0:T(8,128)S(1)} collective-permute-done((f32[160,512]{1,0:T(8,128)}, f32[160,512]{1,0:T(8,128)S(1)}, u32[]{:S(2)}, u32[]{:S(2)}) %collective-permute-start) | collective-permute-done | bytes 327712 | tf_op jit(solution)/shard_map/ppermute | solution.py:483
  18.7 1.0 add.98
  19.7 4.6 %collective-permute-done.1.refs_0_ = f32[3,1,512,128]{3,2,1,0:T(8,128)} collective-permute-done((f32[3,1,512,128]{3,2,1,0:T(8,128)}, f32[3,1,512,128]{3,2,1,0:T(8,128)}, u32[]{:S(2)}, u32[]{:S(2)}) %collective-permute-start.1) | collective-permute-done | bytes 786464 | tf_op jit(solution)/shard_map/ppermute | solution.py:525
  24.3 2.2 %collective-permute-start.2 = (f32[80,512]{1,0:T(8,128)S(1)}, f32[80,512]{1,0:T(8,128)S(1)}, u32[]{:S(2)}, u32[]{:S(2)}) collective-permute-start(f32[80,512]{1,0:T(8,128)S(1)} %dynamic-slice_bitcast_fusion), channel_id=1, source_target_pairs={{0,2},{1,3},{2,0},{3,1},{16,18},{17,19},{18,16},{19,17},{4,6},{5,7... | collective-permute-start | bytes 491528 | tf_op jit(solution)/shard_map/ppermute | solution.py:489
  26.5 1.5 %collective-permute-start.8 = (f32[2,1,512,128]{3,2,1,0:T(8,128)}, f32[2,1,512,128]{3,2,1,0:T(8,128)S(1)}, u32[]{:S(2)}, u32[]{:S(2)}) collective-permute-start(f32[2,1,512,128]{3,2,1,0:T(8,128)} %constant_dynamic-slice_fusion.3), channel_id=1, source_target_pairs={{0,16},{16,0},{1,17},{17,1},{2,18},{18,2},{3,19},{19,3},{4,20},{20... | collective-permute-start | bytes 1572872 | tf_op jit(solution)/shard_map/ppermute | solution.py:525
  28.0 1.8 %collective-permute-done.2 = f32[80,512]{1,0:T(8,128)S(1)} collective-permute-done((f32[80,512]{1,0:T(8,128)S(1)}, f32[80,512]{1,0:T(8,128)S(1)}, u32[]{:S(2)}, u32[]{:S(2)}) %collective-permute-start.2) | collective-permute-done | bytes 163872 | tf_op jit(solution)/shard_map/ppermute | solution.py:489
  29.8 0.7 bitcast_add_fusion
  30.5 4.1 %collective-permute-start.5 = (f32[80,512]{1,0:T(8,128)}, f32[80,512]{1,0:T(8,128)}, u32[]{:S(2)}, u32[]{:S(2)}) collective-permute-start(f32[80,512]{1,0:T(8,128)} %bitcast_add_fusion), channel_id=1, source_target_pairs={{0,12},{4,0},{8,4},{12,8},{1,13},{5,1},{9,5},{13,9},{2,14},{6,2},{... | collective-permute-start | bytes 491528 | tf_op jit(solution)/shard_map/ppermute | solution.py:494
  34.6 0.0 collective-permute-start.4
  34.6 1.0 collective-permute-start.3
  35.6 1.5 %constant_dynamic-slice_fusion.1 = (f32[3,1,512,128]{3,2,1,0:T(8,128)S(1)}, f32[3,1,512,128]{3,2,1,0:T(8,128)S(1)}) fusion(f32[16,1,512,128]{3,2,1,0:T(8,128)} %field_ref, s32[]{:T(128)S(6)} %select_n.44, s32[]{:T(128)S(6)} %select_n.43), kind=kLoop, calls=%fused_computation.6 | loop fusion | bytes 3145736 | tf_op jit(solution)/shard_map/dynamic_slice | solution.py:520
  37.1 1.2 copy.4
  38.3 1.1 constant_dynamic-slice_fusion.refs_1_.refs_5_
  39.4 1.7 %collective-permute-done.6.refs_1_ = f32[3,1,512,128]{3,2,1,0:T(8,128)S(1)} collective-permute-done((f32[3,1,512,128]{3,2,1,0:T(8,128)}, f32[3,1,512,128]{3,2,1,0:T(8,128)S(1)}, u32[]{:S(2)}, u32[]{:S(2)}) %collective-permute-start.6) | collective-permute-done | bytes 786464 | tf_op jit(solution)/shard_map/ppermute | solution.py:525
  41.1 2.8 %cross_block.2 = (f32[256,512]{1,0:T(8,128)S(1)}, f32[256,512]{1,0:T(8,128)S(1)}) custom-call(s32[5]{0:T(128)S(1)} %copy-done, f32[3,1,512,128]{3,2,1,0:T(8,128)} %collective-permute-done.1.refs_0_, f32[3,1,512,128]{3,2,1,0:T(8,128)S(1)} %collective-permute-done.6.refs_1_, f32[3,1,512,128]{3,2,1,0:T(8,128)S(1)} %get-tuple-element.57.refs_2_.refs_3_, ...), custom_call_target="tpu_custom_call" | custom-call | tf_op jit(solution)/shard_map/cross_block/pallas_call | solution.py:365
  43.9 0.0 collective-permute-done.5
  43.9 3.0 %collective-permute-done.4 = f32[80,512]{1,0:T(8,128)} collective-permute-done((f32[80,512]{1,0:T(8,128)}, f32[80,512]{1,0:T(8,128)}, u32[]{:S(2)}, u32[]{:S(2)}) %collective-permute-start.4) | collective-permute-done | bytes 163872 | tf_op jit(solution)/shard_map/ppermute | solution.py:494
  46.9 1.2 add_add_fusion.refs_0_
  48.1 1.6 %collective-permute-start.7 = (f32[80,512]{1,0:T(8,128)S(1)}, f32[80,512]{1,0:T(8,128)S(1)}, u32[]{:S(2)}, u32[]{:S(2)}) collective-permute-start(f32[80,512]{1,0:T(8,128)S(1)} %add_add_fusion.refs_0_), channel_id=1, source_target_pairs={{0,2},{1,3},{2,0},{3,1},{16,18},{17,19},{18,16},{19,17},{4,6},{5,7... | collective-permute-start | bytes 491528 | tf_op jit(solution)/shard_map/ppermute | solution.py:489
  49.7 1.8 %collective-permute-done.8.refs_0_.refs_2_ = f32[2,1,512,128]{3,2,1,0:T(8,128)S(1)} collective-permute-done((f32[2,1,512,128]{3,2,1,0:T(8,128)}, f32[2,1,512,128]{3,2,1,0:T(8,128)S(1)}, u32[]{:S(2)}, u32[]{:S(2)}) %collective-permute-start.8) | collective-permute-done | bytes 524320 | tf_op jit(solution)/shard_map/ppermute | solution.py:525
  51.5 2.0 %collective-permute-done.7.refs_2_ = f32[80,512]{1,0:T(8,128)S(1)} collective-permute-done((f32[80,512]{1,0:T(8,128)S(1)}, f32[80,512]{1,0:T(8,128)S(1)}, u32[]{:S(2)}, u32[]{:S(2)}) %collective-permute-start.7) | collective-permute-done | bytes 163872 | tf_op jit(solution)/shard_map/ppermute | solution.py:489
  53.5 1.2 cross_block.3
  54.7 0.1 collective-permute-start.9
  54.8 1.9 %collective-permute-done.9.right_ref = f32[256,512]{1,0:T(8,128)S(1)} collective-permute-done((f32[256,512]{1,0:T(8,128)S(1)}, f32[256,512]{1,0:T(8,128)S(1)}, u32[]{:S(2)}, u32[]{:S(2)}) %collective-permute-start.9) | collective-permute-done | bytes 524320 | tf_op jit(solution)/shard_map/ppermute | solution.py:483
  56.7 0.6 quarters.1
  57.3 1.6 %collective-permute-start.10 = (f32[64,512]{1,0:T(8,128)S(1)}, f32[64,512]{1,0:T(8,128)S(1)}, u32[]{:S(2)}, u32[]{:S(2)}) collective-permute-start(f32[64,512]{1,0:T(8,128)S(1)} %get-tuple-element.42), channel_id=1, source_target_pairs={{0,16},{1,17},{2,18},{3,19},{16,0},{17,1},{18,2},{19,3},{4,20},{5,... | collective-permute-start | bytes 393224 | tf_op jit(solution)/shard_map/ppermute | solution.py:489
  58.9 1.5 %collective-permute-start.17 = (f32[64,512]{1,0:T(8,128)S(1)}, f32[64,512]{1,0:T(8,128)S(1)}, u32[]{:S(2)}, u32[]{:S(2)}) collective-permute-start(f32[64,512]{1,0:T(8,128)S(1)} %get-tuple-element.46), channel_id=1, source_target_pairs={{0,2},{1,3},{2,0},{3,1},{16,18},{17,19},{18,16},{19,17},{4,6},{5,7... | collective-permute-start | bytes 393224 | tf_op jit(solution)/shard_map/ppermute | solution.py:489
  60.4 0.5 collective-permute-start.18
  60.9 2.4 %collective-permute-done.10 = f32[64,512]{1,0:T(8,128)S(1)} collective-permute-done((f32[64,512]{1,0:T(8,128)S(1)}, f32[64,512]{1,0:T(8,128)S(1)}, u32[]{:S(2)}, u32[]{:S(2)}) %collective-permute-start.10) | collective-permute-done | bytes 131104 | tf_op jit(solution)/shard_map/ppermute | solution.py:489
  63.3 1.9 %collective-permute-start.11 = (f32[80,512]{1,0:T(8,128)S(1)}, f32[80,512]{1,0:T(8,128)S(1)}, u32[]{:S(2)}, u32[]{:S(2)}) collective-permute-start(f32[80,512]{1,0:T(8,128)S(1)} %add_add_fusion.refs_0_), channel_id=1, source_target_pairs={{0,16},{1,17},{2,18},{3,19},{16,0},{17,1},{18,2},{19,3},{4,20},{5,... | collective-permute-start | bytes 491528 | tf_op jit(solution)/shard_map/ppermute | solution.py:489
  65.2 0.1 collective-permute-start.12
  65.3 0.9 collective-permute-done.17
  66.2 1.5 %collective-permute-done.18 = f32[64,512]{1,0:T(8,128)S(1)} collective-permute-done((f32[64,512]{1,0:T(8,128)S(1)}, f32[64,512]{1,0:T(8,128)S(1)}, u32[]{:S(2)}, u32[]{:S(2)}) %collective-permute-start.18) | collective-permute-done | bytes 131104 | tf_op jit(solution)/shard_map/ppermute | solution.py:489
  67.7 1.9 %collective-permute-start.21 = (f32[64,512]{1,0:T(8,128)S(1)}, f32[64,512]{1,0:T(8,128)S(1)}, u32[]{:S(2)}, u32[]{:S(2)}) collective-permute-start(f32[64,512]{1,0:T(8,128)S(1)} %add_add_fusion.2), channel_id=1, source_target_pairs={{0,12},{4,0},{8,4},{12,8},{1,13},{5,1},{9,5},{13,9},{2,14},{6,2},{... | collective-permute-start | bytes 393224 | tf_op jit(solution)/shard_map/ppermute | solution.py:494
  69.6 0.0 collective-permute-start.20
  69.7 1.9 %collective-permute-start.19 = (f32[64,512]{1,0:T(8,128)S(1)}, f32[64,512]{1,0:T(8,128)S(1)}, u32[]{:S(2)}, u32[]{:S(2)}) collective-permute-start(f32[64,512]{1,0:T(8,128)S(1)} %add_add_fusion.2), channel_id=1, source_target_pairs={{0,4},{4,8},{8,12},{12,0},{1,5},{5,9},{9,13},{13,1},{2,6},{6,10},{... | collective-permute-start | bytes 393224 | tf_op jit(solution)/shard_map/ppermute | solution.py:494
  71.6 1.9 %collective-permute-done.21 = f32[64,512]{1,0:T(8,128)S(1)} collective-permute-done((f32[64,512]{1,0:T(8,128)S(1)}, f32[64,512]{1,0:T(8,128)S(1)}, u32[]{:S(2)}, u32[]{:S(2)}) %collective-permute-start.21) | collective-permute-done | bytes 131104 | tf_op jit(solution)/shard_map/ppermute | solution.py:494
  73.5 7.3 %collective-permute-done.20 = f32[64,512]{1,0:T(8,128)S(1)} collective-permute-done((f32[64,512]{1,0:T(8,128)S(1)}, f32[64,512]{1,0:T(8,128)S(1)}, u32[]{:S(2)}, u32[]{:S(2)}) %collective-permute-start.20) | collective-permute-done | bytes 131104 | tf_op jit(solution)/shard_map/ppermute | solution.py:494
  80.8 0.0 collective-permute-done.19
  80.8 0.6 collective-permute-start.25
  81.4 1.5 %collective-permute-start.24 = (f32[64,512]{1,0:T(8,128)S(1)}, f32[64,512]{1,0:T(8,128)S(1)}, u32[]{:S(2)}, u32[]{:S(2)}) collective-permute-start(f32[64,512]{1,0:T(8,128)S(1)} %add_add_fusion.1.refs_8_), channel_id=1, source_target_pairs={{0,18},{1,19},{2,16},{3,17},{16,2},{17,3},{18,0},{19,1},{4,22},{5,... | collective-permute-start | bytes 393224 | tf_op jit(solution)/shard_map/ppermute | solution.py:489
  82.9 1.5 %collective-permute-start.23 = (f32[64,512]{1,0:T(8,128)S(1)}, f32[64,512]{1,0:T(8,128)S(1)}, u32[]{:S(2)}, u32[]{:S(2)}) collective-permute-start(f32[64,512]{1,0:T(8,128)S(1)} %add_add_fusion.1.refs_8_), channel_id=1, source_target_pairs={{0,2},{1,3},{2,0},{3,1},{16,18},{17,19},{18,16},{19,17},{4,6},{5,7... | collective-permute-start | bytes 393224 | tf_op jit(solution)/shard_map/ppermute | solution.py:489
  84.3 0.6 collective-permute-start.22
  84.9 0.5 collective-permute-start.16
  85.4 3.3 %collective-permute-done.24.refs_11_ = f32[64,512]{1,0:T(8,128)S(1)} collective-permute-done((f32[64,512]{1,0:T(8,128)S(1)}, f32[64,512]{1,0:T(8,128)S(1)}, u32[]{:S(2)}, u32[]{:S(2)}) %collective-permute-start.24) | collective-permute-done | bytes 131104 | tf_op jit(solution)/shard_map/ppermute | solution.py:489
  88.7 1.9 %collective-permute-done.23.refs_10_ = f32[64,512]{1,0:T(8,128)S(1)} collective-permute-done((f32[64,512]{1,0:T(8,128)S(1)}, f32[64,512]{1,0:T(8,128)S(1)}, u32[]{:S(2)}, u32[]{:S(2)}) %collective-permute-start.23) | collective-permute-done | bytes 131104 | tf_op jit(solution)/shard_map/ppermute | solution.py:489
  90.6 0.0 collective-permute-start.27
  90.6 0.5 collective-permute-start.26
  91.1 0.8 collective-permute-done.27.refs_14_
  91.9 0.2 collective-permute-done.26.refs_13_
  92.1 23.7 %subspace.1.basis_ref = f32[128,1024]{1,0:T(8,128)S(1)} custom-call(s32[5]{0:T(128)S(1)} %copy-done, f32[80,512]{1,0:T(8,128)S(1)} %add_add_fusion.refs_0_, f32[80,512]{1,0:T(8,128)S(1)} %collective-permute-done.11.refs_1_, f32[80,512]{1,0:T(8,128)S(1)} %collective-permute-done.7.refs_2_, f32[80,512]{1,0:T(8,128)S(1)} %collective-permute-done.12.refs_3_, ...), custom_call_target="tpu_custom_call" | custom-call | tf_op jit(solution)/shard_map/subspace/pallas_call | solution.py:247
  115.9 3.1 %project.1 = (f32[32,128]{1,0:T(8,128)}, f32[8,1,32,128]{3,2,1,0:T(8,128)S(1)}, f32[8,1,32,128]{3,2,1,0:T(8,128)S(1)}, f32[8,1,32,128]{3,2,1,0:T(8,128)S(1)}, f32[8,1,32,128]{3,2,1,0:T(8,128)S(1)}) custom-call(s32[5]{0:T(128)S(1)} %copy-done, f32[128,1024]{1,0:T(8,128)S(1)} %subspace.1.basis_ref, f32[3,1,512,128]{3,2,1,0:T(8,128)} %collective-permute-done.1.refs_0_, ...), custom_call_target="tpu_custom_call" | custom-call | tf_op jit(solution)/shard_map/project/pallas_call | solution.py:430
  119.0 1.7 %collective-permute-start.30 = (f32[8,1,32,128]{3,2,1,0:T(8,128)S(1)}, f32[8,1,32,128]{3,2,1,0:T(8,128)S(1)}, u32[]{:S(2)}, u32[]{:S(2)}) collective-permute-start(f32[8,1,32,128]{3,2,1,0:T(8,128)S(1)} %get-tuple-element.53), channel_id=1, source_target_pairs={{0,8},{4,12},{8,0},{12,4},{1,9},{5,13},{9,1},{13,5},{2,10},{6,14},... | collective-permute-start | bytes 393224 | tf_op jit(solution)/shard_map/ppermute | solution.py:556
  120.7 2.9 %collective-permute-start.31 = (f32[8,1,32,128]{3,2,1,0:T(8,128)S(1)}, f32[8,1,32,128]{3,2,1,0:T(8,128)S(1)}, u32[]{:S(2)}, u32[]{:S(2)}) collective-permute-start(f32[8,1,32,128]{3,2,1,0:T(8,128)S(1)} %get-tuple-element.54), channel_id=1, source_target_pairs={{0,12},{4,0},{8,4},{12,8},{1,13},{5,1},{9,5},{13,9},{2,14},{6,2},{... | collective-permute-start | bytes 393224 | tf_op jit(solution)/shard_map/ppermute | solution.py:556
  123.6 3.7 %collective-permute-done.29.refs_1_ = f32[8,1,32,128]{3,2,1,0:T(8,128)S(1)} collective-permute-done((f32[8,1,32,128]{3,2,1,0:T(8,128)S(1)}, f32[8,1,32,128]{3,2,1,0:T(8,128)S(1)}, u32[]{:S(2)}, u32[]{:S(2)}) %collective-permute-start.29) | collective-permute-done | bytes 131104 | tf_op jit(solution)/shard_map/ppermute | solution.py:556
  127.3 4.6 %collective-permute-done.30.refs_2_ = f32[8,1,32,128]{3,2,1,0:T(8,128)S(1)} collective-permute-done((f32[8,1,32,128]{3,2,1,0:T(8,128)S(1)}, f32[8,1,32,128]{3,2,1,0:T(8,128)S(1)}, u32[]{:S(2)}, u32[]{:S(2)}) %collective-permute-start.30) | collective-permute-done | bytes 131104 | tf_op jit(solution)/shard_map/ppermute | solution.py:556
  131.9 1.4 %join.1 = f32[8,1,32,512]{3,2,1,0:T(8,128)} custom-call(s32[5]{0:T(128)S(1)} %copy-done, f32[8,1,32,128]{3,2,1,0:T(8,128)S(1)} %get-tuple-element.51.refs_0_, f32[8,1,32,128]{3,2,1,0:T(8,128)S(1)} %collective-permute-done.29.refs_1_, f32[8,1,32,128]{3,2,1,0:T(8,128)S(1)} %collective-permute-done.30.refs_2_, f32[8,1,32,128]{3,2,1,0:T(8,128)S(1)} %collective-permute-done.31.refs_3_), custom_call_target="tpu_custom_call" | custom-call | tf_op jit(solution)/shard_map/join/pallas_call | solution.py:452
  (22 shorter events, 0.1 us)
Async XLA Ops:
  2.7 21.6 %collective-permute-start.1 = (f32[3,1,512,128]{3,2,1,0:T(8,128)}, f32[3,1,512,128]{3,2,1,0:T(8,128)}, u32[]{:S(2)}, u32[]{:S(2)}) collective-permute-start(f32[3,1,512,128]{3,2,1,0:T(8,128)} %constant_dynamic-slice_fusion.5), channel_id=1, source_target_pairs={{0,16},{16,0},{1,17},{17,1},{2,18},{18,2},{3,19},{19,3},{4,20},{20... | collective-permute-start | bytes 2359304 | tf_op jit(solution)/shard_map/ppermute | solution.py:525
  16.8 24.3 %copy-start = (s32[5]{0:T(128)S(1)}, s32[5]{0:T(128)}, u32[]{:S(2)}) copy-start(s32[5]{0:T(128)} %stack.23.place_ref) | copy-start | bytes 64
  16.8 1.8 %collective-permute-start = (f32[160,512]{1,0:T(8,128)}, f32[160,512]{1,0:T(8,128)S(1)}, u32[]{:S(2)}, u32[]{:S(2)}) collective-permute-start(f32[160,512]{1,0:T(8,128)} %get-tuple-element.32), channel_id=1, source_target_pairs={{0,1},{1,0},{2,3},{3,2},{4,5},{5,4},{6,7},{7,6},{8,9},{9,8},{10,11... | collective-permute-start | bytes 983048 | tf_op jit(solution)/shard_map/ppermute | solution.py:483
  16.8 24.2 %collective-permute-start.6 = (f32[3,1,512,128]{3,2,1,0:T(8,128)}, f32[3,1,512,128]{3,2,1,0:T(8,128)S(1)}, u32[]{:S(2)}, u32[]{:S(2)}) collective-permute-start(f32[3,1,512,128]{3,2,1,0:T(8,128)} %constant_dynamic-slice_fusion.4), channel_id=1, source_target_pairs={{0,16},{16,0},{1,17},{17,1},{2,18},{18,2},{3,19},{19,3},{4,20},{20... | collective-permute-start | bytes 2359304 | tf_op jit(solution)/shard_map/ppermute | solution.py:525
  24.3 5.5 %collective-permute-start.2 = (f32[80,512]{1,0:T(8,128)S(1)}, f32[80,512]{1,0:T(8,128)S(1)}, u32[]{:S(2)}, u32[]{:S(2)}) collective-permute-start(f32[80,512]{1,0:T(8,128)S(1)} %dynamic-slice_bitcast_fusion), channel_id=1, source_target_pairs={{0,2},{1,3},{2,0},{3,1},{16,18},{17,19},{18,16},{19,17},{4,6},{5,7... | collective-permute-start | bytes 491528 | tf_op jit(solution)/shard_map/ppermute | solution.py:489
  26.5 25.0 %collective-permute-start.8 = (f32[2,1,512,128]{3,2,1,0:T(8,128)}, f32[2,1,512,128]{3,2,1,0:T(8,128)S(1)}, u32[]{:S(2)}, u32[]{:S(2)}) collective-permute-start(f32[2,1,512,128]{3,2,1,0:T(8,128)} %constant_dynamic-slice_fusion.3), channel_id=1, source_target_pairs={{0,16},{16,0},{1,17},{17,1},{2,18},{18,2},{3,19},{19,3},{4,20},{20... | collective-permute-start | bytes 1572872 | tf_op jit(solution)/shard_map/ppermute | solution.py:525
  30.5 13.4 %collective-permute-start.5 = (f32[80,512]{1,0:T(8,128)}, f32[80,512]{1,0:T(8,128)}, u32[]{:S(2)}, u32[]{:S(2)}) collective-permute-start(f32[80,512]{1,0:T(8,128)} %bitcast_add_fusion), channel_id=1, source_target_pairs={{0,12},{4,0},{8,4},{12,8},{1,13},{5,1},{9,5},{13,9},{2,14},{6,2},{... | collective-permute-start | bytes 491528 | tf_op jit(solution)/shard_map/ppermute | solution.py:494
  34.6 12.3 %collective-permute-start.4 = (f32[80,512]{1,0:T(8,128)}, f32[80,512]{1,0:T(8,128)}, u32[]{:S(2)}, u32[]{:S(2)}) collective-permute-start(f32[80,512]{1,0:T(8,128)} %bitcast_add_fusion), channel_id=1, source_target_pairs={{0,8},{4,12},{8,0},{12,4},{1,9},{5,13},{9,1},{13,5},{2,10},{6,14},... | collective-permute-start | bytes 491528 | tf_op jit(solution)/shard_map/ppermute | solution.py:494
  34.6 12.3 %collective-permute-start.3 = (f32[80,512]{1,0:T(8,128)}, f32[80,512]{1,0:T(8,128)}, u32[]{:S(2)}, u32[]{:S(2)}) collective-permute-start(f32[80,512]{1,0:T(8,128)} %bitcast_add_fusion), channel_id=1, source_target_pairs={{0,4},{4,8},{8,12},{12,0},{1,5},{5,9},{9,13},{13,1},{2,6},{6,10},{... | collective-permute-start | bytes 491528 | tf_op jit(solution)/shard_map/ppermute | solution.py:494
  48.1 5.4 %collective-permute-start.7 = (f32[80,512]{1,0:T(8,128)S(1)}, f32[80,512]{1,0:T(8,128)S(1)}, u32[]{:S(2)}, u32[]{:S(2)}) collective-permute-start(f32[80,512]{1,0:T(8,128)S(1)} %add_add_fusion.refs_0_), channel_id=1, source_target_pairs={{0,2},{1,3},{2,0},{3,1},{16,18},{17,19},{18,16},{19,17},{4,6},{5,7... | collective-permute-start | bytes 491528 | tf_op jit(solution)/shard_map/ppermute | solution.py:489
  54.7 2.0 %collective-permute-start.9 = (f32[256,512]{1,0:T(8,128)S(1)}, f32[256,512]{1,0:T(8,128)S(1)}, u32[]{:S(2)}, u32[]{:S(2)}) collective-permute-start(f32[256,512]{1,0:T(8,128)S(1)} %get-tuple-element.41), channel_id=1, source_target_pairs={{0,1},{1,0},{2,3},{3,2},{4,5},{5,4},{6,7},{7,6},{8,9},{9,8},{10,11... | collective-permute-start | bytes 1572872 | tf_op jit(solution)/shard_map/ppermute | solution.py:483
  57.3 5.9 %collective-permute-start.10 = (f32[64,512]{1,0:T(8,128)S(1)}, f32[64,512]{1,0:T(8,128)S(1)}, u32[]{:S(2)}, u32[]{:S(2)}) collective-permute-start(f32[64,512]{1,0:T(8,128)S(1)} %get-tuple-element.42), channel_id=1, source_target_pairs={{0,16},{1,17},{2,18},{3,19},{16,0},{17,1},{18,2},{19,3},{4,20},{5,... | collective-permute-start | bytes 393224 | tf_op jit(solution)/shard_map/ppermute | solution.py:489
  58.9 7.3 %collective-permute-start.17 = (f32[64,512]{1,0:T(8,128)S(1)}, f32[64,512]{1,0:T(8,128)S(1)}, u32[]{:S(2)}, u32[]{:S(2)}) collective-permute-start(f32[64,512]{1,0:T(8,128)S(1)} %get-tuple-element.46), channel_id=1, source_target_pairs={{0,2},{1,3},{2,0},{3,1},{16,18},{17,19},{18,16},{19,17},{4,6},{5,7... | collective-permute-start | bytes 393224 | tf_op jit(solution)/shard_map/ppermute | solution.py:489
  60.4 7.3 %collective-permute-start.18 = (f32[64,512]{1,0:T(8,128)S(1)}, f32[64,512]{1,0:T(8,128)S(1)}, u32[]{:S(2)}, u32[]{:S(2)}) collective-permute-start(f32[64,512]{1,0:T(8,128)S(1)} %get-tuple-element.47), channel_id=1, source_target_pairs={{0,18},{1,19},{2,16},{3,17},{16,2},{17,3},{18,0},{19,1},{4,22},{5,... | collective-permute-start | bytes 393224 | tf_op jit(solution)/shard_map/ppermute | solution.py:489
  63.3 17.5 %collective-permute-start.11 = (f32[80,512]{1,0:T(8,128)S(1)}, f32[80,512]{1,0:T(8,128)S(1)}, u32[]{:S(2)}, u32[]{:S(2)}) collective-permute-start(f32[80,512]{1,0:T(8,128)S(1)} %add_add_fusion.refs_0_), channel_id=1, source_target_pairs={{0,16},{1,17},{2,18},{3,19},{16,0},{17,1},{18,2},{19,3},{4,20},{5,... | collective-permute-start | bytes 491528 | tf_op jit(solution)/shard_map/ppermute | solution.py:489
  65.2 15.6 %collective-permute-start.12 = (f32[80,512]{1,0:T(8,128)S(1)}, f32[80,512]{1,0:T(8,128)S(1)}, u32[]{:S(2)}, u32[]{:S(2)}) collective-permute-start(f32[80,512]{1,0:T(8,128)S(1)} %collective-permute-done.7.refs_2_), channel_id=1, source_target_pairs={{0,16},{1,17},{2,18},{3,19},{16,0},{17,1},{18,2},{19,3},{4,20},{5,... | collective-permute-start | bytes 491528 | tf_op jit(solution)/shard_map/ppermute | solution.py:489
  67.7 5.8 %collective-permute-start.21 = (f32[64,512]{1,0:T(8,128)S(1)}, f32[64,512]{1,0:T(8,128)S(1)}, u32[]{:S(2)}, u32[]{:S(2)}) collective-permute-start(f32[64,512]{1,0:T(8,128)S(1)} %add_add_fusion.2), channel_id=1, source_target_pairs={{0,12},{4,0},{8,4},{12,8},{1,13},{5,1},{9,5},{13,9},{2,14},{6,2},{... | collective-permute-start | bytes 393224 | tf_op jit(solution)/shard_map/ppermute | solution.py:494
  69.6 11.2 %collective-permute-start.20 = (f32[64,512]{1,0:T(8,128)S(1)}, f32[64,512]{1,0:T(8,128)S(1)}, u32[]{:S(2)}, u32[]{:S(2)}) collective-permute-start(f32[64,512]{1,0:T(8,128)S(1)} %add_add_fusion.2), channel_id=1, source_target_pairs={{0,8},{4,12},{8,0},{12,4},{1,9},{5,13},{9,1},{13,5},{2,10},{6,14},... | collective-permute-start | bytes 393224 | tf_op jit(solution)/shard_map/ppermute | solution.py:494
  69.7 11.1 %collective-permute-start.19 = (f32[64,512]{1,0:T(8,128)S(1)}, f32[64,512]{1,0:T(8,128)S(1)}, u32[]{:S(2)}, u32[]{:S(2)}) collective-permute-start(f32[64,512]{1,0:T(8,128)S(1)} %add_add_fusion.2), channel_id=1, source_target_pairs={{0,4},{4,8},{8,12},{12,0},{1,5},{5,9},{9,13},{13,1},{2,6},{6,10},{... | collective-permute-start | bytes 393224 | tf_op jit(solution)/shard_map/ppermute | solution.py:494
  73.5 10.8 %collective-permute-start.13 = (f32[80,512]{1,0:T(8,128)S(1)}, f32[80,512]{1,0:T(8,128)S(1)}, u32[]{:S(2)}, u32[]{:S(2)}) collective-permute-start(f32[80,512]{1,0:T(8,128)S(1)} %add_add_fusion.refs_0_), channel_id=1, source_target_pairs={{0,1},{1,0},{2,3},{3,2},{4,5},{5,4},{6,7},{7,6},{8,9},{9,8},{10,11... | collective-permute-start | bytes 491528 | tf_op jit(solution)/shard_map/ppermute | solution.py:483
  80.8 4.1 %collective-permute-start.15 = (f32[80,512]{1,0:T(8,128)S(1)}, f32[80,512]{1,0:T(8,128)S(1)}, u32[]{:S(2)}, u32[]{:S(2)}) collective-permute-start(f32[80,512]{1,0:T(8,128)S(1)} %collective-permute-done.7.refs_2_), channel_id=1, source_target_pairs={{0,1},{1,0},{2,3},{3,2},{4,5},{5,4},{6,7},{7,6},{8,9},{9,8},{10,11... | collective-permute-start | bytes 491528 | tf_op jit(solution)/shard_map/ppermute | solution.py:483
  80.8 4.1 %collective-permute-start.25 = (f32[64,512]{1,0:T(8,128)S(1)}, f32[64,512]{1,0:T(8,128)S(1)}, u32[]{:S(2)}, u32[]{:S(2)}) collective-permute-start(f32[64,512]{1,0:T(8,128)S(1)} %add_add_fusion.1.refs_8_), channel_id=1, source_target_pairs={{0,1},{1,0},{2,3},{3,2},{4,5},{5,4},{6,7},{7,6},{8,9},{9,8},{10,11... | collective-permute-start | bytes 393224 | tf_op jit(solution)/shard_map/ppermute | solution.py:483
  81.4 7.3 %collective-permute-start.24 = (f32[64,512]{1,0:T(8,128)S(1)}, f32[64,512]{1,0:T(8,128)S(1)}, u32[]{:S(2)}, u32[]{:S(2)}) collective-permute-start(f32[64,512]{1,0:T(8,128)S(1)} %add_add_fusion.1.refs_8_), channel_id=1, source_target_pairs={{0,18},{1,19},{2,16},{3,17},{16,2},{17,3},{18,0},{19,1},{4,22},{5,... | collective-permute-start | bytes 393224 | tf_op jit(solution)/shard_map/ppermute | solution.py:489
  82.9 7.7 %collective-permute-start.23 = (f32[64,512]{1,0:T(8,128)S(1)}, f32[64,512]{1,0:T(8,128)S(1)}, u32[]{:S(2)}, u32[]{:S(2)}) collective-permute-start(f32[64,512]{1,0:T(8,128)S(1)} %add_add_fusion.1.refs_8_), channel_id=1, source_target_pairs={{0,2},{1,3},{2,0},{3,1},{16,18},{17,19},{18,16},{19,17},{4,6},{5,7... | collective-permute-start | bytes 393224 | tf_op jit(solution)/shard_map/ppermute | solution.py:489
  84.3 6.3 %collective-permute-start.22 = (f32[64,512]{1,0:T(8,128)S(1)}, f32[64,512]{1,0:T(8,128)S(1)}, u32[]{:S(2)}, u32[]{:S(2)}) collective-permute-start(f32[64,512]{1,0:T(8,128)S(1)} %add_add_fusion.1.refs_8_), channel_id=1, source_target_pairs={{0,16},{1,17},{2,18},{3,19},{16,0},{17,1},{18,2},{19,3},{4,20},{5,... | collective-permute-start | bytes 393224 | tf_op jit(solution)/shard_map/ppermute | solution.py:489
  84.9 6.2 %collective-permute-start.14 = (f32[80,512]{1,0:T(8,128)S(1)}, f32[80,512]{1,0:T(8,128)S(1)}, u32[]{:S(2)}, u32[]{:S(2)}) collective-permute-start(f32[80,512]{1,0:T(8,128)S(1)} %collective-permute-done.11.refs_1_), channel_id=1, source_target_pairs={{0,1},{1,0},{2,3},{3,2},{4,5},{5,4},{6,7},{7,6},{8,9},{9,8},{10,11... | collective-permute-start | bytes 491528 | tf_op jit(solution)/shard_map/ppermute | solution.py:483
  84.9 6.2 %collective-permute-start.16 = (f32[80,512]{1,0:T(8,128)S(1)}, f32[80,512]{1,0:T(8,128)S(1)}, u32[]{:S(2)}, u32[]{:S(2)}) collective-permute-start(f32[80,512]{1,0:T(8,128)S(1)} %collective-permute-done.12.refs_3_), channel_id=1, source_target_pairs={{0,1},{1,0},{2,3},{3,2},{4,5},{5,4},{6,7},{7,6},{8,9},{9,8},{10,11... | collective-permute-start | bytes 491528 | tf_op jit(solution)/shard_map/ppermute | solution.py:483
  88.7 2.4 %collective-permute-start.28 = (f32[64,512]{1,0:T(8,128)S(1)}, f32[64,512]{1,0:T(8,128)S(1)}, u32[]{:S(2)}, u32[]{:S(2)}) collective-permute-start(f32[64,512]{1,0:T(8,128)S(1)} %collective-permute-done.24.refs_11_), channel_id=1, source_target_pairs={{0,1},{1,0},{2,3},{3,2},{4,5},{5,4},{6,7},{7,6},{8,9},{9,8},{10,11... | collective-permute-start | bytes 393224 | tf_op jit(solution)/shard_map/ppermute | solution.py:483
  90.6 1.3 %collective-permute-start.27 = (f32[64,512]{1,0:T(8,128)S(1)}, f32[64,512]{1,0:T(8,128)S(1)}, u32[]{:S(2)}, u32[]{:S(2)}) collective-permute-start(f32[64,512]{1,0:T(8,128)S(1)} %collective-permute-done.23.refs_10_), channel_id=1, source_target_pairs={{0,1},{1,0},{2,3},{3,2},{4,5},{5,4},{6,7},{7,6},{8,9},{9,8},{10,11... | collective-permute-start | bytes 393224 | tf_op jit(solution)/shard_map/ppermute | solution.py:483
  90.6 1.5 %collective-permute-start.26 = (f32[64,512]{1,0:T(8,128)S(1)}, f32[64,512]{1,0:T(8,128)S(1)}, u32[]{:S(2)}, u32[]{:S(2)}) collective-permute-start(f32[64,512]{1,0:T(8,128)S(1)} %collective-permute-done.22.refs_9_), channel_id=1, source_target_pairs={{0,1},{1,0},{2,3},{3,2},{4,5},{5,4},{6,7},{7,6},{8,9},{9,8},{10,11... | collective-permute-start | bytes 393224 | tf_op jit(solution)/shard_map/ppermute | solution.py:483
  119.0 8.3 %collective-permute-start.29 = (f32[8,1,32,128]{3,2,1,0:T(8,128)S(1)}, f32[8,1,32,128]{3,2,1,0:T(8,128)S(1)}, u32[]{:S(2)}, u32[]{:S(2)}) collective-permute-start(f32[8,1,32,128]{3,2,1,0:T(8,128)S(1)} %get-tuple-element.52), channel_id=1, source_target_pairs={{0,4},{4,8},{8,12},{12,0},{1,5},{5,9},{9,13},{13,1},{2,6},{6,10},{... | collective-permute-start | bytes 393224 | tf_op jit(solution)/shard_map/ppermute | solution.py:556
  119.0 12.9 %collective-permute-start.30 = (f32[8,1,32,128]{3,2,1,0:T(8,128)S(1)}, f32[8,1,32,128]{3,2,1,0:T(8,128)S(1)}, u32[]{:S(2)}, u32[]{:S(2)}) collective-permute-start(f32[8,1,32,128]{3,2,1,0:T(8,128)S(1)} %get-tuple-element.53), channel_id=1, source_target_pairs={{0,8},{4,12},{8,0},{12,4},{1,9},{5,13},{9,1},{13,5},{2,10},{6,14},... | collective-permute-start | bytes 393224 | tf_op jit(solution)/shard_map/ppermute | solution.py:556
  120.7 11.2 %collective-permute-start.31 = (f32[8,1,32,128]{3,2,1,0:T(8,128)S(1)}, f32[8,1,32,128]{3,2,1,0:T(8,128)S(1)}, u32[]{:S(2)}, u32[]{:S(2)}) collective-permute-start(f32[8,1,32,128]{3,2,1,0:T(8,128)S(1)} %get-tuple-element.54), channel_id=1, source_target_pairs={{0,12},{4,0},{8,4},{12,8},{1,13},{5,1},{9,5},{13,9},{2,14},{6,2},{... | collective-permute-start | bytes 393224 | tf_op jit(solution)/shard_map/ppermute | solution.py:556

commit v4 on v3

--- a/solution.py
+++ b/solution.py
@@ -133,15 +133,23 @@
     )
 
 
-def iterate(scale, start_ref, basis_ref, gram_ref, inverse_ref):
+def iterate(scale, first_map, start_ref, basis_ref, gram_ref, inverse_ref, mapped_ref):
     rank = start_ref.shape[0]
     row = lax.broadcasted_iota(jnp.int32, (rank, rank), 0)
     col = lax.broadcasted_iota(jnp.int32, (rank, rank), 1)
     eye = jnp.where(row == col, 1.0, 0.0)
     basis_ref[...] = start_ref[...]
 
-    def iteration(_, carry):
-        mapped = mul(basis_ref[...], gram_ref[...]) * scale
+    def iteration(index, carry):
+        @pl.when(index == 0)
+        def _():
+            first_map()
+
+        @pl.when(index > 0)
+        def _():
+            mapped_ref[...] = mul(basis_ref[...], gram_ref[...])
+
+        mapped = mapped_ref[...] * scale
         once = apply(inverse_factor(inner_products(mapped)), mapped)
         inner = inner_products(once)
         error = inner - eye
@@ -176,8 +184,11 @@
     return pltpu.CompilerParams(vmem_limit_bytes=mebibytes << 20)
 
 
-def whole_kernel(gram_ref, start_ref, basis_ref, inverse_ref):
-    iterate(1.0, start_ref, basis_ref, gram_ref, inverse_ref)
+def whole_kernel(gram_ref, start_ref, basis_ref, inverse_ref, mapped_ref):
+    def first_map():
+        mapped_ref[...] = mul(start_ref[...], gram_ref[...])
+
+    iterate(1.0, first_map, start_ref, basis_ref, gram_ref, inverse_ref, mapped_ref)
 
 
 def subspace_whole(gram, start):
@@ -187,77 +198,131 @@
         out_shape=jax.ShapeDtypeStruct((rank, order), jnp.float32),
         in_specs=[VMEM_SPEC] * 2,
         out_specs=VMEM_SPEC,
-        scratch_shapes=[pltpu.VMEM((rank, rank), jnp.float32)],
+        scratch_shapes=[pltpu.VMEM((rank, rank), jnp.float32), pltpu.VMEM((rank, order), jnp.float32)],
         compiler_params=params(24),
         name="subspace_whole",
     )(gram, start)
 
 
-def pieces_kernel(scale, place_ref, *refs):
-    own_refs, cross_refs = refs[:8], refs[8:16]
-    start_ref, basis_ref, gram_ref, packed_ref, inverse_ref, sems = refs[16:]
+def diagonal_kernel(place_ref, *refs):
+    own_refs, (start_ref, gram_ref, head_ref, packed_ref) = refs[:8], refs[8:]
+    x, y, core = place_ref[0], place_ref[1], place_ref[2]
+    half = gram_ref.shape[1]
+    side = half // 4
+    for ref, (dc, dx, dy) in zip(own_refs, PIECES):
+        rows = ref.shape[0]
+        at = pl.multiple_of(((core ^ dc) * 2 + (y ^ dy)) * rows, 8)
+        packed_ref[x ^ dx, pl.ds(at, rows), :] = ref[...]
+    at = [side * i for i in range(5)]
+    for p in range(2):
+        last = packed_ref[p, :side, :]
+        third = packed_ref[p, side : 2 * side, :]
+        gram_ref[p, at[3] : at[4], at[0] : at[4]] = last
+        gram_ref[p, at[0] : at[3], at[3] : at[4]] = last[:, : 3 * side].T
+        gram_ref[p, at[2] : at[3], at[0] : at[3]] = third[:, : 3 * side]
+        gram_ref[p, at[0] : at[2], at[2] : at[3]] = third[:, : 2 * side].T
+        gram_ref[p, at[0] : at[1], at[0] : at[1]] = third[:, 3 * side :]
+        second = packed_ref[p, 2 * side :, :]
+        second = jnp.concatenate([second[:, : 2 * side], second[:, 2 * side :]], axis=0)
+        gram_ref[p, at[1] : at[2], at[0] : at[2]] = second
+        gram_ref[p, at[0] : at[1], at[1] : at[2]] = second[:, :side].T
+        columns = slice(half * p, half * (p + 1))
+        head_ref[:, columns] = mul(start_ref[:, columns], gram_ref[p])
+
+
+def diagonal_blocks(place, own, start):
+    rank, order = start.shape
+    half = order // 2
+    return pl.pallas_call(
+        diagonal_kernel,
+        out_shape=[
+            jax.ShapeDtypeStruct((2, half, half), jnp.float32),
+            jax.ShapeDtypeStruct((rank, order), jnp.float32),
+        ],
+        in_specs=[SMEM_SPEC] + [VMEM_SPEC] * 9,
+        out_specs=[VMEM_SPEC] * 2,
+        scratch_shapes=[pltpu.VMEM((2, 5 * half // 8, half), jnp.float32)],
+        compiler_params=params(16),
+        name="diagonal",
+    )(place, *own, start)
+
+
+def pieces_kernel(scale, count, place_ref, *refs):
+    diagonal_ref, head_ref, start_ref, refs = refs[0], refs[1], refs[2], refs[3:]
+    cross_refs, refs = refs[:8], refs[8:]
+    kept_refs, got_refs, refs = refs[:count], refs[count : 2 * count], refs[2 * count :]
+    own_rows_ref, *slab_refs = refs[:-8]
+    basis_ref, gram_ref, mapped_ref, inverse_ref, fields_ref, value_ref, sems, field_sems = refs[-8:]
     x, y, core = place_ref[0], place_ref[1], place_ref[2]
     half = gram_ref.shape[0] // 2
-    own_copies, cross_copies = [], []
+    cross_copies, later_copies = [], []
     for index, (dc, dx, dy) in enumerate(PIECES):
-        rows = own_refs[index].shape[0]
-        at = pl.multiple_of(((core ^ dc) * 2 + (y ^ dy)) * rows, 8)
-        own_copies.append(
-            pltpu.make_async_copy(
-                own_refs[index], packed_ref.at[x ^ dx, pl.ds(at, rows), :], sems.at[index]
-            )
-        )
         rows = cross_refs[index].shape[0]
         at = pl.multiple_of(((core ^ dc) * 4 + (x ^ dx) * 2 + (y ^ dy)) * rows, 8)
         cross_copies.append(
             pltpu.make_async_copy(
-                cross_refs[index], gram_ref.at[pl.ds(at, rows), half:], sems.at[8 + index]
+                cross_refs[index], gram_ref.at[pl.ds(at, rows), half:], sems.at[index]
             )
         )
-    for copy in own_copies + cross_copies:
+    for p in range(2):
+        square = pl.ds(half * p, half)
+        later_copies.append(
+            pltpu.make_async_copy(diagonal_ref.at[p], gram_ref.at[square, square], sems.at[8 + p])
+        )
+    for side, sources in enumerate((kept_refs, got_refs)):
+        first = 0
+        for index, ref in enumerate(sources):
+            later_copies.append(
+                pltpu.make_async_copy(
+                    ref.at[:, 0],
+                    fields_ref.at[side, first : first + ref.shape[0]],
+                    field_sems.at[side, index],
+                )
+            )
+            first += ref.shape[0]
+    for copy in cross_copies + later_copies:
         copy.start()
-    for copy in own_copies:
-        copy.wait()
-    side = half // 4
-    for p in range(2):
-        at = [p * half + side * i for i in range(5)]
-        last = packed_ref[p, :side, :]
-        third = packed_ref[p, side : 2 * side, :]
-        gram_ref[at[3] : at[4], at[0] : at[4]] = last
-        gram_ref[at[0] : at[3], at[3] : at[4]] = last[:, : 3 * side].T
-        gram_ref[at[2] : at[3], at[0] : at[3]] = third[:, : 3 * side]
-        gram_ref[at[0] : at[2], at[2] : at[3]] = third[:, : 2 * side].T
-        gram_ref[at[0] : at[1], at[0] : at[1]] = third[:, 3 * side :]
-        second = packed_ref[p, 2 * side :, :]
-        second = jnp.concatenate([second[:, : 2 * side], second[:, 2 * side :]], axis=0)
-        gram_ref[at[1] : at[2], at[0] : at[2]] = second
-        gram_ref[at[0] : at[1], at[1] : at[2]] = second[:, :side].T
     for copy in cross_copies:
         copy.wait()
     gram_ref[half:, :half] = gram_ref[:half, half:].T
-    iterate(scale, start_ref, basis_ref, gram_ref, inverse_ref)
+
+    def first_map():
+        mapped_ref[:, :half] = head_ref[:, :half] + mul(start_ref[:, half:], gram_ref[half:, :half])
+        mapped_ref[:, half:] = head_ref[:, half:] + mul(start_ref[:, :half], gram_ref[:half, half:])
+        for copy in later_copies:
+            copy.wait()
+
+    iterate(scale, first_map, start_ref, basis_ref, gram_ref, inverse_ref, mapped_ref)
+    project(place_ref, basis_ref, fields_ref, own_rows_ref, slab_refs, value_ref)
 
 
 PIECES = [(dc, dx, dy) for dc in range(2) for dx, dy in ((0, 0), (1, 0), (0, 1), (1, 1))]
 
 
-def subspace_pieces(place, own, cross, start, scale):
+def subspace_pieces(place, diagonal, head, start, cross, kept, got, scale, slabs, own_rows):
     rank, order = start.shape
     half = order // 2
+    species = sum(piece.shape[0] for piece in got)
+    width = got[0].shape[3]
+    slab = jax.ShapeDtypeStruct((species, 1, rank // slabs, width), jnp.float32)
     return pl.pallas_call(
-        functools.partial(pieces_kernel, scale),
-        out_shape=jax.ShapeDtypeStruct((rank, order), jnp.float32),
-        in_specs=[SMEM_SPEC] + [ANY_SPEC] * 16 + [VMEM_SPEC],
-        out_specs=VMEM_SPEC,
+        functools.partial(pieces_kernel, scale, len(got)),
+        out_shape=[jax.ShapeDtypeStruct((own_rows, rank), jnp.float32)] + [slab] * slabs,
+        in_specs=[SMEM_SPEC, ANY_SPEC] + [VMEM_SPEC] * 2 + [ANY_SPEC] * (8 + 2 * len(got)),
+        out_specs=[VMEM_SPEC] * (1 + slabs),
         scratch_shapes=[
+            pltpu.VMEM((rank, order), jnp.float32),
             pltpu.VMEM((order, order), jnp.float32),
-            pltpu.VMEM((2, 5 * half // 8, half), jnp.float32),
+            pltpu.VMEM((rank, order), jnp.float32),
             pltpu.VMEM((rank, rank), jnp.float32),
-            pltpu.SemaphoreType.DMA((16,)),
+            pltpu.VMEM((2, species, half, width), jnp.float32),
+            pltpu.VMEM((rank, 2 * width), jnp.float32),
+            pltpu.SemaphoreType.DMA((10,)),
+            pltpu.SemaphoreType.DMA((2, len(got))),
         ],
-        compiler_params=params(16),
+        compiler_params=params(24),
         name="subspace",
-    )(place, *own, *cross, start)
+    )(place, diagonal, head, start, *cross, *kept, *got)
 
 
 def split(value):
@@ -276,6 +341,33 @@
 
 def pick(parts, rows):
     return parts[0][rows], parts[1][rows]
+
+
+def project(place_ref, basis_ref, fields_ref, own_rows_ref, slab_refs, value_ref):
+    x, z, index = place_ref[0], place_ref[3], place_ref[4]
+    species, half, width = fields_ref.shape[1:]
+    near = split(basis_ref[:, pl.ds(pl.multiple_of(x * half, 128), half)])
+    far = split(basis_ref[:, pl.ds(pl.multiple_of((1 - x) * half, 128), half)])
+    slabs = len(slab_refs)
+    rows = slab_refs[0].shape[2]
+    for first in range(0, species, 2):
+
+        def two(side):
+            return split(jnp.concatenate([fields_ref[side, first], fields_ref[side, first + 1]], axis=1))
+
+        value_ref[...] = dot3(near, two(0), NN) + dot3(far, two(1), NN)
+        for step in range(slabs):
+            at = pl.multiple_of(lax.rem(z + step, slabs) * rows, 8)
+            for j in range(2):
+                slab_refs[step][first + j, 0] = value_ref[
+                    pl.ds(at, rows), width * j : width * (j + 1)
+                ]
+    count_rows = own_rows_ref.shape[0]
+    per_tile = 128 // count_rows
+    tile = basis_ref[:, pl.ds(pl.multiple_of(index // per_tile * 128, 128), 128)].T
+    shift = lax.rem(index, per_tile)
+    value_ref[:, :width] = tile
+    own_rows_ref[...] = value_ref[pl.ds(pl.multiple_of(shift * count_rows, 8), count_rows), :width]
 
 
 def own_kernel(place_ref, field_ref, keep_ref, send_ref, total_ref):
@@ -326,7 +418,7 @@
     return [slots[i : i + 2] for i in range(0, len(slots), 2)]
 
 
-def cross_kernel(count, last, place_ref, *refs):
+def cross_kernel(count, last, halves, place_ref, *refs):
     got_refs, kept_refs = refs[:count], refs[count : 2 * count]
     refs = refs[2 * count :]
     x, core = place_ref[0], place_ref[2]
@@ -347,26 +439,19 @@
             total = value if total is None else total + value
         return total
 
-    keep_at = pl.multiple_of(core * rows, 8)
-    send_at = pl.multiple_of((1 - core) * rows, 8)
-    if last:
-        so_far_keep, so_far_send, keep_ref, send_ref = refs
-        send_ref[...] = so_far_send[...] + product(send_at)
-        keep_ref[...] = so_far_keep[...] + product(keep_at)
-    else:
-        keep_ref, send_ref = refs
-        send_ref[...] = product(send_at)
-        keep_ref[...] = product(keep_at)
-
-
-def cross_block(place, got, kept, so_far):
+    for name, so_far, out in zip(halves, refs, refs[-len(halves) :]):
+        at = pl.multiple_of((core if name == "keep" else 1 - core) * rows, 8)
+        out[...] = product(at) + so_far[...] if last else product(at)
+
+
+def cross_block(place, got, kept, halves, so_far=()):
     half = got[0].shape[2]
     shape = jax.ShapeDtypeStruct((half // 2, half), jnp.float32)
     return pl.pallas_call(
-        functools.partial(cross_kernel, len(got), bool(so_far)),
-        out_shape=[shape, shape],
+        functools.partial(cross_kernel, len(got), bool(so_far), halves),
+        out_shape=[shape] * len(halves),
         in_specs=[SMEM_SPEC] + [VMEM_SPEC] * (2 * len(got) + len(so_far)),
-        out_specs=[VMEM_SPEC] * 2,
+        out_specs=[VMEM_SPEC] * len(halves),
         compiler_params=params(24),
         name="cross_block",
     )(place, *got, *kept, *so_far)
@@ -392,52 +477,6 @@
     )(place, left, right)
 
 
-def project_kernel(count, place_ref, basis_ref, *refs):
-    got_refs, kept_refs = refs[:count], refs[count : 2 * count]
-    own_rows_ref, slab_refs, value_ref = refs[2 * count], refs[2 * count + 1 : -1], refs[-1]
-    x, z, index = place_ref[0], place_ref[3], place_ref[4]
-    half = got_refs[0].shape[2]
-    width = got_refs[0].shape[3]
-    near = split(basis_ref[:, pl.ds(pl.multiple_of(x * half, 128), half)])
-    far = split(basis_ref[:, pl.ds(pl.multiple_of((1 - x) * half, 128), half)])
-    slabs = len(slab_refs)
-    rows = slab_refs[0].shape[2]
-    for number, pair in enumerate(species_pairs(got_refs)):
-        def two(refs):
-            return split(jnp.concatenate([refs[i][s, 0] for i, s in pair], axis=1))
-
-        value_ref[...] = dot3(near, two(kept_refs), NN) + dot3(far, two(got_refs), NN)
-        for step in range(slabs):
-            at = pl.multiple_of(lax.rem(z + step, slabs) * rows, 8)
-            for j in range(len(pair)):
-                slab_refs[step][2 * number + j, 0] = value_ref[
-                    pl.ds(at, rows), width * j : width * (j + 1)
-                ]
-    count_rows = own_rows_ref.shape[0]
-    per_tile = 128 // count_rows
-    tile = basis_ref[:, pl.ds(pl.multiple_of(index // per_tile * 128, 128), 128)].T
-    shift = lax.rem(index, per_tile)
-    value_ref[:, :width] = tile
-    own_rows_ref[...] = value_ref[pl.ds(pl.multiple_of(shift * count_rows, 8), count_rows), :width]
-
-
-def project_slabs(place, basis, got, kept, slabs, own_rows):
-    rank = basis.shape[0]
-    species = sum(piece.shape[0] for piece in got)
-    width = got[0].shape[3]
-    slab = jax.ShapeDtypeStruct((species, 1, rank // slabs, width), jnp.float32)
-    rows = jax.ShapeDtypeStruct((own_rows, rank), jnp.float32)
-    return pl.pallas_call(
-        functools.partial(project_kernel, len(got)),
-        out_shape=[rows] + [slab] * slabs,
-        in_specs=[SMEM_SPEC] + [VMEM_SPEC] * (1 + 2 * len(got)),
-        out_specs=[VMEM_SPEC] * (1 + slabs),
-        scratch_shapes=[pltpu.VMEM((rank, 2 * width), jnp.float32)],
-        compiler_params=params(24),
-        name="project",
-    )(place, basis, *got, *kept)
-
-
 def join_kernel(place_ref, *refs):
     out_ref = refs[-1]
     slabs = len(refs) - 1
@@ -493,11 +532,6 @@
     size = lax.axis_size("gy")
     shares = [lax.ppermute(array, "gy", turn(size, step)) for step in range(1, size)]
     return sum(after(shares, others), array)
-
-
-def gather_pieces(array):
-    near = [array] + [send_corner(array, dx, dy) for dx, dy in CORNERS]
-    return near + [send_core(piece) for piece in near]
 
 
 def chunk_sizes(species):
@@ -531,26 +565,39 @@
     kept = [chunk(own_field, x, i) for i in range(len(sizes))]
     start_t = start.T
     *early_got, final_got = got
-    so_far = cross_block(place, early_got, kept[:-1], ())
-    own = sum_z(own, so_far, kept, start_t)
+    so_far_send, so_far_keep = cross_block(place, early_got, kept[:-1], ("send", "keep"))
+    own = sum_z(own, so_far_send, so_far_keep, kept, start_t)
     beside = send_corner(own, 0, 1)
 
-    final_got = after(final_got, beside)
-    cross_keep, cross_send = cross_block(place, [final_got], kept[-1:], so_far)
-    cross, *shares = sum_quarters(place, cross_keep, send_core(cross_send))
+    final_got = after(final_got, own)
+    (cross_send,) = cross_block(place, [final_got], kept[-1:], ("send",), (so_far_send,))
+    cross_sent = send_core(after(cross_send, beside))
+    (cross_keep,) = cross_block(
+        place, [final_got], kept[-1:], ("keep",), (after(so_far_keep, cross_send),)
+    )
+    cross, *shares = sum_quarters(place, cross_keep, cross_sent)
     shares = [send_corner(share, dx, dy) for share, (dx, dy) in zip(shares, CORNERS)]
     own, beside = after((own, beside), shares[0])
     cross = sum(shares, cross)
-    far, far_beside = send_corner(own, 1, 0), send_corner(beside, 1, 0)
-    own_pieces = [own, far, beside, far_beside]
+    own_pieces = [own, send_corner(own, 1, 0), beside, send_corner(beside, 1, 0)]
     own_pieces = own_pieces + [send_core(piece) for piece in own_pieces]
-    cross_pieces = gather_pieces(sum_z(cross, far, far_beside))
-
-    basis = subspace_pieces(place, own_pieces, cross_pieces, start_t, 1.0 / columns)
-    devices = lax.axis_size(("gx", "gy", "sa"))
+    cross = sum_z(cross, own_pieces[:4])
+    diagonal, head = diagonal_blocks(place, own_pieces, start_t)
+    near = [cross] + [send_corner(cross, dx, dy) for dx, dy in CORNERS]
+    cross_pieces = near + [send_core(after(piece, head)) for piece in near]
+
     slabs = lax.axis_size("gy")
-    own_rows, *projected = project_slabs(
-        place, basis, early_got + [final_got], kept, slabs, start.shape[0] // devices
+    own_rows, *projected = subspace_pieces(
+        place,
+        diagonal,
+        head,
+        start_t,
+        cross_pieces,
+        kept,
+        early_got + [final_got],
+        1.0 / columns,
+        slabs,
+        start.shape[0] // lax.axis_size(("gx", "gy", "sa")),
     )
     arrived = [projected[0]] + [
         lax.ppermute(projected[i], "gy", turn(slabs, i)) for i in range(1, slabs)

time: 134 us -> 129 us (0.963)
  waiting for transfers between devices: 47 us -> 38.7 us
  starting transfers between devices: 32.5 us -> 36.1 us
    ppermute x6, waiting for transfers between devices: 12.2 us -> 6.09 us  [sum_z(): lax.ppermute(array, 'gy', turn(size, step))]
    ppermute x10, waiting for transfers between devices: 13.8 us -> 10.4 us  [send_corner(): return lax.ppermute(array, ('gx', 'sa'), pairs)]
    ppermute x6, starting transfers between devices: 8.99 us -> 11.6 us  [sum_z(): lax.ppermute(array, 'gy', turn(size, step))]
    ppermute x3, waiting for transfers between devices: 8.05 us -> 9.58 us  [on_halves(): got = [lax.ppermute(piece, 'gx', flip(2, 1)) for piece in sent]]
    pallas_call x4 -> x5, Pallas kernels: 30.9 us -> 30.4 us  [the longest x1 23.6 us: subspace_pieces(): pl.pallas_call(functools.partial(pieces_kernel, scale, len(got)), out_sha...]
  transfers between devices with their start and end apart: 32 -> 32, of which waited for: 19 -> 19; matrix products, arithmetic and copies ran while one was open for 9% -> 9% of each run, Pallas kernels for 7% -> 10%
where the time goes in v4:
time: 129 us; the launch traced here: 128 us
  Pallas kernels  38.9 us (30%)
  waiting for transfers between devices  38.7 us (30%)
  starting transfers between devices  36.1 us (28%)
  local copies, waits for them, and re-layouts  10.5 us (8%)
  other arithmetic  3 us (2%)
    pallas_call x1, Pallas kernels, subspace_pieces(): pl.pallas_call(functools.partial(pieces_kernel, scale, len(got)), out_sha...  23.6 us
    ppermute x10, starting transfers between devices, send_corner(): return lax.ppermute(array, ('gx', 'sa'), pairs)  13.8 us
    ppermute x6, starting transfers between devices, sum_z(): lax.ppermute(array, 'gy', turn(size, step))  11.6 us
    ppermute x10, waiting for transfers between devices, send_corner(): return lax.ppermute(array, ('gx', 'sa'), pairs)  10.4 us
    ppermute x3, waiting for transfers between devices, on_halves(): got = [lax.ppermute(piece, 'gx', flip(2, 1)) for piece in sent]  9.58 us
    ppermute x3, waiting for transfers between devices, on_halves(): lax.ppermute(projected[i], 'gy', turn(slabs, i))  8.62 us
    dynamic_slice x5, local copies, waits for them, and re-layouts, chunk(): lax.dynamic_slice_in_dim(source, owner * species + starts[i], sizes[i], 0)  8.59 us
    pallas_call x1, Pallas kernels, own_blocks(): pl.pallas_call(own_kernel, grid=(field.shape[0] // step,), out_shape=[sha...  6.54 us
  transfers between devices with their start and end apart: 32, of which 19 were waited for; matrix products, arithmetic and copies ran while one was open for 9% of the time, Pallas kernels for 10%

profile of v4, /device:TPU:0, one launch (start us, length us, event | category | flops | bytes accessed | tf_op | source)
XLA Modules:
  0.0 128.0 jit_solution(10058101535581949899)
XLA Ops:
  0.6 2.1 %constant_dynamic-slice_fusion.5 = f32[3,1,512,128]{3,2,1,0:T(8,128)} fusion(f32[16,1,512,128]{3,2,1,0:T(8,128)} %field_ref, s32[]{:T(128)S(6)} %select_n.38), kind=kLoop, calls=%fused_computation.10 | loop fusion | bytes 1572868 | tf_op jit(solution)/shard_map/dynamic_slice | solution.py:554
  2.7 2.9 %collective-permute-start.1 = (f32[3,1,512,128]{3,2,1,0:T(8,128)}, f32[3,1,512,128]{3,2,1,0:T(8,128)}, u32[]{:S(2)}, u32[]{:S(2)}) collective-permute-start(f32[3,1,512,128]{3,2,1,0:T(8,128)} %constant_dynamic-slice_fusion.5), channel_id=1, source_target_pairs={{0,16},{16,0},{1,17},{17,1},{2,18},{18,2},{3,19},{19,3},{4,20},{20... | collective-permute-start | bytes 2359304 | tf_op jit(solution)/shard_map/ppermute | solution.py:559
  5.6 2.1 %constant_dynamic-slice_fusion.4 = f32[3,1,512,128]{3,2,1,0:T(8,128)} fusion(f32[16,1,512,128]{3,2,1,0:T(8,128)} %field_ref, s32[]{:T(128)S(6)} %select_n.39), kind=kLoop, calls=%fused_computation.9 | loop fusion | bytes 1572868 | tf_op jit(solution)/shard_map/dynamic_slice | solution.py:554
  7.7 1.9 %constant_dynamic-slice_fusion.3 = f32[2,1,512,128]{3,2,1,0:T(8,128)} fusion(f32[16,1,512,128]{3,2,1,0:T(8,128)} %field_ref, s32[]{:T(128)S(6)} %select_n.40), kind=kLoop, calls=%fused_computation.8 | loop fusion | bytes 1048580 | tf_op jit(solution)/shard_map/dynamic_slice | solution.py:554
  9.6 0.7 stack.23.place_ref
  10.3 6.5 %own_blocks.1 = (f32[160,512]{1,0:T(8,128)}, f32[160,512]{1,0:T(8,128)}) custom-call(s32[5]{0:T(128)} %stack.23.place_ref, f32[16,1,512,128]{3,2,1,0:T(8,128)} %field_ref), custom_call_target="tpu_custom_call" | custom-call | flops 199999995904 | bytes 4194304 | tf_op jit(solution)/shard_map/own_blocks/pallas_call | solution.py:403
  16.8 0.0 collective-permute-start.6
  16.9 1.8 %collective-permute-done = f32[160,512]{1,0:T(8,128)S(1)} collective-permute-done((f32[160,512]{1,0:T(8,128)}, f32[160,512]{1,0:T(8,128)S(1)}, u32[]{:S(2)}, u32[]{:S(2)}) %collective-permute-start) | collective-permute-done | bytes 327712 | tf_op jit(solution)/shard_map/ppermute | solution.py:522
  18.7 1.0 add.98
  19.7 4.6 %collective-permute-done.1.refs_0_.refs_14_ = f32[3,1,512,128]{3,2,1,0:T(8,128)} collective-permute-done((f32[3,1,512,128]{3,2,1,0:T(8,128)}, f32[3,1,512,128]{3,2,1,0:T(8,128)}, u32[]{:S(2)}, u32[]{:S(2)}) %collective-permute-start.1) | collective-permute-done | bytes 786464 | tf_op jit(solution)/shard_map/ppermute | solution.py:559
  24.3 2.2 %collective-permute-start.2 = (f32[80,512]{1,0:T(8,128)S(1)}, f32[80,512]{1,0:T(8,128)S(1)}, u32[]{:S(2)}, u32[]{:S(2)}) collective-permute-start(f32[80,512]{1,0:T(8,128)S(1)} %dynamic-slice_bitcast_fusion), channel_id=1, source_target_pairs={{0,2},{1,3},{2,0},{3,1},{16,18},{17,19},{18,16},{19,17},{4,6},{5,7... | collective-permute-start | bytes 491528 | tf_op jit(solution)/shard_map/ppermute | solution.py:528
  26.5 1.5 %collective-permute-start.8 = (f32[2,1,512,128]{3,2,1,0:T(8,128)}, f32[2,1,512,128]{3,2,1,0:T(8,128)S(1)}, u32[]{:S(2)}, u32[]{:S(2)}) collective-permute-start(f32[2,1,512,128]{3,2,1,0:T(8,128)} %constant_dynamic-slice_fusion.3), channel_id=1, source_target_pairs={{0,16},{16,0},{1,17},{17,1},{2,18},{18,2},{3,19},{19,3},{4,20},{20... | collective-permute-start | bytes 1572872 | tf_op jit(solution)/shard_map/ppermute | solution.py:559
  28.0 1.8 %collective-permute-done.2 = f32[80,512]{1,0:T(8,128)S(1)} collective-permute-done((f32[80,512]{1,0:T(8,128)S(1)}, f32[80,512]{1,0:T(8,128)S(1)}, u32[]{:S(2)}, u32[]{:S(2)}) %collective-permute-start.2) | collective-permute-done | bytes 163872 | tf_op jit(solution)/shard_map/ppermute | solution.py:528
  29.8 0.7 bitcast_add_fusion
  30.5 2.1 %collective-permute-start.3 = (f32[80,512]{1,0:T(8,128)}, f32[80,512]{1,0:T(8,128)}, u32[]{:S(2)}, u32[]{:S(2)}) collective-permute-start(f32[80,512]{1,0:T(8,128)} %bitcast_add_fusion), channel_id=1, source_target_pairs={{0,4},{4,8},{8,12},{12,0},{1,5},{5,9},{9,13},{13,1},{2,6},{6,10},{... | collective-permute-start | bytes 491528 | tf_op jit(solution)/shard_map/ppermute | solution.py:533
  32.6 2.6 %collective-permute-start.4 = (f32[80,512]{1,0:T(8,128)}, f32[80,512]{1,0:T(8,128)}, u32[]{:S(2)}, u32[]{:S(2)}) collective-permute-start(f32[80,512]{1,0:T(8,128)} %bitcast_add_fusion), channel_id=1, source_target_pairs={{0,8},{4,12},{8,0},{12,4},{1,9},{5,13},{9,1},{13,5},{2,10},{6,14},... | collective-permute-start | bytes 491528 | tf_op jit(solution)/shard_map/ppermute | solution.py:533
  35.2 1.3 %collective-permute-start.5 = (f32[80,512]{1,0:T(8,128)}, f32[80,512]{1,0:T(8,128)}, u32[]{:S(2)}, u32[]{:S(2)}) collective-permute-start(f32[80,512]{1,0:T(8,128)} %bitcast_add_fusion), channel_id=1, source_target_pairs={{0,12},{4,0},{8,4},{12,8},{1,13},{5,1},{9,5},{13,9},{2,14},{6,2},{... | collective-permute-start | bytes 491528 | tf_op jit(solution)/shard_map/ppermute | solution.py:533
  36.5 1.5 %constant_dynamic-slice_fusion.1 = (f32[3,1,512,128]{3,2,1,0:T(8,128)S(1)}, f32[3,1,512,128]{3,2,1,0:T(8,128)S(1)}) fusion(f32[16,1,512,128]{3,2,1,0:T(8,128)} %field_ref, s32[]{:T(128)S(6)} %select_n.44, s32[]{:T(128)S(6)} %select_n.43), kind=kLoop, calls=%fused_computation.6 | loop fusion | bytes 3145736 | tf_op jit(solution)/shard_map/dynamic_slice | solution.py:554
  38.0 1.2 copy.4
  39.2 1.1 constant_dynamic-slice_fusion.refs_1_.refs_13_
  40.3 0.8 collective-permute-done.6.refs_1_.refs_15_
  41.1 2.8 %cross_block.3 = (f32[256,512]{1,0:T(8,128)S(1)}, f32[256,512]{1,0:T(8,128)S(1)}) custom-call(s32[5]{0:T(128)S(1)} %copy-done, f32[3,1,512,128]{3,2,1,0:T(8,128)} %collective-permute-done.1.refs_0_.refs_14_, f32[3,1,512,128]{3,2,1,0:T(8,128)S(1)} %collective-permute-done.6.refs_1_.refs_15_, f32[3,1,512,128]{3,2,1,0:T(8,128)S(1)} %get-tuple-element.69.refs_2_.refs_11_, ...), custom_call_target="tpu_custom_call" | custom-call | tf_op jit(solution)/shard_map/cross_block/pallas_call | solution.py:450
  43.9 0.1 collective-permute-done.4
  44.0 1.2 add_add_fusion.refs_0_
  45.2 2.1 %collective-permute-start.7 = (f32[80,512]{1,0:T(8,128)S(1)}, f32[80,512]{1,0:T(8,128)S(1)}, u32[]{:S(2)}, u32[]{:S(2)}) collective-permute-start(f32[80,512]{1,0:T(8,128)S(1)} %add_add_fusion.refs_0_), channel_id=1, source_target_pairs={{0,2},{1,3},{2,0},{3,1},{16,18},{17,19},{18,16},{19,17},{4,6},{5,7... | collective-permute-start | bytes 491528 | tf_op jit(solution)/shard_map/ppermute | solution.py:528
  47.3 4.2 %collective-permute-done.8.refs_0_.refs_16_ = f32[2,1,512,128]{3,2,1,0:T(8,128)S(1)} collective-permute-done((f32[2,1,512,128]{3,2,1,0:T(8,128)}, f32[2,1,512,128]{3,2,1,0:T(8,128)S(1)}, u32[]{:S(2)}, u32[]{:S(2)}) %collective-permute-start.8) | collective-permute-done | bytes 524320 | tf_op jit(solution)/shard_map/ppermute | solution.py:559
  51.5 1.0 cross_block.4
  52.5 0.1 collective-permute-start.9
  52.5 1.0 cross_block.5.left_ref
  53.5 0.9 collective-permute-done.9.right_ref
  54.4 0.6 quarters.1
  55.1 1.8 %collective-permute-start.10 = (f32[64,512]{1,0:T(8,128)S(1)}, f32[64,512]{1,0:T(8,128)S(1)}, u32[]{:S(2)}, u32[]{:S(2)}) collective-permute-start(f32[64,512]{1,0:T(8,128)S(1)} %get-tuple-element.48), channel_id=1, source_target_pairs={{0,16},{1,17},{2,18},{3,19},{16,0},{17,1},{18,2},{19,3},{4,20},{5,... | collective-permute-start | bytes 393224 | tf_op jit(solution)/shard_map/ppermute | solution.py:528
  56.9 1.5 %collective-permute-start.17 = (f32[64,512]{1,0:T(8,128)S(1)}, f32[64,512]{1,0:T(8,128)S(1)}, u32[]{:S(2)}, u32[]{:S(2)}) collective-permute-start(f32[64,512]{1,0:T(8,128)S(1)} %get-tuple-element.54), channel_id=1, source_target_pairs={{0,2},{1,3},{2,0},{3,1},{16,18},{17,19},{18,16},{19,17},{4,6},{5,7... | collective-permute-start | bytes 393224 | tf_op jit(solution)/shard_map/ppermute | solution.py:528
  58.4 0.2 collective-permute-start.18
  58.6 2.2 %collective-permute-done.10 = f32[64,512]{1,0:T(8,128)S(1)} collective-permute-done((f32[64,512]{1,0:T(8,128)S(1)}, f32[64,512]{1,0:T(8,128)S(1)}, u32[]{:S(2)}, u32[]{:S(2)}) %collective-permute-start.10) | collective-permute-done | bytes 131104 | tf_op jit(solution)/shard_map/ppermute | solution.py:528
  60.8 2.4 %collective-permute-start.11 = (f32[80,512]{1,0:T(8,128)S(1)}, f32[80,512]{1,0:T(8,128)S(1)}, u32[]{:S(2)}, u32[]{:S(2)}) collective-permute-start(f32[80,512]{1,0:T(8,128)S(1)} %add_add_fusion.refs_0_), channel_id=1, source_target_pairs={{0,16},{1,17},{2,18},{3,19},{16,0},{17,1},{18,2},{19,3},{4,20},{5,... | collective-permute-start | bytes 491528 | tf_op jit(solution)/shard_map/ppermute | solution.py:528
  63.2 0.9 collective-permute-done.17
  64.2 1.5 %collective-permute-done.18 = f32[64,512]{1,0:T(8,128)S(1)} collective-permute-done((f32[64,512]{1,0:T(8,128)S(1)}, f32[64,512]{1,0:T(8,128)S(1)}, u32[]{:S(2)}, u32[]{:S(2)}) %collective-permute-start.18) | collective-permute-done | bytes 131104 | tf_op jit(solution)/shard_map/ppermute | solution.py:528
  65.7 1.6 %collective-permute-start.19 = (f32[64,512]{1,0:T(8,128)S(1)}, f32[64,512]{1,0:T(8,128)S(1)}, u32[]{:S(2)}, u32[]{:S(2)}) collective-permute-start(f32[64,512]{1,0:T(8,128)S(1)} %add_add_fusion.2), channel_id=1, source_target_pairs={{0,4},{4,8},{8,12},{12,0},{1,5},{5,9},{9,13},{13,1},{2,6},{6,10},{... | collective-permute-start | bytes 393224 | tf_op jit(solution)/shard_map/ppermute | solution.py:533
  67.4 2.6 %collective-permute-start.20 = (f32[64,512]{1,0:T(8,128)S(1)}, f32[64,512]{1,0:T(8,128)S(1)}, u32[]{:S(2)}, u32[]{:S(2)}) collective-permute-start(f32[64,512]{1,0:T(8,128)S(1)} %add_add_fusion.2), channel_id=1, source_target_pairs={{0,8},{4,12},{8,0},{12,4},{1,9},{5,13},{9,1},{13,5},{2,10},{6,14},... | collective-permute-start | bytes 393224 | tf_op jit(solution)/shard_map/ppermute | solution.py:533
  69.9 1.3 %collective-permute-start.21 = (f32[64,512]{1,0:T(8,128)S(1)}, f32[64,512]{1,0:T(8,128)S(1)}, u32[]{:S(2)}, u32[]{:S(2)}) collective-permute-start(f32[64,512]{1,0:T(8,128)S(1)} %add_add_fusion.2), channel_id=1, source_target_pairs={{0,12},{4,0},{8,4},{12,8},{1,13},{5,1},{9,5},{13,9},{2,14},{6,2},{... | collective-permute-start | bytes 393224 | tf_op jit(solution)/shard_map/ppermute | solution.py:533
  71.3 2.8 %collective-permute-done.19 = f32[64,512]{1,0:T(8,128)S(1)} collective-permute-done((f32[64,512]{1,0:T(8,128)S(1)}, f32[64,512]{1,0:T(8,128)S(1)}, u32[]{:S(2)}, u32[]{:S(2)}) %collective-permute-start.19) | collective-permute-done | bytes 131104 | tf_op jit(solution)/shard_map/ppermute | solution.py:533
  74.1 3.2 %collective-permute-done.20 = f32[64,512]{1,0:T(8,128)S(1)} collective-permute-done((f32[64,512]{1,0:T(8,128)S(1)}, f32[64,512]{1,0:T(8,128)S(1)}, u32[]{:S(2)}, u32[]{:S(2)}) %collective-permute-start.20) | collective-permute-done | bytes 131104 | tf_op jit(solution)/shard_map/ppermute | solution.py:533
  77.3 0.6 collective-permute-start.14
  77.9 0.1 collective-permute-start.16
  78.0 1.4 %collective-permute-start.24 = (f32[64,512]{1,0:T(8,128)S(1)}, f32[64,512]{1,0:T(8,128)S(1)}, u32[]{:S(2)}, u32[]{:S(2)}) collective-permute-start(f32[64,512]{1,0:T(8,128)S(1)} %add_add_fusion.1.refs_3_), channel_id=1, source_target_pairs={{0,18},{1,19},{2,16},{3,17},{16,2},{17,3},{18,0},{19,1},{4,22},{5,... | collective-permute-start | bytes 393224 | tf_op jit(solution)/shard_map/ppermute | solution.py:528
  79.4 1.5 %collective-permute-start.23 = (f32[64,512]{1,0:T(8,128)S(1)}, f32[64,512]{1,0:T(8,128)S(1)}, u32[]{:S(2)}, u32[]{:S(2)}) collective-permute-start(f32[64,512]{1,0:T(8,128)S(1)} %add_add_fusion.1.refs_3_), channel_id=1, source_target_pairs={{0,2},{1,3},{2,0},{3,1},{16,18},{17,19},{18,16},{19,17},{4,6},{5,7... | collective-permute-start | bytes 393224 | tf_op jit(solution)/shard_map/ppermute | solution.py:528
  80.9 0.7 collective-permute-start.22
  81.6 2.0 %diagonal.1 = (f32[2,512,512]{2,1,0:T(8,128)S(1)}, f32[128,1024]{1,0:T(8,128)S(1)}) custom-call(s32[5]{0:T(128)S(1)} %copy-done, f32[80,512]{1,0:T(8,128)S(1)} %add_add_fusion.refs_0_, f32[80,512]{1,0:T(8,128)S(1)} %collective-permute-done.11.refs_1_, f32[80,512]{1,0:T(8,128)S(1)} %collective-permute-done.7.refs_2_, ...), custom_call_target="tpu_custom_call" | custom-call | tf_op jit(solution)/shard_map/diagonal/pallas_call | solution.py:236
  83.6 1.7 %collective-permute-done.24.refs_6_ = f32[64,512]{1,0:T(8,128)S(1)} collective-permute-done((f32[64,512]{1,0:T(8,128)S(1)}, f32[64,512]{1,0:T(8,128)S(1)}, u32[]{:S(2)}, u32[]{:S(2)}) %collective-permute-start.24) | collective-permute-done | bytes 131104 | tf_op jit(solution)/shard_map/ppermute | solution.py:528
  85.3 2.3 %collective-permute-done.23.refs_5_ = f32[64,512]{1,0:T(8,128)S(1)} collective-permute-done((f32[64,512]{1,0:T(8,128)S(1)}, f32[64,512]{1,0:T(8,128)S(1)}, u32[]{:S(2)}, u32[]{:S(2)}) %collective-permute-start.23) | collective-permute-done | bytes 131104 | tf_op jit(solution)/shard_map/ppermute | solution.py:528
  87.6 0.0 collective-permute-start.27
  87.6 0.5 collective-permute-start.26
  88.1 0.0 collective-permute-start.25
  88.2 0.8 collective-permute-done.27.refs_9_
  89.0 0.2 collective-permute-done.26.refs_8_
  89.1 0.3 collective-permute-done.25.refs_7_
  89.5 23.6 %subspace.1 = (f32[32,128]{1,0:T(8,128)}, f32[8,1,32,128]{3,2,1,0:T(8,128)S(1)}, f32[8,1,32,128]{3,2,1,0:T(8,128)S(1)}, f32[8,1,32,128]{3,2,1,0:T(8,128)S(1)}, f32[8,1,32,128]{3,2,1,0:T(8,128)S(1)}) custom-call(s32[5]{0:T(128)S(1)} %copy-done, f32[2,512,512]{2,1,0:T(8,128)S(1)} %get-tuple-element.51.refs_0_, f32[128,1024]{1,0:T(8,128)S(1)} %get-tuple-element.52.refs_1_, ...), custom_call_target="tpu_custom_call" | custom-call | tf_op jit(solution)/shard_map/subspace/pallas_call | solution.py:308
  113.1 2.5 %collective-permute-start.29 = (f32[8,1,32,128]{3,2,1,0:T(8,128)S(1)}, f32[8,1,32,128]{3,2,1,0:T(8,128)S(1)}, u32[]{:S(2)}, u32[]{:S(2)}) collective-permute-start(f32[8,1,32,128]{3,2,1,0:T(8,128)S(1)} %get-tuple-element.64), channel_id=1, source_target_pairs={{0,4},{4,8},{8,12},{12,0},{1,5},{5,9},{9,13},{13,1},{2,6},{6,10},{... | collective-permute-start | bytes 393224 | tf_op jit(solution)/shard_map/ppermute | solution.py:603
  115.6 2.1 %collective-permute-start.30 = (f32[8,1,32,128]{3,2,1,0:T(8,128)S(1)}, f32[8,1,32,128]{3,2,1,0:T(8,128)S(1)}, u32[]{:S(2)}, u32[]{:S(2)}) collective-permute-start(f32[8,1,32,128]{3,2,1,0:T(8,128)S(1)} %get-tuple-element.65), channel_id=1, source_target_pairs={{0,8},{4,12},{8,0},{12,4},{1,9},{5,13},{9,1},{13,5},{2,10},{6,14},... | collective-permute-start | bytes 393224 | tf_op jit(solution)/shard_map/ppermute | solution.py:603
  117.6 0.4 collective-permute-start.31
  118.0 3.4 %collective-permute-done.29.refs_1_ = f32[8,1,32,128]{3,2,1,0:T(8,128)S(1)} collective-permute-done((f32[8,1,32,128]{3,2,1,0:T(8,128)S(1)}, f32[8,1,32,128]{3,2,1,0:T(8,128)S(1)}, u32[]{:S(2)}, u32[]{:S(2)}) %collective-permute-start.29) | collective-permute-done | bytes 131104 | tf_op jit(solution)/shard_map/ppermute | solution.py:603
  121.4 5.2 %collective-permute-done.30.refs_2_ = f32[8,1,32,128]{3,2,1,0:T(8,128)S(1)} collective-permute-done((f32[8,1,32,128]{3,2,1,0:T(8,128)S(1)}, f32[8,1,32,128]{3,2,1,0:T(8,128)S(1)}, u32[]{:S(2)}, u32[]{:S(2)}) %collective-permute-start.30) | collective-permute-done | bytes 131104 | tf_op jit(solution)/shard_map/ppermute | solution.py:603
  126.6 1.4 %join.1 = f32[8,1,32,512]{3,2,1,0:T(8,128)} custom-call(s32[5]{0:T(128)S(1)} %copy-done, f32[8,1,32,128]{3,2,1,0:T(8,128)S(1)} %get-tuple-element.63.refs_0_, f32[8,1,32,128]{3,2,1,0:T(8,128)S(1)} %collective-permute-done.29.refs_1_, f32[8,1,32,128]{3,2,1,0:T(8,128)S(1)} %collective-permute-done.30.refs_2_, f32[8,1,32,128]{3,2,1,0:T(8,128)S(1)} %collective-permute-done.31.refs_3_), custom_call_target="tpu_custom_call" | custom-call | tf_op jit(solution)/shard_map/join/pallas_call | solution.py:491
  (23 shorter events, 0.2 us)
Async XLA Ops:
  2.7 21.6 %collective-permute-start.1 = (f32[3,1,512,128]{3,2,1,0:T(8,128)}, f32[3,1,512,128]{3,2,1,0:T(8,128)}, u32[]{:S(2)}, u32[]{:S(2)}) collective-permute-start(f32[3,1,512,128]{3,2,1,0:T(8,128)} %constant_dynamic-slice_fusion.5), channel_id=1, source_target_pairs={{0,16},{16,0},{1,17},{17,1},{2,18},{18,2},{3,19},{19,3},{4,20},{20... | collective-permute-start | bytes 2359304 | tf_op jit(solution)/shard_map/ppermute | solution.py:559
  16.8 24.3 %copy-start = (s32[5]{0:T(128)S(1)}, s32[5]{0:T(128)}, u32[]{:S(2)}) copy-start(s32[5]{0:T(128)} %stack.23.place_ref) | copy-start | bytes 64
  16.8 1.8 %collective-permute-start = (f32[160,512]{1,0:T(8,128)}, f32[160,512]{1,0:T(8,128)S(1)}, u32[]{:S(2)}, u32[]{:S(2)}) collective-permute-start(f32[160,512]{1,0:T(8,128)} %get-tuple-element.38), channel_id=1, source_target_pairs={{0,1},{1,0},{2,3},{3,2},{4,5},{5,4},{6,7},{7,6},{8,9},{9,8},{10,11... | collective-permute-start | bytes 983048 | tf_op jit(solution)/shard_map/ppermute | solution.py:522
  16.8 24.2 %collective-permute-start.6 = (f32[3,1,512,128]{3,2,1,0:T(8,128)}, f32[3,1,512,128]{3,2,1,0:T(8,128)S(1)}, u32[]{:S(2)}, u32[]{:S(2)}) collective-permute-start(f32[3,1,512,128]{3,2,1,0:T(8,128)} %constant_dynamic-slice_fusion.4), channel_id=1, source_target_pairs={{0,16},{16,0},{1,17},{17,1},{2,18},{18,2},{3,19},{19,3},{4,20},{20... | collective-permute-start | bytes 2359304 | tf_op jit(solution)/shard_map/ppermute | solution.py:559
  24.3 5.5 %collective-permute-start.2 = (f32[80,512]{1,0:T(8,128)S(1)}, f32[80,512]{1,0:T(8,128)S(1)}, u32[]{:S(2)}, u32[]{:S(2)}) collective-permute-start(f32[80,512]{1,0:T(8,128)S(1)} %dynamic-slice_bitcast_fusion), channel_id=1, source_target_pairs={{0,2},{1,3},{2,0},{3,1},{16,18},{17,19},{18,16},{19,17},{4,6},{5,7... | collective-permute-start | bytes 491528 | tf_op jit(solution)/shard_map/ppermute | solution.py:528
  26.5 25.0 %collective-permute-start.8 = (f32[2,1,512,128]{3,2,1,0:T(8,128)}, f32[2,1,512,128]{3,2,1,0:T(8,128)S(1)}, u32[]{:S(2)}, u32[]{:S(2)}) collective-permute-start(f32[2,1,512,128]{3,2,1,0:T(8,128)} %constant_dynamic-slice_fusion.3), channel_id=1, source_target_pairs={{0,16},{16,0},{1,17},{17,1},{2,18},{18,2},{3,19},{19,3},{4,20},{20... | collective-permute-start | bytes 1572872 | tf_op jit(solution)/shard_map/ppermute | solution.py:559
  30.5 13.4 %collective-permute-start.3 = (f32[80,512]{1,0:T(8,128)}, f32[80,512]{1,0:T(8,128)}, u32[]{:S(2)}, u32[]{:S(2)}) collective-permute-start(f32[80,512]{1,0:T(8,128)} %bitcast_add_fusion), channel_id=1, source_target_pairs={{0,4},{4,8},{8,12},{12,0},{1,5},{5,9},{9,13},{13,1},{2,6},{6,10},{... | collective-permute-start | bytes 491528 | tf_op jit(solution)/shard_map/ppermute | solution.py:533
  32.6 11.4 %collective-permute-start.4 = (f32[80,512]{1,0:T(8,128)}, f32[80,512]{1,0:T(8,128)}, u32[]{:S(2)}, u32[]{:S(2)}) collective-permute-start(f32[80,512]{1,0:T(8,128)} %bitcast_add_fusion), channel_id=1, source_target_pairs={{0,8},{4,12},{8,0},{12,4},{1,9},{5,13},{9,1},{13,5},{2,10},{6,14},... | collective-permute-start | bytes 491528 | tf_op jit(solution)/shard_map/ppermute | solution.py:533
  35.2 8.9 %collective-permute-start.5 = (f32[80,512]{1,0:T(8,128)}, f32[80,512]{1,0:T(8,128)}, u32[]{:S(2)}, u32[]{:S(2)}) collective-permute-start(f32[80,512]{1,0:T(8,128)} %bitcast_add_fusion), channel_id=1, source_target_pairs={{0,12},{4,0},{8,4},{12,8},{1,13},{5,1},{9,5},{13,9},{2,14},{6,2},{... | collective-permute-start | bytes 491528 | tf_op jit(solution)/shard_map/ppermute | solution.py:533
  45.2 7.2 %collective-permute-start.7 = (f32[80,512]{1,0:T(8,128)S(1)}, f32[80,512]{1,0:T(8,128)S(1)}, u32[]{:S(2)}, u32[]{:S(2)}) collective-permute-start(f32[80,512]{1,0:T(8,128)S(1)} %add_add_fusion.refs_0_), channel_id=1, source_target_pairs={{0,2},{1,3},{2,0},{3,1},{16,18},{17,19},{18,16},{19,17},{4,6},{5,7... | collective-permute-start | bytes 491528 | tf_op jit(solution)/shard_map/ppermute | solution.py:528
  52.5 2.0 %collective-permute-start.9 = (f32[256,512]{1,0:T(8,128)S(1)}, f32[256,512]{1,0:T(8,128)S(1)}, u32[]{:S(2)}, u32[]{:S(2)}) collective-permute-start(f32[256,512]{1,0:T(8,128)S(1)} %cross_block.4), channel_id=1, source_target_pairs={{0,1},{1,0},{2,3},{3,2},{4,5},{5,4},{6,7},{7,6},{8,9},{9,8},{10,11... | collective-permute-start | bytes 1572872 | tf_op jit(solution)/shard_map/ppermute | solution.py:522
  55.1 5.7 %collective-permute-start.10 = (f32[64,512]{1,0:T(8,128)S(1)}, f32[64,512]{1,0:T(8,128)S(1)}, u32[]{:S(2)}, u32[]{:S(2)}) collective-permute-start(f32[64,512]{1,0:T(8,128)S(1)} %get-tuple-element.48), channel_id=1, source_target_pairs={{0,16},{1,17},{2,18},{3,19},{16,0},{17,1},{18,2},{19,3},{4,20},{5,... | collective-permute-start | bytes 393224 | tf_op jit(solution)/shard_map/ppermute | solution.py:528
  56.9 7.3 %collective-permute-start.17 = (f32[64,512]{1,0:T(8,128)S(1)}, f32[64,512]{1,0:T(8,128)S(1)}, u32[]{:S(2)}, u32[]{:S(2)}) collective-permute-start(f32[64,512]{1,0:T(8,128)S(1)} %get-tuple-element.54), channel_id=1, source_target_pairs={{0,2},{1,3},{2,0},{3,1},{16,18},{17,19},{18,16},{19,17},{4,6},{5,7... | collective-permute-start | bytes 393224 | tf_op jit(solution)/shard_map/ppermute | solution.py:528
  58.4 7.3 %collective-permute-start.18 = (f32[64,512]{1,0:T(8,128)S(1)}, f32[64,512]{1,0:T(8,128)S(1)}, u32[]{:S(2)}, u32[]{:S(2)}) collective-permute-start(f32[64,512]{1,0:T(8,128)S(1)} %get-tuple-element.55), channel_id=1, source_target_pairs={{0,18},{1,19},{2,16},{3,17},{16,2},{17,3},{18,0},{19,1},{4,22},{5,... | collective-permute-start | bytes 393224 | tf_op jit(solution)/shard_map/ppermute | solution.py:528
  60.8 16.5 %collective-permute-start.11 = (f32[80,512]{1,0:T(8,128)S(1)}, f32[80,512]{1,0:T(8,128)S(1)}, u32[]{:S(2)}, u32[]{:S(2)}) collective-permute-start(f32[80,512]{1,0:T(8,128)S(1)} %add_add_fusion.refs_0_), channel_id=1, source_target_pairs={{0,16},{1,17},{2,18},{3,19},{16,0},{17,1},{18,2},{19,3},{4,20},{5,... | collective-permute-start | bytes 491528 | tf_op jit(solution)/shard_map/ppermute | solution.py:528
  63.2 14.1 %collective-permute-start.12 = (f32[80,512]{1,0:T(8,128)S(1)}, f32[80,512]{1,0:T(8,128)S(1)}, u32[]{:S(2)}, u32[]{:S(2)}) collective-permute-start(f32[80,512]{1,0:T(8,128)S(1)} %collective-permute-done.7.refs_2_), channel_id=1, source_target_pairs={{0,16},{1,17},{2,18},{3,19},{16,0},{17,1},{18,2},{19,3},{4,20},{5,... | collective-permute-start | bytes 491528 | tf_op jit(solution)/shard_map/ppermute | solution.py:528
  65.7 8.3 %collective-permute-start.19 = (f32[64,512]{1,0:T(8,128)S(1)}, f32[64,512]{1,0:T(8,128)S(1)}, u32[]{:S(2)}, u32[]{:S(2)}) collective-permute-start(f32[64,512]{1,0:T(8,128)S(1)} %add_add_fusion.2), channel_id=1, source_target_pairs={{0,4},{4,8},{8,12},{12,0},{1,5},{5,9},{9,13},{13,1},{2,6},{6,10},{... | collective-permute-start | bytes 393224 | tf_op jit(solution)/shard_map/ppermute | solution.py:533
  67.4 9.9 %collective-permute-start.20 = (f32[64,512]{1,0:T(8,128)S(1)}, f32[64,512]{1,0:T(8,128)S(1)}, u32[]{:S(2)}, u32[]{:S(2)}) collective-permute-start(f32[64,512]{1,0:T(8,128)S(1)} %add_add_fusion.2), channel_id=1, source_target_pairs={{0,8},{4,12},{8,0},{12,4},{1,9},{5,13},{9,1},{13,5},{2,10},{6,14},... | collective-permute-start | bytes 393224 | tf_op jit(solution)/shard_map/ppermute | solution.py:533
  69.9 7.3 %collective-permute-start.21 = (f32[64,512]{1,0:T(8,128)S(1)}, f32[64,512]{1,0:T(8,128)S(1)}, u32[]{:S(2)}, u32[]{:S(2)}) collective-permute-start(f32[64,512]{1,0:T(8,128)S(1)} %add_add_fusion.2), channel_id=1, source_target_pairs={{0,12},{4,0},{8,4},{12,8},{1,13},{5,1},{9,5},{13,9},{2,14},{6,2},{... | collective-permute-start | bytes 393224 | tf_op jit(solution)/shard_map/ppermute | solution.py:533
  74.1 5.3 %collective-permute-start.13 = (f32[80,512]{1,0:T(8,128)S(1)}, f32[80,512]{1,0:T(8,128)S(1)}, u32[]{:S(2)}, u32[]{:S(2)}) collective-permute-start(f32[80,512]{1,0:T(8,128)S(1)} %add_add_fusion.refs_0_), channel_id=1, source_target_pairs={{0,1},{1,0},{2,3},{3,2},{4,5},{5,4},{6,7},{7,6},{8,9},{9,8},{10,11... | collective-permute-start | bytes 491528 | tf_op jit(solution)/shard_map/ppermute | solution.py:522
  77.3 3.6 %collective-permute-start.15 = (f32[80,512]{1,0:T(8,128)S(1)}, f32[80,512]{1,0:T(8,128)S(1)}, u32[]{:S(2)}, u32[]{:S(2)}) collective-permute-start(f32[80,512]{1,0:T(8,128)S(1)} %collective-permute-done.7.refs_2_), channel_id=1, source_target_pairs={{0,1},{1,0},{2,3},{3,2},{4,5},{5,4},{6,7},{7,6},{8,9},{9,8},{10,11... | collective-permute-start | bytes 491528 | tf_op jit(solution)/shard_map/ppermute | solution.py:522
  77.3 4.2 %collective-permute-start.14 = (f32[80,512]{1,0:T(8,128)S(1)}, f32[80,512]{1,0:T(8,128)S(1)}, u32[]{:S(2)}, u32[]{:S(2)}) collective-permute-start(f32[80,512]{1,0:T(8,128)S(1)} %collective-permute-done.11.refs_1_), channel_id=1, source_target_pairs={{0,1},{1,0},{2,3},{3,2},{4,5},{5,4},{6,7},{7,6},{8,9},{9,8},{10,11... | collective-permute-start | bytes 491528 | tf_op jit(solution)/shard_map/ppermute | solution.py:522
  77.9 3.7 %collective-permute-start.16 = (f32[80,512]{1,0:T(8,128)S(1)}, f32[80,512]{1,0:T(8,128)S(1)}, u32[]{:S(2)}, u32[]{:S(2)}) collective-permute-start(f32[80,512]{1,0:T(8,128)S(1)} %collective-permute-done.12.refs_3_), channel_id=1, source_target_pairs={{0,1},{1,0},{2,3},{3,2},{4,5},{5,4},{6,7},{7,6},{8,9},{9,8},{10,11... | collective-permute-start | bytes 491528 | tf_op jit(solution)/shard_map/ppermute | solution.py:522
  78.0 7.3 %collective-permute-start.24 = (f32[64,512]{1,0:T(8,128)S(1)}, f32[64,512]{1,0:T(8,128)S(1)}, u32[]{:S(2)}, u32[]{:S(2)}) collective-permute-start(f32[64,512]{1,0:T(8,128)S(1)} %add_add_fusion.1.refs_3_), channel_id=1, source_target_pairs={{0,18},{1,19},{2,16},{3,17},{16,2},{17,3},{18,0},{19,1},{4,22},{5,... | collective-permute-start | bytes 393224 | tf_op jit(solution)/shard_map/ppermute | solution.py:528
  79.4 8.2 %collective-permute-start.23 = (f32[64,512]{1,0:T(8,128)S(1)}, f32[64,512]{1,0:T(8,128)S(1)}, u32[]{:S(2)}, u32[]{:S(2)}) collective-permute-start(f32[64,512]{1,0:T(8,128)S(1)} %add_add_fusion.1.refs_3_), channel_id=1, source_target_pairs={{0,2},{1,3},{2,0},{3,1},{16,18},{17,19},{18,16},{19,17},{4,6},{5,7... | collective-permute-start | bytes 393224 | tf_op jit(solution)/shard_map/ppermute | solution.py:528
  80.9 6.8 %collective-permute-start.22 = (f32[64,512]{1,0:T(8,128)S(1)}, f32[64,512]{1,0:T(8,128)S(1)}, u32[]{:S(2)}, u32[]{:S(2)}) collective-permute-start(f32[64,512]{1,0:T(8,128)S(1)} %add_add_fusion.1.refs_3_), channel_id=1, source_target_pairs={{0,16},{1,17},{2,18},{3,19},{16,0},{17,1},{18,2},{19,3},{4,20},{5,... | collective-permute-start | bytes 393224 | tf_op jit(solution)/shard_map/ppermute | solution.py:528
  85.3 2.9 %collective-permute-start.28 = (f32[64,512]{1,0:T(8,128)S(1)}, f32[64,512]{1,0:T(8,128)S(1)}, u32[]{:S(2)}, u32[]{:S(2)}) collective-permute-start(f32[64,512]{1,0:T(8,128)S(1)} %collective-permute-done.24.refs_6_), channel_id=1, source_target_pairs={{0,1},{1,0},{2,3},{3,2},{4,5},{5,4},{6,7},{7,6},{8,9},{9,8},{10,11... | collective-permute-start | bytes 393224 | tf_op jit(solution)/shard_map/ppermute | solution.py:522
  87.6 1.3 %collective-permute-start.27 = (f32[64,512]{1,0:T(8,128)S(1)}, f32[64,512]{1,0:T(8,128)S(1)}, u32[]{:S(2)}, u32[]{:S(2)}) collective-permute-start(f32[64,512]{1,0:T(8,128)S(1)} %collective-permute-done.23.refs_5_), channel_id=1, source_target_pairs={{0,1},{1,0},{2,3},{3,2},{4,5},{5,4},{6,7},{7,6},{8,9},{9,8},{10,11... | collective-permute-start | bytes 393224 | tf_op jit(solution)/shard_map/ppermute | solution.py:522
  87.6 1.5 %collective-permute-start.26 = (f32[64,512]{1,0:T(8,128)S(1)}, f32[64,512]{1,0:T(8,128)S(1)}, u32[]{:S(2)}, u32[]{:S(2)}) collective-permute-start(f32[64,512]{1,0:T(8,128)S(1)} %collective-permute-done.22.refs_4_), channel_id=1, source_target_pairs={{0,1},{1,0},{2,3},{3,2},{4,5},{5,4},{6,7},{7,6},{8,9},{9,8},{10,11... | collective-permute-start | bytes 393224 | tf_op jit(solution)/shard_map/ppermute | solution.py:522
  88.1 1.3 %collective-permute-start.25 = (f32[64,512]{1,0:T(8,128)S(1)}, f32[64,512]{1,0:T(8,128)S(1)}, u32[]{:S(2)}, u32[]{:S(2)}) collective-permute-start(f32[64,512]{1,0:T(8,128)S(1)} %add_add_fusion.1.refs_3_), channel_id=1, source_target_pairs={{0,1},{1,0},{2,3},{3,2},{4,5},{5,4},{6,7},{7,6},{8,9},{9,8},{10,11... | collective-permute-start | bytes 393224 | tf_op jit(solution)/shard_map/ppermute | solution.py:522
  113.1 8.4 %collective-permute-start.29 = (f32[8,1,32,128]{3,2,1,0:T(8,128)S(1)}, f32[8,1,32,128]{3,2,1,0:T(8,128)S(1)}, u32[]{:S(2)}, u32[]{:S(2)}) collective-permute-start(f32[8,1,32,128]{3,2,1,0:T(8,128)S(1)} %get-tuple-element.64), channel_id=1, source_target_pairs={{0,4},{4,8},{8,12},{12,0},{1,5},{5,9},{9,13},{13,1},{2,6},{6,10},{... | collective-permute-start | bytes 393224 | tf_op jit(solution)/shard_map/ppermute | solution.py:603
  115.6 11.1 %collective-permute-start.30 = (f32[8,1,32,128]{3,2,1,0:T(8,128)S(1)}, f32[8,1,32,128]{3,2,1,0:T(8,128)S(1)}, u32[]{:S(2)}, u32[]{:S(2)}) collective-permute-start(f32[8,1,32,128]{3,2,1,0:T(8,128)S(1)} %get-tuple-element.65), channel_id=1, source_target_pairs={{0,8},{4,12},{8,0},{12,4},{1,9},{5,13},{9,1},{13,5},{2,10},{6,14},... | collective-permute-start | bytes 393224 | tf_op jit(solution)/shard_map/ppermute | solution.py:603
  117.6 9.0 %collective-permute-start.31 = (f32[8,1,32,128]{3,2,1,0:T(8,128)S(1)}, f32[8,1,32,128]{3,2,1,0:T(8,128)S(1)}, u32[]{:S(2)}, u32[]{:S(2)}) collective-permute-start(f32[8,1,32,128]{3,2,1,0:T(8,128)S(1)} %get-tuple-element.66), channel_id=1, source_target_pairs={{0,12},{4,0},{8,4},{12,8},{1,13},{5,1},{9,5},{13,9},{2,14},{6,2},{... | collective-permute-start | bytes 393224 | tf_op jit(solution)/shard_map/ppermute | solution.py:603

commit v5 on v4

--- a/solution.py
+++ b/solution.py
@@ -12,7 +12,7 @@
 CORNERS = ((1, 0), (0, 1), (1, 1))
 PANEL = 8
 AHEAD = 3
-SMALL = 1e-6
+SMALL = 1e-4
 MEDIUM = 4e-4
 NN = ((1,), (0,))
 NT = ((1,), (1,))
@@ -103,7 +103,9 @@
 def inverse_factor_near_one(error, row, col):
     first = lower(error, row, col)
     eye = jnp.where(row == col, 1.0, 0.0)
-    return eye - first + (lower(mul_t(first, first), row, col) + mul(first, first))
+    part = first.astype(jnp.bfloat16)
+    square = lax.dot_general(part, part, (NN, ((), ())), preferred_element_type=jnp.float32)
+    return eye - first + (lower(dot_t(part, part), row, col) + square)
 
 
 def dot_t(left, right):
@@ -247,12 +249,12 @@
     )(place, *own, start)
 
 
-def pieces_kernel(scale, count, place_ref, *refs):
+def pieces_kernel(scale, place_ref, *refs):
     diagonal_ref, head_ref, start_ref, refs = refs[0], refs[1], refs[2], refs[3:]
     cross_refs, refs = refs[:8], refs[8:]
-    kept_refs, got_refs, refs = refs[:count], refs[count : 2 * count], refs[2 * count :]
+    field_refs, refs = refs[:2], refs[2:]
     own_rows_ref, *slab_refs = refs[:-8]
-    basis_ref, gram_ref, mapped_ref, inverse_ref, fields_ref, value_ref, sems, field_sems = refs[-8:]
+    basis_ref, gram_ref, mapped_ref, inverse_ref, high_ref, low_ref, value_ref, sems = refs[-8:]
     x, y, core = place_ref[0], place_ref[1], place_ref[2]
     half = gram_ref.shape[0] // 2
     cross_copies, later_copies = [], []
@@ -269,17 +271,8 @@
         later_copies.append(
             pltpu.make_async_copy(diagonal_ref.at[p], gram_ref.at[square, square], sems.at[8 + p])
         )
-    for side, sources in enumerate((kept_refs, got_refs)):
-        first = 0
-        for index, ref in enumerate(sources):
-            later_copies.append(
-                pltpu.make_async_copy(
-                    ref.at[:, 0],
-                    fields_ref.at[side, first : first + ref.shape[0]],
-                    field_sems.at[side, index],
-                )
-            )
-            first += ref.shape[0]
+    for index, (source, target) in enumerate(zip(field_refs, (high_ref, low_ref))):
+        later_copies.append(pltpu.make_async_copy(source, target, sems.at[10 + index]))
     for copy in cross_copies + later_copies:
         copy.start()
     for copy in cross_copies:
@@ -293,36 +286,34 @@
             copy.wait()
 
     iterate(scale, first_map, start_ref, basis_ref, gram_ref, inverse_ref, mapped_ref)
-    project(place_ref, basis_ref, fields_ref, own_rows_ref, slab_refs, value_ref)
+    project(place_ref, basis_ref, high_ref, low_ref, own_rows_ref, slab_refs, value_ref)
 
 
 PIECES = [(dc, dx, dy) for dc in range(2) for dx, dy in ((0, 0), (1, 0), (0, 1), (1, 1))]
 
 
-def subspace_pieces(place, diagonal, head, start, cross, kept, got, scale, slabs, own_rows):
+def subspace_pieces(place, diagonal, head, start, cross, fields, scale, slabs, own_rows):
     rank, order = start.shape
-    half = order // 2
-    species = sum(piece.shape[0] for piece in got)
-    width = got[0].shape[3]
-    slab = jax.ShapeDtypeStruct((species, 1, rank // slabs, width), jnp.float32)
-    return pl.pallas_call(
-        functools.partial(pieces_kernel, scale, len(got)),
+    pairs, _, width = fields[0].shape
+    slab = jax.ShapeDtypeStruct((2 * pairs, 1, rank // slabs, width // 2), jnp.float32)
+    return pl.pallas_call(
+        functools.partial(pieces_kernel, scale),
         out_shape=[jax.ShapeDtypeStruct((own_rows, rank), jnp.float32)] + [slab] * slabs,
-        in_specs=[SMEM_SPEC, ANY_SPEC] + [VMEM_SPEC] * 2 + [ANY_SPEC] * (8 + 2 * len(got)),
+        in_specs=[SMEM_SPEC, ANY_SPEC] + [VMEM_SPEC] * 2 + [ANY_SPEC] * 10,
         out_specs=[VMEM_SPEC] * (1 + slabs),
         scratch_shapes=[
             pltpu.VMEM((rank, order), jnp.float32),
             pltpu.VMEM((order, order), jnp.float32),
             pltpu.VMEM((rank, order), jnp.float32),
             pltpu.VMEM((rank, rank), jnp.float32),
-            pltpu.VMEM((2, species, half, width), jnp.float32),
-            pltpu.VMEM((rank, 2 * width), jnp.float32),
-            pltpu.SemaphoreType.DMA((10,)),
-            pltpu.SemaphoreType.DMA((2, len(got))),
+            pltpu.VMEM((pairs, order, width), jnp.bfloat16),
+            pltpu.VMEM((pairs, order, width), jnp.bfloat16),
+            pltpu.VMEM((rank, width), jnp.float32),
+            pltpu.SemaphoreType.DMA((12,)),
         ],
         compiler_params=params(24),
         name="subspace",
-    )(place, diagonal, head, start, *cross, *kept, *got)
+    )(place, diagonal, head, start, *cross, *fields)
 
 
 def split(value):
@@ -343,23 +334,22 @@
     return parts[0][rows], parts[1][rows]
 
 
-def project(place_ref, basis_ref, fields_ref, own_rows_ref, slab_refs, value_ref):
-    x, z, index = place_ref[0], place_ref[3], place_ref[4]
-    species, half, width = fields_ref.shape[1:]
-    near = split(basis_ref[:, pl.ds(pl.multiple_of(x * half, 128), half)])
-    far = split(basis_ref[:, pl.ds(pl.multiple_of((1 - x) * half, 128), half)])
+def project(place_ref, basis_ref, high_ref, low_ref, own_rows_ref, slab_refs, value_ref):
+    z, index = place_ref[3], place_ref[4]
+    high, low = split(basis_ref[...])
     slabs = len(slab_refs)
-    rows = slab_refs[0].shape[2]
-    for first in range(0, species, 2):
-
-        def two(side):
-            return split(jnp.concatenate([fields_ref[side, first], fields_ref[side, first + 1]], axis=1))
-
-        value_ref[...] = dot3(near, two(0), NN) + dot3(far, two(1), NN)
+    rows, width = slab_refs[0].shape[2:]
+
+    def dot(left, right):
+        return lax.dot_general(left, right, (NN, ((), ())), preferred_element_type=jnp.float32)
+
+    for number in range(high_ref.shape[0]):
+        field_high, field_low = high_ref[number], low_ref[number]
+        value_ref[...] = dot(high, field_high) + (dot(high, field_low) + dot(low, field_high))
         for step in range(slabs):
             at = pl.multiple_of(lax.rem(z + step, slabs) * rows, 8)
             for j in range(2):
-                slab_refs[step][first + j, 0] = value_ref[
+                slab_refs[step][2 * number + j, 0] = value_ref[
                     pl.ds(at, rows), width * j : width * (j + 1)
                 ]
     count_rows = own_rows_ref.shape[0]
@@ -368,6 +358,31 @@
     shift = lax.rem(index, per_tile)
     value_ref[:, :width] = tile
     own_rows_ref[...] = value_ref[pl.ds(pl.multiple_of(shift * count_rows, 8), count_rows), :width]
+
+
+def halves_kernel(count, place_ref, *refs):
+    got_refs, kept_refs, (high_ref, low_ref) = refs[:count], refs[count : 2 * count], refs[2 * count :]
+    x = place_ref[0]
+    half = got_refs[0].shape[2]
+    for number, pair in enumerate(species_pairs(got_refs)):
+        for sources, owner in ((kept_refs, x), (got_refs, 1 - x)):
+            value = jnp.concatenate([sources[i][s, 0] for i, s in pair], axis=1)
+            rows = pl.ds(pl.multiple_of(owner * half, 128), half)
+            high_ref[number, rows, :], low_ref[number, rows, :] = split(value)
+
+
+def field_halves(place, got, kept):
+    species = sum(piece.shape[0] for piece in got)
+    half, width = got[0].shape[2:]
+    shape = jax.ShapeDtypeStruct((species // 2, 2 * half, 2 * width), jnp.bfloat16)
+    return pl.pallas_call(
+        functools.partial(halves_kernel, len(got)),
+        out_shape=[shape] * 2,
+        in_specs=[SMEM_SPEC] + [VMEM_SPEC] * (2 * len(got)),
+        out_specs=[VMEM_SPEC] * 2,
+        compiler_params=params(24),
+        name="field_halves",
+    )(place, *got, *kept)
 
 
 def own_kernel(place_ref, field_ref, keep_ref, send_ref, total_ref):
@@ -478,12 +493,18 @@
 
 
 def join_kernel(place_ref, *refs):
-    out_ref = refs[-1]
-    slabs = len(refs) - 1
-    width = refs[0].shape[3]
+    *slab_refs, out_ref, sems = refs
+    slabs = len(slab_refs)
+    width = slab_refs[0].shape[3]
+    copies = []
     for step in range(slabs):
         source = lax.rem(place_ref[3] + slabs - step, slabs)
-        out_ref[:, :, :, pl.ds(pl.multiple_of(source * width, 128), width)] = refs[step][...]
+        target = out_ref.at[:, :, :, pl.ds(pl.multiple_of(source * width, 128), width)]
+        copies.append(pltpu.make_async_copy(slab_refs[step], target, sems.at[step]))
+    for copy in copies:
+        copy.start()
+    for copy in copies:
+        copy.wait()
 
 
 def join_slabs(place, slabs):
@@ -492,7 +513,8 @@
         join_kernel,
         out_shape=jax.ShapeDtypeStruct(shape, jnp.float32),
         in_specs=[SMEM_SPEC] + [VMEM_SPEC] * len(slabs),
-        out_specs=VMEM_SPEC,
+        out_specs=ANY_SPEC,
+        scratch_shapes=[pltpu.SemaphoreType.DMA((len(slabs),))],
         compiler_params=params(24),
         name="join",
     )(place, *slabs)
@@ -530,7 +552,7 @@
 
 def sum_z(array, *others):
     size = lax.axis_size("gy")
-    shares = [lax.ppermute(array, "gy", turn(size, step)) for step in range(1, size)]
+    shares = [lax.ppermute(array, "gy", turn(size, step)) for step in range(size - 1, 0, -1)]
     return sum(after(shares, others), array)
 
 
@@ -581,10 +603,12 @@
     cross = sum(shares, cross)
     own_pieces = [own, send_corner(own, 1, 0), beside, send_corner(beside, 1, 0)]
     own_pieces = own_pieces + [send_core(piece) for piece in own_pieces]
-    cross = sum_z(cross, own_pieces[:4])
+    fields = field_halves(place, early_got + [final_got], kept)
+    cross = sum_z(cross, own_pieces[:4], fields)
     diagonal, head = diagonal_blocks(place, own_pieces, start_t)
-    near = [cross] + [send_corner(cross, dx, dy) for dx, dy in CORNERS]
-    cross_pieces = near + [send_core(after(piece, head)) for piece in near]
+    across = {(dx, dy): send_corner(cross, dx, dy) for dx, dy in CORNERS[::-1]}
+    near = [after(across[corner], head) for corner in CORNERS]
+    cross_pieces = [cross] + near + [send_core(piece) for piece in [cross] + near]
 
     slabs = lax.axis_size("gy")
     own_rows, *projected = subspace_pieces(
@@ -593,8 +617,7 @@
         head,
         start_t,
         cross_pieces,
-        kept,
-        early_got + [final_got],
+        fields,
         1.0 / columns,
         slabs,
         start.shape[0] // lax.axis_size(("gx", "gy", "sa")),

time: 129 us -> 128 us (level)
  waiting for transfers between devices: 38.7 us -> 36.9 us
    ppermute x6, waiting for transfers between devices: 6.09 us -> 4.18 us  [sum_z(): lax.ppermute(array, 'gy', turn(size, step))]
    pallas_call x1 -> x2, Pallas kernels: 23.6 us -> 24.1 us  [the longest x1 22.2 us: subspace_pieces(): pl.pallas_call(functools.partial(pieces_kernel, scale), out_shape=[jax.Sh...]
  transfers between devices with their start and end apart: 32 -> 32, of which waited for: 19 -> 19; matrix products, arithmetic and copies ran while one was open for 9% -> 9% of each run, Pallas kernels for 10% -> 12%
where the time goes in v5:
time: 128 us; the launch traced here: 127 us
  Pallas kernels  39.3 us (31%)
  waiting for transfers between devices  36.9 us (29%)
  starting transfers between devices  36.1 us (28%)
  local copies, waits for them, and re-layouts  10.4 us (8%)
  other arithmetic  2.99 us (2%)
    pallas_call x1, Pallas kernels, subspace_pieces(): pl.pallas_call(functools.partial(pieces_kernel, scale), out_shape=[jax.Sh...  22.2 us
    ppermute x10, starting transfers between devices, send_corner(): return lax.ppermute(array, ('gx', 'sa'), pairs)  13.8 us
    ppermute x6, starting transfers between devices, sum_z(): lax.ppermute(array, 'gy', turn(size, step))  11.6 us
    ppermute x10, waiting for transfers between devices, send_corner(): return lax.ppermute(array, ('gx', 'sa'), pairs)  10.4 us
    ppermute x3, waiting for transfers between devices, on_halves(): got = [lax.ppermute(piece, 'gx', flip(2, 1)) for piece in sent]  9.66 us
    ppermute x3, waiting for transfers between devices, on_halves(): lax.ppermute(projected[i], 'gy', turn(slabs, i))  8.62 us
    dynamic_slice x5, local copies, waits for them, and re-layouts, chunk(): lax.dynamic_slice_in_dim(source, owner * species + starts[i], sizes[i], 0)  8.58 us
    pallas_call x1, Pallas kernels, own_blocks(): pl.pallas_call(own_kernel, grid=(field.shape[0] // step,), out_shape=[sha...  6.54 us
  transfers between devices with their start and end apart: 32, of which 19 were waited for; matrix products, arithmetic and copies ran while one was open for 9% of the time, Pallas kernels for 12%

profile of v5, /device:TPU:0, one launch (start us, length us, event | category | flops | bytes accessed | tf_op | source)
XLA Modules:
  0.0 126.7 jit_solution(6201627900650312469)
XLA Ops:
  0.6 2.1 %constant_dynamic-slice_fusion.5 = f32[3,1,512,128]{3,2,1,0:T(8,128)} fusion(f32[16,1,512,128]{3,2,1,0:T(8,128)} %field_ref, s32[]{:T(128)S(6)} %select_n.38), kind=kLoop, calls=%fused_computation.10 | loop fusion | bytes 1572868 | tf_op jit(solution)/shard_map/dynamic_slice | solution.py:576
  2.7 2.9 %collective-permute-start.1 = (f32[3,1,512,128]{3,2,1,0:T(8,128)}, f32[3,1,512,128]{3,2,1,0:T(8,128)}, u32[]{:S(2)}, u32[]{:S(2)}) collective-permute-start(f32[3,1,512,128]{3,2,1,0:T(8,128)} %constant_dynamic-slice_fusion.5), channel_id=1, source_target_pairs={{0,16},{16,0},{1,17},{17,1},{2,18},{18,2},{3,19},{19,3},{4,20},{20... | collective-permute-start | bytes 2359304 | tf_op jit(solution)/shard_map/ppermute | solution.py:581
  5.6 1.9 %constant_dynamic-slice_fusion.3 = f32[2,1,512,128]{3,2,1,0:T(8,128)} fusion(f32[16,1,512,128]{3,2,1,0:T(8,128)} %field_ref, s32[]{:T(128)S(6)} %select_n.40), kind=kLoop, calls=%fused_computation.8 | loop fusion | bytes 1048580 | tf_op jit(solution)/shard_map/dynamic_slice | solution.py:576
  7.5 2.1 %constant_dynamic-slice_fusion.4 = f32[3,1,512,128]{3,2,1,0:T(8,128)} fusion(f32[16,1,512,128]{3,2,1,0:T(8,128)} %field_ref, s32[]{:T(128)S(6)} %select_n.39), kind=kLoop, calls=%fused_computation.9 | loop fusion | bytes 1572868 | tf_op jit(solution)/shard_map/dynamic_slice | solution.py:576
  9.6 0.6 stack.23.place_ref
  10.2 6.5 %own_blocks.1 = (f32[160,512]{1,0:T(8,128)}, f32[160,512]{1,0:T(8,128)}) custom-call(s32[5]{0:T(128)} %stack.23.place_ref, f32[16,1,512,128]{3,2,1,0:T(8,128)} %field_ref), custom_call_target="tpu_custom_call" | custom-call | flops 199999995904 | bytes 4194304 | tf_op jit(solution)/shard_map/own_blocks/pallas_call | solution.py:418
  16.7 0.0 collective-permute-start.6
  16.8 1.8 %collective-permute-done = f32[160,512]{1,0:T(8,128)S(1)} collective-permute-done((f32[160,512]{1,0:T(8,128)}, f32[160,512]{1,0:T(8,128)S(1)}, u32[]{:S(2)}, u32[]{:S(2)}) %collective-permute-start) | collective-permute-done | bytes 327712 | tf_op jit(solution)/shard_map/ppermute | solution.py:544
  18.6 1.0 add.98
  19.6 4.7 %collective-permute-done.1.refs_0_ = f32[3,1,512,128]{3,2,1,0:T(8,128)} collective-permute-done((f32[3,1,512,128]{3,2,1,0:T(8,128)}, f32[3,1,512,128]{3,2,1,0:T(8,128)}, u32[]{:S(2)}, u32[]{:S(2)}) %collective-permute-start.1) | collective-permute-done | bytes 786464 | tf_op jit(solution)/shard_map/ppermute | solution.py:581
  24.3 2.2 %collective-permute-start.2 = (f32[80,512]{1,0:T(8,128)S(1)}, f32[80,512]{1,0:T(8,128)S(1)}, u32[]{:S(2)}, u32[]{:S(2)}) collective-permute-start(f32[80,512]{1,0:T(8,128)S(1)} %dynamic-slice_bitcast_fusion), channel_id=1, source_target_pairs={{0,2},{1,3},{2,0},{3,1},{16,18},{17,19},{18,16},{19,17},{4,6},{5,7... | collective-permute-start | bytes 491528 | tf_op jit(solution)/shard_map/ppermute | solution.py:550
  26.5 1.5 %collective-permute-start.8 = (f32[2,1,512,128]{3,2,1,0:T(8,128)}, f32[2,1,512,128]{3,2,1,0:T(8,128)S(1)}, u32[]{:S(2)}, u32[]{:S(2)}) collective-permute-start(f32[2,1,512,128]{3,2,1,0:T(8,128)} %constant_dynamic-slice_fusion.3), channel_id=1, source_target_pairs={{0,16},{16,0},{1,17},{17,1},{2,18},{18,2},{3,19},{19,3},{4,20},{20... | collective-permute-start | bytes 1572872 | tf_op jit(solution)/shard_map/ppermute | solution.py:581
  28.0 1.8 %collective-permute-done.2 = f32[80,512]{1,0:T(8,128)S(1)} collective-permute-done((f32[80,512]{1,0:T(8,128)S(1)}, f32[80,512]{1,0:T(8,128)S(1)}, u32[]{:S(2)}, u32[]{:S(2)}) %collective-permute-start.2) | collective-permute-done | bytes 163872 | tf_op jit(solution)/shard_map/ppermute | solution.py:550
  29.8 0.7 bitcast_add_fusion
  30.5 2.1 %collective-permute-start.5 = (f32[80,512]{1,0:T(8,128)}, f32[80,512]{1,0:T(8,128)}, u32[]{:S(2)}, u32[]{:S(2)}) collective-permute-start(f32[80,512]{1,0:T(8,128)} %bitcast_add_fusion), channel_id=1, source_target_pairs={{0,4},{4,8},{8,12},{12,0},{1,5},{5,9},{9,13},{13,1},{2,6},{6,10},{... | collective-permute-start | bytes 491528 | tf_op jit(solution)/shard_map/ppermute | solution.py:555
  32.5 2.6 %collective-permute-start.4 = (f32[80,512]{1,0:T(8,128)}, f32[80,512]{1,0:T(8,128)}, u32[]{:S(2)}, u32[]{:S(2)}) collective-permute-start(f32[80,512]{1,0:T(8,128)} %bitcast_add_fusion), channel_id=1, source_target_pairs={{0,8},{4,12},{8,0},{12,4},{1,9},{5,13},{9,1},{13,5},{2,10},{6,14},... | collective-permute-start | bytes 491528 | tf_op jit(solution)/shard_map/ppermute | solution.py:555
  35.1 1.3 %collective-permute-start.3 = (f32[80,512]{1,0:T(8,128)}, f32[80,512]{1,0:T(8,128)}, u32[]{:S(2)}, u32[]{:S(2)}) collective-permute-start(f32[80,512]{1,0:T(8,128)} %bitcast_add_fusion), channel_id=1, source_target_pairs={{0,12},{4,0},{8,4},{12,8},{1,13},{5,1},{9,5},{13,9},{2,14},{6,2},{... | collective-permute-start | bytes 491528 | tf_op jit(solution)/shard_map/ppermute | solution.py:555
  36.5 1.5 %constant_dynamic-slice_fusion.1 = (f32[3,1,512,128]{3,2,1,0:T(8,128)S(1)}, f32[3,1,512,128]{3,2,1,0:T(8,128)S(1)}) fusion(f32[16,1,512,128]{3,2,1,0:T(8,128)} %field_ref, s32[]{:T(128)S(6)} %select_n.44, s32[]{:T(128)S(6)} %select_n.43), kind=kLoop, calls=%fused_computation.6 | loop fusion | bytes 3145736 | tf_op jit(solution)/shard_map/dynamic_slice | solution.py:576
  38.0 1.2 copy.4
  39.2 1.1 constant_dynamic-slice_fusion.refs_1_.refs_5_
  40.3 0.8 collective-permute-done.6.refs_1_
  41.1 2.8 %cross_block.3 = (f32[256,512]{1,0:T(8,128)S(1)}, f32[256,512]{1,0:T(8,128)S(1)}) custom-call(s32[5]{0:T(128)S(1)} %copy-done, f32[3,1,512,128]{3,2,1,0:T(8,128)} %collective-permute-done.1.refs_0_, f32[3,1,512,128]{3,2,1,0:T(8,128)S(1)} %collective-permute-done.6.refs_1_, f32[3,1,512,128]{3,2,1,0:T(8,128)S(1)} %get-tuple-element.71.refs_2_.refs_3_, ...), custom_call_target="tpu_custom_call" | custom-call | tf_op jit(solution)/shard_map/cross_block/pallas_call | solution.py:465
  43.9 0.1 collective-permute-done.4
  44.0 1.2 add_add_fusion.refs_0_
  45.2 2.1 %collective-permute-start.7 = (f32[80,512]{1,0:T(8,128)S(1)}, f32[80,512]{1,0:T(8,128)S(1)}, u32[]{:S(2)}, u32[]{:S(2)}) collective-permute-start(f32[80,512]{1,0:T(8,128)S(1)} %add_add_fusion.refs_0_), channel_id=1, source_target_pairs={{0,2},{1,3},{2,0},{3,1},{16,18},{17,19},{18,16},{19,17},{4,6},{5,7... | collective-permute-start | bytes 491528 | tf_op jit(solution)/shard_map/ppermute | solution.py:550
  47.3 4.2 %collective-permute-done.8.refs_0_.refs_2_ = f32[2,1,512,128]{3,2,1,0:T(8,128)S(1)} collective-permute-done((f32[2,1,512,128]{3,2,1,0:T(8,128)}, f32[2,1,512,128]{3,2,1,0:T(8,128)S(1)}, u32[]{:S(2)}, u32[]{:S(2)}) %collective-permute-start.8) | collective-permute-done | bytes 524320 | tf_op jit(solution)/shard_map/ppermute | solution.py:581
  51.5 1.0 cross_block.4
  52.5 0.1 collective-permute-start.9
  52.5 1.0 cross_block.5.left_ref
  53.5 0.9 collective-permute-done.9.right_ref
  54.4 0.6 quarters.1
  55.0 1.8 %collective-permute-start.10 = (f32[64,512]{1,0:T(8,128)S(1)}, f32[64,512]{1,0:T(8,128)S(1)}, u32[]{:S(2)}, u32[]{:S(2)}) collective-permute-start(f32[64,512]{1,0:T(8,128)S(1)} %get-tuple-element.49), channel_id=1, source_target_pairs={{0,16},{1,17},{2,18},{3,19},{16,0},{17,1},{18,2},{19,3},{4,20},{5,... | collective-permute-start | bytes 393224 | tf_op jit(solution)/shard_map/ppermute | solution.py:550
  56.9 1.5 %collective-permute-start.17 = (f32[64,512]{1,0:T(8,128)S(1)}, f32[64,512]{1,0:T(8,128)S(1)}, u32[]{:S(2)}, u32[]{:S(2)}) collective-permute-start(f32[64,512]{1,0:T(8,128)S(1)} %get-tuple-element.55), channel_id=1, source_target_pairs={{0,2},{1,3},{2,0},{3,1},{16,18},{17,19},{18,16},{19,17},{4,6},{5,7... | collective-permute-start | bytes 393224 | tf_op jit(solution)/shard_map/ppermute | solution.py:550
  58.4 0.2 collective-permute-start.18
  58.6 2.2 %collective-permute-done.10 = f32[64,512]{1,0:T(8,128)S(1)} collective-permute-done((f32[64,512]{1,0:T(8,128)S(1)}, f32[64,512]{1,0:T(8,128)S(1)}, u32[]{:S(2)}, u32[]{:S(2)}) %collective-permute-start.10) | collective-permute-done | bytes 131104 | tf_op jit(solution)/shard_map/ppermute | solution.py:550
  60.7 2.4 %collective-permute-start.11 = (f32[80,512]{1,0:T(8,128)S(1)}, f32[80,512]{1,0:T(8,128)S(1)}, u32[]{:S(2)}, u32[]{:S(2)}) collective-permute-start(f32[80,512]{1,0:T(8,128)S(1)} %add_add_fusion.refs_0_), channel_id=1, source_target_pairs={{0,16},{1,17},{2,18},{3,19},{16,0},{17,1},{18,2},{19,3},{4,20},{5,... | collective-permute-start | bytes 491528 | tf_op jit(solution)/shard_map/ppermute | solution.py:550
  63.2 0.9 collective-permute-done.17
  64.2 1.5 %collective-permute-done.18 = f32[64,512]{1,0:T(8,128)S(1)} collective-permute-done((f32[64,512]{1,0:T(8,128)S(1)}, f32[64,512]{1,0:T(8,128)S(1)}, u32[]{:S(2)}, u32[]{:S(2)}) %collective-permute-start.18) | collective-permute-done | bytes 131104 | tf_op jit(solution)/shard_map/ppermute | solution.py:550
  65.7 1.6 %collective-permute-start.21 = (f32[64,512]{1,0:T(8,128)S(1)}, f32[64,512]{1,0:T(8,128)S(1)}, u32[]{:S(2)}, u32[]{:S(2)}) collective-permute-start(f32[64,512]{1,0:T(8,128)S(1)} %add_add_fusion.2), channel_id=1, source_target_pairs={{0,4},{4,8},{8,12},{12,0},{1,5},{5,9},{9,13},{13,1},{2,6},{6,10},{... | collective-permute-start | bytes 393224 | tf_op jit(solution)/shard_map/ppermute | solution.py:555
  67.3 2.6 %collective-permute-start.20 = (f32[64,512]{1,0:T(8,128)S(1)}, f32[64,512]{1,0:T(8,128)S(1)}, u32[]{:S(2)}, u32[]{:S(2)}) collective-permute-start(f32[64,512]{1,0:T(8,128)S(1)} %add_add_fusion.2), channel_id=1, source_target_pairs={{0,8},{4,12},{8,0},{12,4},{1,9},{5,13},{9,1},{13,5},{2,10},{6,14},... | collective-permute-start | bytes 393224 | tf_op jit(solution)/shard_map/ppermute | solution.py:555
  69.9 1.3 %collective-permute-start.19 = (f32[64,512]{1,0:T(8,128)S(1)}, f32[64,512]{1,0:T(8,128)S(1)}, u32[]{:S(2)}, u32[]{:S(2)}) collective-permute-start(f32[64,512]{1,0:T(8,128)S(1)} %add_add_fusion.2), channel_id=1, source_target_pairs={{0,12},{4,0},{8,4},{12,8},{1,13},{5,1},{9,5},{13,9},{2,14},{6,2},{... | collective-permute-start | bytes 393224 | tf_op jit(solution)/shard_map/ppermute | solution.py:555
  71.3 1.9 %field_halves.1 = (bf16[4,1024,256]{2,1,0:T(8,128)(2,1)S(1)}, bf16[4,1024,256]{2,1,0:T(8,128)(2,1)S(1)}) custom-call(s32[5]{0:T(128)S(1)} %copy-done, f32[3,1,512,128]{3,2,1,0:T(8,128)} %collective-permute-done.1.refs_0_, f32[3,1,512,128]{3,2,1,0:T(8,128)S(1)} %collective-permute-done.6.refs_1_, ...), custom_call_target="tpu_custom_call" | custom-call | tf_op jit(solution)/shard_map/field_halves/pallas_call | solution.py:378
  73.2 0.9 collective-permute-done.21
  74.1 3.2 %collective-permute-done.20 = f32[64,512]{1,0:T(8,128)S(1)} collective-permute-done((f32[64,512]{1,0:T(8,128)S(1)}, f32[64,512]{1,0:T(8,128)S(1)}, u32[]{:S(2)}, u32[]{:S(2)}) %collective-permute-start.20) | collective-permute-done | bytes 131104 | tf_op jit(solution)/shard_map/ppermute | solution.py:555
  77.3 0.6 collective-permute-start.14
  77.9 0.1 collective-permute-start.16
  78.0 1.4 %collective-permute-start.24 = (f32[64,512]{1,0:T(8,128)S(1)}, f32[64,512]{1,0:T(8,128)S(1)}, u32[]{:S(2)}, u32[]{:S(2)}) collective-permute-start(f32[64,512]{1,0:T(8,128)S(1)} %add_add_fusion.1.refs_3_), channel_id=1, source_target_pairs={{0,18},{1,19},{2,16},{3,17},{16,2},{17,3},{18,0},{19,1},{4,22},{5,... | collective-permute-start | bytes 393224 | tf_op jit(solution)/shard_map/ppermute | solution.py:550
  79.4 1.5 %collective-permute-start.23 = (f32[64,512]{1,0:T(8,128)S(1)}, f32[64,512]{1,0:T(8,128)S(1)}, u32[]{:S(2)}, u32[]{:S(2)}) collective-permute-start(f32[64,512]{1,0:T(8,128)S(1)} %add_add_fusion.1.refs_3_), channel_id=1, source_target_pairs={{0,2},{1,3},{2,0},{3,1},{16,18},{17,19},{18,16},{19,17},{4,6},{5,7... | collective-permute-start | bytes 393224 | tf_op jit(solution)/shard_map/ppermute | solution.py:550
  80.9 0.7 collective-permute-start.22
  81.5 2.0 %diagonal.1 = (f32[2,512,512]{2,1,0:T(8,128)S(1)}, f32[128,1024]{1,0:T(8,128)S(1)}) custom-call(s32[5]{0:T(128)S(1)} %copy-done, f32[80,512]{1,0:T(8,128)S(1)} %add_add_fusion.refs_0_, f32[80,512]{1,0:T(8,128)S(1)} %collective-permute-done.11.refs_1_, f32[80,512]{1,0:T(8,128)S(1)} %collective-permute-done.7.refs_2_, ...), custom_call_target="tpu_custom_call" | custom-call | tf_op jit(solution)/shard_map/diagonal/pallas_call | solution.py:238
  83.6 1.7 %collective-permute-done.24.refs_6_ = f32[64,512]{1,0:T(8,128)S(1)} collective-permute-done((f32[64,512]{1,0:T(8,128)S(1)}, f32[64,512]{1,0:T(8,128)S(1)}, u32[]{:S(2)}, u32[]{:S(2)}) %collective-permute-start.24) | collective-permute-done | bytes 131104 | tf_op jit(solution)/shard_map/ppermute | solution.py:550
  85.3 2.3 %collective-permute-done.23.refs_5_ = f32[64,512]{1,0:T(8,128)S(1)} collective-permute-done((f32[64,512]{1,0:T(8,128)S(1)}, f32[64,512]{1,0:T(8,128)S(1)}, u32[]{:S(2)}, u32[]{:S(2)}) %collective-permute-start.23) | collective-permute-done | bytes 131104 | tf_op jit(solution)/shard_map/ppermute | solution.py:550
  87.6 0.0 collective-permute-start.26
  87.6 0.5 collective-permute-start.27
  88.1 0.8 collective-permute-done.26.refs_8_
  88.9 0.2 collective-permute-done.27.refs_9_
  89.1 0.3 collective-permute-done.28.refs_10_
  89.5 22.2 %subspace.1 = (f32[32,128]{1,0:T(8,128)}, f32[8,1,32,128]{3,2,1,0:T(8,128)S(1)}, f32[8,1,32,128]{3,2,1,0:T(8,128)S(1)}, f32[8,1,32,128]{3,2,1,0:T(8,128)S(1)}, f32[8,1,32,128]{3,2,1,0:T(8,128)S(1)}) custom-call(s32[5]{0:T(128)S(1)} %copy-done, f32[2,512,512]{2,1,0:T(8,128)S(1)} %get-tuple-element.52.refs_0_, f32[128,1024]{1,0:T(8,128)S(1)} %get-tuple-element.53.refs_1_, ...), custom_call_target="tpu_custom_call" | custom-call | tf_op jit(solution)/shard_map/subspace/pallas_call | solution.py:299
  111.6 2.5 %collective-permute-start.29 = (f32[8,1,32,128]{3,2,1,0:T(8,128)S(1)}, f32[8,1,32,128]{3,2,1,0:T(8,128)S(1)}, u32[]{:S(2)}, u32[]{:S(2)}) collective-permute-start(f32[8,1,32,128]{3,2,1,0:T(8,128)S(1)} %get-tuple-element.66), channel_id=1, source_target_pairs={{0,4},{4,8},{8,12},{12,0},{1,5},{5,9},{9,13},{13,1},{2,6},{6,10},{... | collective-permute-start | bytes 393224 | tf_op jit(solution)/shard_map/ppermute | solution.py:626
  114.1 2.1 %collective-permute-start.30 = (f32[8,1,32,128]{3,2,1,0:T(8,128)S(1)}, f32[8,1,32,128]{3,2,1,0:T(8,128)S(1)}, u32[]{:S(2)}, u32[]{:S(2)}) collective-permute-start(f32[8,1,32,128]{3,2,1,0:T(8,128)S(1)} %get-tuple-element.67), channel_id=1, source_target_pairs={{0,8},{4,12},{8,0},{12,4},{1,9},{5,13},{9,1},{13,5},{2,10},{6,14},... | collective-permute-start | bytes 393224 | tf_op jit(solution)/shard_map/ppermute | solution.py:626
  116.2 0.4 collective-permute-start.31
  116.6 3.4 %collective-permute-done.29.refs_1_ = f32[8,1,32,128]{3,2,1,0:T(8,128)S(1)} collective-permute-done((f32[8,1,32,128]{3,2,1,0:T(8,128)S(1)}, f32[8,1,32,128]{3,2,1,0:T(8,128)S(1)}, u32[]{:S(2)}, u32[]{:S(2)}) %collective-permute-start.29) | collective-permute-done | bytes 131104 | tf_op jit(solution)/shard_map/ppermute | solution.py:626
  120.0 5.2 %collective-permute-done.30.refs_2_ = f32[8,1,32,128]{3,2,1,0:T(8,128)S(1)} collective-permute-done((f32[8,1,32,128]{3,2,1,0:T(8,128)S(1)}, f32[8,1,32,128]{3,2,1,0:T(8,128)S(1)}, u32[]{:S(2)}, u32[]{:S(2)}) %collective-permute-start.30) | collective-permute-done | bytes 131104 | tf_op jit(solution)/shard_map/ppermute | solution.py:626
  125.2 1.4 %join.1 = f32[8,1,32,512]{3,2,1,0:T(8,128)} custom-call(s32[5]{0:T(128)S(1)} %copy-done, f32[8,1,32,128]{3,2,1,0:T(8,128)S(1)} %get-tuple-element.65.refs_0_, f32[8,1,32,128]{3,2,1,0:T(8,128)S(1)} %collective-permute-done.29.refs_1_, f32[8,1,32,128]{3,2,1,0:T(8,128)S(1)} %collective-permute-done.30.refs_2_, f32[8,1,32,128]{3,2,1,0:T(8,128)S(1)} %collective-permute-done.31.refs_3_), custom_call_target="tpu_custom_call" | custom-call | tf_op jit(solution)/shard_map/join/pallas_call | solution.py:512
  (24 shorter events, 0.2 us)
Async XLA Ops:
  2.7 21.6 %collective-permute-start.1 = (f32[3,1,512,128]{3,2,1,0:T(8,128)}, f32[3,1,512,128]{3,2,1,0:T(8,128)}, u32[]{:S(2)}, u32[]{:S(2)}) collective-permute-start(f32[3,1,512,128]{3,2,1,0:T(8,128)} %constant_dynamic-slice_fusion.5), channel_id=1, source_target_pairs={{0,16},{16,0},{1,17},{17,1},{2,18},{18,2},{3,19},{19,3},{4,20},{20... | collective-permute-start | bytes 2359304 | tf_op jit(solution)/shard_map/ppermute | solution.py:581
  16.7 24.3 %copy-start = (s32[5]{0:T(128)S(1)}, s32[5]{0:T(128)}, u32[]{:S(2)}) copy-start(s32[5]{0:T(128)} %stack.23.place_ref) | copy-start | bytes 64
  16.7 1.8 %collective-permute-start = (f32[160,512]{1,0:T(8,128)}, f32[160,512]{1,0:T(8,128)S(1)}, u32[]{:S(2)}, u32[]{:S(2)}) collective-permute-start(f32[160,512]{1,0:T(8,128)} %get-tuple-element.39), channel_id=1, source_target_pairs={{0,1},{1,0},{2,3},{3,2},{4,5},{5,4},{6,7},{7,6},{8,9},{9,8},{10,11... | collective-permute-start | bytes 983048 | tf_op jit(solution)/shard_map/ppermute | solution.py:544
  16.7 24.3 %collective-permute-start.6 = (f32[3,1,512,128]{3,2,1,0:T(8,128)}, f32[3,1,512,128]{3,2,1,0:T(8,128)S(1)}, u32[]{:S(2)}, u32[]{:S(2)}) collective-permute-start(f32[3,1,512,128]{3,2,1,0:T(8,128)} %constant_dynamic-slice_fusion.4), channel_id=1, source_target_pairs={{0,16},{16,0},{1,17},{17,1},{2,18},{18,2},{3,19},{19,3},{4,20},{20... | collective-permute-start | bytes 2359304 | tf_op jit(solution)/shard_map/ppermute | solution.py:581
  24.3 5.5 %collective-permute-start.2 = (f32[80,512]{1,0:T(8,128)S(1)}, f32[80,512]{1,0:T(8,128)S(1)}, u32[]{:S(2)}, u32[]{:S(2)}) collective-permute-start(f32[80,512]{1,0:T(8,128)S(1)} %dynamic-slice_bitcast_fusion), channel_id=1, source_target_pairs={{0,2},{1,3},{2,0},{3,1},{16,18},{17,19},{18,16},{19,17},{4,6},{5,7... | collective-permute-start | bytes 491528 | tf_op jit(solution)/shard_map/ppermute | solution.py:550
  26.5 25.0 %collective-permute-start.8 = (f32[2,1,512,128]{3,2,1,0:T(8,128)}, f32[2,1,512,128]{3,2,1,0:T(8,128)S(1)}, u32[]{:S(2)}, u32[]{:S(2)}) collective-permute-start(f32[2,1,512,128]{3,2,1,0:T(8,128)} %constant_dynamic-slice_fusion.3), channel_id=1, source_target_pairs={{0,16},{16,0},{1,17},{17,1},{2,18},{18,2},{3,19},{19,3},{4,20},{20... | collective-permute-start | bytes 1572872 | tf_op jit(solution)/shard_map/ppermute | solution.py:581
  30.5 13.4 %collective-permute-start.5 = (f32[80,512]{1,0:T(8,128)}, f32[80,512]{1,0:T(8,128)}, u32[]{:S(2)}, u32[]{:S(2)}) collective-permute-start(f32[80,512]{1,0:T(8,128)} %bitcast_add_fusion), channel_id=1, source_target_pairs={{0,4},{4,8},{8,12},{12,0},{1,5},{5,9},{9,13},{13,1},{2,6},{6,10},{... | collective-permute-start | bytes 491528 | tf_op jit(solution)/shard_map/ppermute | solution.py:555
  32.5 11.4 %collective-permute-start.4 = (f32[80,512]{1,0:T(8,128)}, f32[80,512]{1,0:T(8,128)}, u32[]{:S(2)}, u32[]{:S(2)}) collective-permute-start(f32[80,512]{1,0:T(8,128)} %bitcast_add_fusion), channel_id=1, source_target_pairs={{0,8},{4,12},{8,0},{12,4},{1,9},{5,13},{9,1},{13,5},{2,10},{6,14},... | collective-permute-start | bytes 491528 | tf_op jit(solution)/shard_map/ppermute | solution.py:555
  35.1 8.9 %collective-permute-start.3 = (f32[80,512]{1,0:T(8,128)}, f32[80,512]{1,0:T(8,128)}, u32[]{:S(2)}, u32[]{:S(2)}) collective-permute-start(f32[80,512]{1,0:T(8,128)} %bitcast_add_fusion), channel_id=1, source_target_pairs={{0,12},{4,0},{8,4},{12,8},{1,13},{5,1},{9,5},{13,9},{2,14},{6,2},{... | collective-permute-start | bytes 491528 | tf_op jit(solution)/shard_map/ppermute | solution.py:555
  45.2 7.2 %collective-permute-start.7 = (f32[80,512]{1,0:T(8,128)S(1)}, f32[80,512]{1,0:T(8,128)S(1)}, u32[]{:S(2)}, u32[]{:S(2)}) collective-permute-start(f32[80,512]{1,0:T(8,128)S(1)} %add_add_fusion.refs_0_), channel_id=1, source_target_pairs={{0,2},{1,3},{2,0},{3,1},{16,18},{17,19},{18,16},{19,17},{4,6},{5,7... | collective-permute-start | bytes 491528 | tf_op jit(solution)/shard_map/ppermute | solution.py:550
  52.5 2.0 %collective-permute-start.9 = (f32[256,512]{1,0:T(8,128)S(1)}, f32[256,512]{1,0:T(8,128)S(1)}, u32[]{:S(2)}, u32[]{:S(2)}) collective-permute-start(f32[256,512]{1,0:T(8,128)S(1)} %cross_block.4), channel_id=1, source_target_pairs={{0,1},{1,0},{2,3},{3,2},{4,5},{5,4},{6,7},{7,6},{8,9},{9,8},{10,11... | collective-permute-start | bytes 1572872 | tf_op jit(solution)/shard_map/ppermute | solution.py:544
  55.0 5.7 %collective-permute-start.10 = (f32[64,512]{1,0:T(8,128)S(1)}, f32[64,512]{1,0:T(8,128)S(1)}, u32[]{:S(2)}, u32[]{:S(2)}) collective-permute-start(f32[64,512]{1,0:T(8,128)S(1)} %get-tuple-element.49), channel_id=1, source_target_pairs={{0,16},{1,17},{2,18},{3,19},{16,0},{17,1},{18,2},{19,3},{4,20},{5,... | collective-permute-start | bytes 393224 | tf_op jit(solution)/shard_map/ppermute | solution.py:550
  56.9 7.3 %collective-permute-start.17 = (f32[64,512]{1,0:T(8,128)S(1)}, f32[64,512]{1,0:T(8,128)S(1)}, u32[]{:S(2)}, u32[]{:S(2)}) collective-permute-start(f32[64,512]{1,0:T(8,128)S(1)} %get-tuple-element.55), channel_id=1, source_target_pairs={{0,2},{1,3},{2,0},{3,1},{16,18},{17,19},{18,16},{19,17},{4,6},{5,7... | collective-permute-start | bytes 393224 | tf_op jit(solution)/shard_map/ppermute | solution.py:550
  58.4 7.3 %collective-permute-start.18 = (f32[64,512]{1,0:T(8,128)S(1)}, f32[64,512]{1,0:T(8,128)S(1)}, u32[]{:S(2)}, u32[]{:S(2)}) collective-permute-start(f32[64,512]{1,0:T(8,128)S(1)} %get-tuple-element.56), channel_id=1, source_target_pairs={{0,18},{1,19},{2,16},{3,17},{16,2},{17,3},{18,0},{19,1},{4,22},{5,... | collective-permute-start | bytes 393224 | tf_op jit(solution)/shard_map/ppermute | solution.py:550
  60.7 16.5 %collective-permute-start.11 = (f32[80,512]{1,0:T(8,128)S(1)}, f32[80,512]{1,0:T(8,128)S(1)}, u32[]{:S(2)}, u32[]{:S(2)}) collective-permute-start(f32[80,512]{1,0:T(8,128)S(1)} %add_add_fusion.refs_0_), channel_id=1, source_target_pairs={{0,16},{1,17},{2,18},{3,19},{16,0},{17,1},{18,2},{19,3},{4,20},{5,... | collective-permute-start | bytes 491528 | tf_op jit(solution)/shard_map/ppermute | solution.py:550
  63.2 14.1 %collective-permute-start.12 = (f32[80,512]{1,0:T(8,128)S(1)}, f32[80,512]{1,0:T(8,128)S(1)}, u32[]{:S(2)}, u32[]{:S(2)}) collective-permute-start(f32[80,512]{1,0:T(8,128)S(1)} %collective-permute-done.7.refs_2_), channel_id=1, source_target_pairs={{0,16},{1,17},{2,18},{3,19},{16,0},{17,1},{18,2},{19,3},{4,20},{5,... | collective-permute-start | bytes 491528 | tf_op jit(solution)/shard_map/ppermute | solution.py:550
  65.7 8.3 %collective-permute-start.21 = (f32[64,512]{1,0:T(8,128)S(1)}, f32[64,512]{1,0:T(8,128)S(1)}, u32[]{:S(2)}, u32[]{:S(2)}) collective-permute-start(f32[64,512]{1,0:T(8,128)S(1)} %add_add_fusion.2), channel_id=1, source_target_pairs={{0,4},{4,8},{8,12},{12,0},{1,5},{5,9},{9,13},{13,1},{2,6},{6,10},{... | collective-permute-start | bytes 393224 | tf_op jit(solution)/shard_map/ppermute | solution.py:555
  67.3 9.9 %collective-permute-start.20 = (f32[64,512]{1,0:T(8,128)S(1)}, f32[64,512]{1,0:T(8,128)S(1)}, u32[]{:S(2)}, u32[]{:S(2)}) collective-permute-start(f32[64,512]{1,0:T(8,128)S(1)} %add_add_fusion.2), channel_id=1, source_target_pairs={{0,8},{4,12},{8,0},{12,4},{1,9},{5,13},{9,1},{13,5},{2,10},{6,14},... | collective-permute-start | bytes 393224 | tf_op jit(solution)/shard_map/ppermute | solution.py:555
  69.9 7.3 %collective-permute-start.19 = (f32[64,512]{1,0:T(8,128)S(1)}, f32[64,512]{1,0:T(8,128)S(1)}, u32[]{:S(2)}, u32[]{:S(2)}) collective-permute-start(f32[64,512]{1,0:T(8,128)S(1)} %add_add_fusion.2), channel_id=1, source_target_pairs={{0,12},{4,0},{8,4},{12,8},{1,13},{5,1},{9,5},{13,9},{2,14},{6,2},{... | collective-permute-start | bytes 393224 | tf_op jit(solution)/shard_map/ppermute | solution.py:555
  74.1 5.3 %collective-permute-start.13 = (f32[80,512]{1,0:T(8,128)S(1)}, f32[80,512]{1,0:T(8,128)S(1)}, u32[]{:S(2)}, u32[]{:S(2)}) collective-permute-start(f32[80,512]{1,0:T(8,128)S(1)} %add_add_fusion.refs_0_), channel_id=1, source_target_pairs={{0,1},{1,0},{2,3},{3,2},{4,5},{5,4},{6,7},{7,6},{8,9},{9,8},{10,11... | collective-permute-start | bytes 491528 | tf_op jit(solution)/shard_map/ppermute | solution.py:544
  77.3 3.6 %collective-permute-start.15 = (f32[80,512]{1,0:T(8,128)S(1)}, f32[80,512]{1,0:T(8,128)S(1)}, u32[]{:S(2)}, u32[]{:S(2)}) collective-permute-start(f32[80,512]{1,0:T(8,128)S(1)} %collective-permute-done.7.refs_2_), channel_id=1, source_target_pairs={{0,1},{1,0},{2,3},{3,2},{4,5},{5,4},{6,7},{7,6},{8,9},{9,8},{10,11... | collective-permute-start | bytes 491528 | tf_op jit(solution)/shard_map/ppermute | solution.py:544
  77.3 4.2 %collective-permute-start.14 = (f32[80,512]{1,0:T(8,128)S(1)}, f32[80,512]{1,0:T(8,128)S(1)}, u32[]{:S(2)}, u32[]{:S(2)}) collective-permute-start(f32[80,512]{1,0:T(8,128)S(1)} %collective-permute-done.11.refs_1_), channel_id=1, source_target_pairs={{0,1},{1,0},{2,3},{3,2},{4,5},{5,4},{6,7},{7,6},{8,9},{9,8},{10,11... | collective-permute-start | bytes 491528 | tf_op jit(solution)/shard_map/ppermute | solution.py:544
  77.9 3.7 %collective-permute-start.16 = (f32[80,512]{1,0:T(8,128)S(1)}, f32[80,512]{1,0:T(8,128)S(1)}, u32[]{:S(2)}, u32[]{:S(2)}) collective-permute-start(f32[80,512]{1,0:T(8,128)S(1)} %collective-permute-done.12.refs_3_), channel_id=1, source_target_pairs={{0,1},{1,0},{2,3},{3,2},{4,5},{5,4},{6,7},{7,6},{8,9},{9,8},{10,11... | collective-permute-start | bytes 491528 | tf_op jit(solution)/shard_map/ppermute | solution.py:544
  78.0 7.3 %collective-permute-start.24 = (f32[64,512]{1,0:T(8,128)S(1)}, f32[64,512]{1,0:T(8,128)S(1)}, u32[]{:S(2)}, u32[]{:S(2)}) collective-permute-start(f32[64,512]{1,0:T(8,128)S(1)} %add_add_fusion.1.refs_3_), channel_id=1, source_target_pairs={{0,18},{1,19},{2,16},{3,17},{16,2},{17,3},{18,0},{19,1},{4,22},{5,... | collective-permute-start | bytes 393224 | tf_op jit(solution)/shard_map/ppermute | solution.py:550
  79.4 8.2 %collective-permute-start.23 = (f32[64,512]{1,0:T(8,128)S(1)}, f32[64,512]{1,0:T(8,128)S(1)}, u32[]{:S(2)}, u32[]{:S(2)}) collective-permute-start(f32[64,512]{1,0:T(8,128)S(1)} %add_add_fusion.1.refs_3_), channel_id=1, source_target_pairs={{0,2},{1,3},{2,0},{3,1},{16,18},{17,19},{18,16},{19,17},{4,6},{5,7... | collective-permute-start | bytes 393224 | tf_op jit(solution)/shard_map/ppermute | solution.py:550
  80.9 6.7 %collective-permute-start.22 = (f32[64,512]{1,0:T(8,128)S(1)}, f32[64,512]{1,0:T(8,128)S(1)}, u32[]{:S(2)}, u32[]{:S(2)}) collective-permute-start(f32[64,512]{1,0:T(8,128)S(1)} %add_add_fusion.1.refs_3_), channel_id=1, source_target_pairs={{0,16},{1,17},{2,18},{3,19},{16,0},{17,1},{18,2},{19,3},{4,20},{5,... | collective-permute-start | bytes 393224 | tf_op jit(solution)/shard_map/ppermute | solution.py:550
  81.5 6.6 %collective-permute-start.25 = (f32[64,512]{1,0:T(8,128)S(1)}, f32[64,512]{1,0:T(8,128)S(1)}, u32[]{:S(2)}, u32[]{:S(2)}) collective-permute-start(f32[64,512]{1,0:T(8,128)S(1)} %add_add_fusion.1.refs_3_), channel_id=1, source_target_pairs={{0,1},{1,0},{2,3},{3,2},{4,5},{5,4},{6,7},{7,6},{8,9},{9,8},{10,11... | collective-permute-start | bytes 393224 | tf_op jit(solution)/shard_map/ppermute | solution.py:544
  87.6 1.3 %collective-permute-start.26 = (f32[64,512]{1,0:T(8,128)S(1)}, f32[64,512]{1,0:T(8,128)S(1)}, u32[]{:S(2)}, u32[]{:S(2)}) collective-permute-start(f32[64,512]{1,0:T(8,128)S(1)} %collective-permute-done.22.refs_4_), channel_id=1, source_target_pairs={{0,1},{1,0},{2,3},{3,2},{4,5},{5,4},{6,7},{7,6},{8,9},{9,8},{10,11... | collective-permute-start | bytes 393224 | tf_op jit(solution)/shard_map/ppermute | solution.py:544
  87.6 1.5 %collective-permute-start.27 = (f32[64,512]{1,0:T(8,128)S(1)}, f32[64,512]{1,0:T(8,128)S(1)}, u32[]{:S(2)}, u32[]{:S(2)}) collective-permute-start(f32[64,512]{1,0:T(8,128)S(1)} %collective-permute-done.23.refs_5_), channel_id=1, source_target_pairs={{0,1},{1,0},{2,3},{3,2},{4,5},{5,4},{6,7},{7,6},{8,9},{9,8},{10,11... | collective-permute-start | bytes 393224 | tf_op jit(solution)/shard_map/ppermute | solution.py:544
  88.1 1.3 %collective-permute-start.28 = (f32[64,512]{1,0:T(8,128)S(1)}, f32[64,512]{1,0:T(8,128)S(1)}, u32[]{:S(2)}, u32[]{:S(2)}) collective-permute-start(f32[64,512]{1,0:T(8,128)S(1)} %collective-permute-done.24.refs_6_), channel_id=1, source_target_pairs={{0,1},{1,0},{2,3},{3,2},{4,5},{5,4},{6,7},{7,6},{8,9},{9,8},{10,11... | collective-permute-start | bytes 393224 | tf_op jit(solution)/shard_map/ppermute | solution.py:544
  111.6 8.4 %collective-permute-start.29 = (f32[8,1,32,128]{3,2,1,0:T(8,128)S(1)}, f32[8,1,32,128]{3,2,1,0:T(8,128)S(1)}, u32[]{:S(2)}, u32[]{:S(2)}) collective-permute-start(f32[8,1,32,128]{3,2,1,0:T(8,128)S(1)} %get-tuple-element.66), channel_id=1, source_target_pairs={{0,4},{4,8},{8,12},{12,0},{1,5},{5,9},{9,13},{13,1},{2,6},{6,10},{... | collective-permute-start | bytes 393224 | tf_op jit(solution)/shard_map/ppermute | solution.py:626
  114.1 11.1 %collective-permute-start.30 = (f32[8,1,32,128]{3,2,1,0:T(8,128)S(1)}, f32[8,1,32,128]{3,2,1,0:T(8,128)S(1)}, u32[]{:S(2)}, u32[]{:S(2)}) collective-permute-start(f32[8,1,32,128]{3,2,1,0:T(8,128)S(1)} %get-tuple-element.67), channel_id=1, source_target_pairs={{0,8},{4,12},{8,0},{12,4},{1,9},{5,13},{9,1},{13,5},{2,10},{6,14},... | collective-permute-start | bytes 393224 | tf_op jit(solution)/shard_map/ppermute | solution.py:626
  116.2 9.0 %collective-permute-start.31 = (f32[8,1,32,128]{3,2,1,0:T(8,128)S(1)}, f32[8,1,32,128]{3,2,1,0:T(8,128)S(1)}, u32[]{:S(2)}, u32[]{:S(2)}) collective-permute-start(f32[8,1,32,128]{3,2,1,0:T(8,128)S(1)} %get-tuple-element.68), channel_id=1, source_target_pairs={{0,12},{4,0},{8,4},{12,8},{1,13},{5,1},{9,5},{13,9},{2,14},{6,2},{... | collective-permute-start | bytes 393224 | tf_op jit(solution)/shard_map/ppermute | solution.py:626

commit v6 on v5

--- a/solution.py
+++ b/solution.py
@@ -140,26 +140,16 @@
     row = lax.broadcasted_iota(jnp.int32, (rank, rank), 0)
     col = lax.broadcasted_iota(jnp.int32, (rank, rank), 1)
     eye = jnp.where(row == col, 1.0, 0.0)
-    basis_ref[...] = start_ref[...]
-
-    def iteration(index, carry):
-        @pl.when(index == 0)
-        def _():
-            first_map()
-
-        @pl.when(index > 0)
-        def _():
-            mapped_ref[...] = mul(basis_ref[...], gram_ref[...])
-
+    first_map()
+
+    def iteration(last):
         mapped = mapped_ref[...] * scale
         once = apply(inverse_factor(inner_products(mapped)), mapped)
+        source = once if last else mul(once, gram_ref[...])
         inner = inner_products(once)
         error = inner - eye
         size = jnp.sum(error * error)
-
-        @pl.when(size <= MEDIUM)
-        def _():
-            inverse_ref[...] = inverse_factor_near_one(error, row, col)
+        inverse_ref[...] = inverse_factor_near_one(error, row, col)
 
         @pl.when(jnp.logical_and(size > SMALL, size <= MEDIUM))
         def _():
@@ -171,10 +161,15 @@
         def _():
             inverse_ref[...] = inverse_factor(inner)
 
-        basis_ref[...] = apply(inverse_ref[...], once)
+        target_ref = basis_ref if last else mapped_ref
+        target_ref[...] = apply(inverse_ref[...], source)
+
+    def step(_, carry):
+        iteration(False)
         return carry
 
-    lax.fori_loop(0, ITERS, iteration, 0)
+    lax.fori_loop(0, ITERS - 1, step, 0)
+    iteration(True)
 
 
 VMEM_SPEC = pl.BlockSpec(memory_space=pltpu.VMEM)

time: 128 us -> 127 us (level)
  no operation moved by 1% of the time
where the time goes in v6:
time: 127 us; the launch traced here: 126 us
  Pallas kernels  38.4 us (30%)
  waiting for transfers between devices  36.9 us (29%)
  starting transfers between devices  36.1 us (28%)
  local copies, waits for them, and re-layouts  10.4 us (8%)
  other arithmetic  2.99 us (2%)
    pallas_call x1, Pallas kernels, subspace_pieces(): pl.pallas_call(functools.partial(pieces_kernel, scale), out_shape=[jax.Sh...  21.3 us
    ppermute x10, starting transfers between devices, send_corner(): return lax.ppermute(array, ('gx', 'sa'), pairs)  13.8 us
    ppermute x6, starting transfers between devices, sum_z(): lax.ppermute(array, 'gy', turn(size, step))  11.6 us
    ppermute x10, waiting for transfers between devices, send_corner(): return lax.ppermute(array, ('gx', 'sa'), pairs)  10.4 us
    ppermute x3, waiting for transfers between devices, on_halves(): got = [lax.ppermute(piece, 'gx', flip(2, 1)) for piece in sent]  9.66 us
    ppermute x3, waiting for transfers between devices, on_halves(): lax.ppermute(projected[i], 'gy', turn(slabs, i))  8.62 us
    dynamic_slice x5, local copies, waits for them, and re-layouts, chunk(): lax.dynamic_slice_in_dim(source, owner * species + starts[i], sizes[i], 0)  8.58 us
    pallas_call x1, Pallas kernels, own_blocks(): pl.pallas_call(own_kernel, grid=(field.shape[0] // step,), out_shape=[sha...  6.54 us
  transfers between devices with their start and end apart: 32, of which 19 were waited for; matrix products, arithmetic and copies ran while one was open for 9% of the time, Pallas kernels for 12%

profile of v6, /device:TPU:0, one launch (start us, length us, event | category | flops | bytes accessed | tf_op | source)
XLA Modules:
  0.0 125.8 jit_solution(13754297403341383091)
XLA Ops:
  0.6 2.1 %constant_dynamic-slice_fusion.5 = f32[3,1,512,128]{3,2,1,0:T(8,128)} fusion(f32[16,1,512,128]{3,2,1,0:T(8,128)} %field_ref, s32[]{:T(128)S(6)} %select_n.38), kind=kLoop, calls=%fused_computation.10 | loop fusion | bytes 1572868 | tf_op jit(solution)/shard_map/dynamic_slice | solution.py:571
  2.7 2.9 %collective-permute-start.1 = (f32[3,1,512,128]{3,2,1,0:T(8,128)}, f32[3,1,512,128]{3,2,1,0:T(8,128)}, u32[]{:S(2)}, u32[]{:S(2)}) collective-permute-start(f32[3,1,512,128]{3,2,1,0:T(8,128)} %constant_dynamic-slice_fusion.5), channel_id=1, source_target_pairs={{0,16},{16,0},{1,17},{17,1},{2,18},{18,2},{3,19},{19,3},{4,20},{20... | collective-permute-start | bytes 2359304 | tf_op jit(solution)/shard_map/ppermute | solution.py:576
  5.6 1.9 %constant_dynamic-slice_fusion.3 = f32[2,1,512,128]{3,2,1,0:T(8,128)} fusion(f32[16,1,512,128]{3,2,1,0:T(8,128)} %field_ref, s32[]{:T(128)S(6)} %select_n.40), kind=kLoop, calls=%fused_computation.8 | loop fusion | bytes 1048580 | tf_op jit(solution)/shard_map/dynamic_slice | solution.py:571
  7.5 2.1 %constant_dynamic-slice_fusion.4 = f32[3,1,512,128]{3,2,1,0:T(8,128)} fusion(f32[16,1,512,128]{3,2,1,0:T(8,128)} %field_ref, s32[]{:T(128)S(6)} %select_n.39), kind=kLoop, calls=%fused_computation.9 | loop fusion | bytes 1572868 | tf_op jit(solution)/shard_map/dynamic_slice | solution.py:571
  9.6 0.6 stack.23.place_ref
  10.2 6.5 %own_blocks.1 = (f32[160,512]{1,0:T(8,128)}, f32[160,512]{1,0:T(8,128)}) custom-call(s32[5]{0:T(128)} %stack.23.place_ref, f32[16,1,512,128]{3,2,1,0:T(8,128)} %field_ref), custom_call_target="tpu_custom_call" | custom-call | flops 199999995904 | bytes 4194304 | tf_op jit(solution)/shard_map/own_blocks/pallas_call | solution.py:413
  16.7 0.0 collective-permute-start.6
  16.8 1.8 %collective-permute-done = f32[160,512]{1,0:T(8,128)S(1)} collective-permute-done((f32[160,512]{1,0:T(8,128)}, f32[160,512]{1,0:T(8,128)S(1)}, u32[]{:S(2)}, u32[]{:S(2)}) %collective-permute-start) | collective-permute-done | bytes 327712 | tf_op jit(solution)/shard_map/ppermute | solution.py:539
  18.6 1.0 add.98
  19.6 4.7 %collective-permute-done.1.refs_0_ = f32[3,1,512,128]{3,2,1,0:T(8,128)} collective-permute-done((f32[3,1,512,128]{3,2,1,0:T(8,128)}, f32[3,1,512,128]{3,2,1,0:T(8,128)}, u32[]{:S(2)}, u32[]{:S(2)}) %collective-permute-start.1) | collective-permute-done | bytes 786464 | tf_op jit(solution)/shard_map/ppermute | solution.py:576
  24.3 2.2 %collective-permute-start.2 = (f32[80,512]{1,0:T(8,128)S(1)}, f32[80,512]{1,0:T(8,128)S(1)}, u32[]{:S(2)}, u32[]{:S(2)}) collective-permute-start(f32[80,512]{1,0:T(8,128)S(1)} %dynamic-slice_bitcast_fusion), channel_id=1, source_target_pairs={{0,2},{1,3},{2,0},{3,1},{16,18},{17,19},{18,16},{19,17},{4,6},{5,7... | collective-permute-start | bytes 491528 | tf_op jit(solution)/shard_map/ppermute | solution.py:545
  26.5 1.5 %collective-permute-start.8 = (f32[2,1,512,128]{3,2,1,0:T(8,128)}, f32[2,1,512,128]{3,2,1,0:T(8,128)S(1)}, u32[]{:S(2)}, u32[]{:S(2)}) collective-permute-start(f32[2,1,512,128]{3,2,1,0:T(8,128)} %constant_dynamic-slice_fusion.3), channel_id=1, source_target_pairs={{0,16},{16,0},{1,17},{17,1},{2,18},{18,2},{3,19},{19,3},{4,20},{20... | collective-permute-start | bytes 1572872 | tf_op jit(solution)/shard_map/ppermute | solution.py:576
  28.0 1.8 %collective-permute-done.2 = f32[80,512]{1,0:T(8,128)S(1)} collective-permute-done((f32[80,512]{1,0:T(8,128)S(1)}, f32[80,512]{1,0:T(8,128)S(1)}, u32[]{:S(2)}, u32[]{:S(2)}) %collective-permute-start.2) | collective-permute-done | bytes 163872 | tf_op jit(solution)/shard_map/ppermute | solution.py:545
  29.8 0.7 bitcast_add_fusion
  30.5 2.1 %collective-permute-start.5 = (f32[80,512]{1,0:T(8,128)}, f32[80,512]{1,0:T(8,128)}, u32[]{:S(2)}, u32[]{:S(2)}) collective-permute-start(f32[80,512]{1,0:T(8,128)} %bitcast_add_fusion), channel_id=1, source_target_pairs={{0,4},{4,8},{8,12},{12,0},{1,5},{5,9},{9,13},{13,1},{2,6},{6,10},{... | collective-permute-start | bytes 491528 | tf_op jit(solution)/shard_map/ppermute | solution.py:550
  32.5 2.6 %collective-permute-start.4 = (f32[80,512]{1,0:T(8,128)}, f32[80,512]{1,0:T(8,128)}, u32[]{:S(2)}, u32[]{:S(2)}) collective-permute-start(f32[80,512]{1,0:T(8,128)} %bitcast_add_fusion), channel_id=1, source_target_pairs={{0,8},{4,12},{8,0},{12,4},{1,9},{5,13},{9,1},{13,5},{2,10},{6,14},... | collective-permute-start | bytes 491528 | tf_op jit(solution)/shard_map/ppermute | solution.py:550
  35.1 1.3 %collective-permute-start.3 = (f32[80,512]{1,0:T(8,128)}, f32[80,512]{1,0:T(8,128)}, u32[]{:S(2)}, u32[]{:S(2)}) collective-permute-start(f32[80,512]{1,0:T(8,128)} %bitcast_add_fusion), channel_id=1, source_target_pairs={{0,12},{4,0},{8,4},{12,8},{1,13},{5,1},{9,5},{13,9},{2,14},{6,2},{... | collective-permute-start | bytes 491528 | tf_op jit(solution)/shard_map/ppermute | solution.py:550
  36.5 1.5 %constant_dynamic-slice_fusion.1 = (f32[3,1,512,128]{3,2,1,0:T(8,128)S(1)}, f32[3,1,512,128]{3,2,1,0:T(8,128)S(1)}) fusion(f32[16,1,512,128]{3,2,1,0:T(8,128)} %field_ref, s32[]{:T(128)S(6)} %select_n.44, s32[]{:T(128)S(6)} %select_n.43), kind=kLoop, calls=%fused_computation.6 | loop fusion | bytes 3145736 | tf_op jit(solution)/shard_map/dynamic_slice | solution.py:571
  38.0 1.2 copy.4
  39.2 1.1 constant_dynamic-slice_fusion.refs_1_.refs_5_
  40.3 0.8 collective-permute-done.6.refs_1_
  41.1 2.8 %cross_block.3 = (f32[256,512]{1,0:T(8,128)S(1)}, f32[256,512]{1,0:T(8,128)S(1)}) custom-call(s32[5]{0:T(128)S(1)} %copy-done, f32[3,1,512,128]{3,2,1,0:T(8,128)} %collective-permute-done.1.refs_0_, f32[3,1,512,128]{3,2,1,0:T(8,128)S(1)} %collective-permute-done.6.refs_1_, f32[3,1,512,128]{3,2,1,0:T(8,128)S(1)} %get-tuple-element.71.refs_2_.refs_3_, ...), custom_call_target="tpu_custom_call" | custom-call | tf_op jit(solution)/shard_map/cross_block/pallas_call | solution.py:460
  43.9 0.1 collective-permute-done.4
  44.0 1.2 add_add_fusion.refs_0_
  45.2 2.1 %collective-permute-start.7 = (f32[80,512]{1,0:T(8,128)S(1)}, f32[80,512]{1,0:T(8,128)S(1)}, u32[]{:S(2)}, u32[]{:S(2)}) collective-permute-start(f32[80,512]{1,0:T(8,128)S(1)} %add_add_fusion.refs_0_), channel_id=1, source_target_pairs={{0,2},{1,3},{2,0},{3,1},{16,18},{17,19},{18,16},{19,17},{4,6},{5,7... | collective-permute-start | bytes 491528 | tf_op jit(solution)/shard_map/ppermute | solution.py:545
  47.3 4.2 %collective-permute-done.8.refs_0_.refs_2_ = f32[2,1,512,128]{3,2,1,0:T(8,128)S(1)} collective-permute-done((f32[2,1,512,128]{3,2,1,0:T(8,128)}, f32[2,1,512,128]{3,2,1,0:T(8,128)S(1)}, u32[]{:S(2)}, u32[]{:S(2)}) %collective-permute-start.8) | collective-permute-done | bytes 524320 | tf_op jit(solution)/shard_map/ppermute | solution.py:576
  51.5 1.0 cross_block.4
  52.5 0.1 collective-permute-start.9
  52.5 1.0 cross_block.5.left_ref
  53.5 0.9 collective-permute-done.9.right_ref
  54.4 0.6 quarters.1
  55.0 1.8 %collective-permute-start.10 = (f32[64,512]{1,0:T(8,128)S(1)}, f32[64,512]{1,0:T(8,128)S(1)}, u32[]{:S(2)}, u32[]{:S(2)}) collective-permute-start(f32[64,512]{1,0:T(8,128)S(1)} %get-tuple-element.49), channel_id=1, source_target_pairs={{0,16},{1,17},{2,18},{3,19},{16,0},{17,1},{18,2},{19,3},{4,20},{5,... | collective-permute-start | bytes 393224 | tf_op jit(solution)/shard_map/ppermute | solution.py:545
  56.9 1.5 %collective-permute-start.17 = (f32[64,512]{1,0:T(8,128)S(1)}, f32[64,512]{1,0:T(8,128)S(1)}, u32[]{:S(2)}, u32[]{:S(2)}) collective-permute-start(f32[64,512]{1,0:T(8,128)S(1)} %get-tuple-element.55), channel_id=1, source_target_pairs={{0,2},{1,3},{2,0},{3,1},{16,18},{17,19},{18,16},{19,17},{4,6},{5,7... | collective-permute-start | bytes 393224 | tf_op jit(solution)/shard_map/ppermute | solution.py:545
  58.4 0.2 collective-permute-start.18
  58.6 2.2 %collective-permute-done.10 = f32[64,512]{1,0:T(8,128)S(1)} collective-permute-done((f32[64,512]{1,0:T(8,128)S(1)}, f32[64,512]{1,0:T(8,128)S(1)}, u32[]{:S(2)}, u32[]{:S(2)}) %collective-permute-start.10) | collective-permute-done | bytes 131104 | tf_op jit(solution)/shard_map/ppermute | solution.py:545
  60.7 2.4 %collective-permute-start.11 = (f32[80,512]{1,0:T(8,128)S(1)}, f32[80,512]{1,0:T(8,128)S(1)}, u32[]{:S(2)}, u32[]{:S(2)}) collective-permute-start(f32[80,512]{1,0:T(8,128)S(1)} %add_add_fusion.refs_0_), channel_id=1, source_target_pairs={{0,16},{1,17},{2,18},{3,19},{16,0},{17,1},{18,2},{19,3},{4,20},{5,... | collective-permute-start | bytes 491528 | tf_op jit(solution)/shard_map/ppermute | solution.py:545
  63.2 0.9 collective-permute-done.17
  64.2 1.5 %collective-permute-done.18 = f32[64,512]{1,0:T(8,128)S(1)} collective-permute-done((f32[64,512]{1,0:T(8,128)S(1)}, f32[64,512]{1,0:T(8,128)S(1)}, u32[]{:S(2)}, u32[]{:S(2)}) %collective-permute-start.18) | collective-permute-done | bytes 131104 | tf_op jit(solution)/shard_map/ppermute | solution.py:545
  65.7 1.6 %collective-permute-start.21 = (f32[64,512]{1,0:T(8,128)S(1)}, f32[64,512]{1,0:T(8,128)S(1)}, u32[]{:S(2)}, u32[]{:S(2)}) collective-permute-start(f32[64,512]{1,0:T(8,128)S(1)} %add_add_fusion.2), channel_id=1, source_target_pairs={{0,4},{4,8},{8,12},{12,0},{1,5},{5,9},{9,13},{13,1},{2,6},{6,10},{... | collective-permute-start | bytes 393224 | tf_op jit(solution)/shard_map/ppermute | solution.py:550
  67.3 2.6 %collective-permute-start.20 = (f32[64,512]{1,0:T(8,128)S(1)}, f32[64,512]{1,0:T(8,128)S(1)}, u32[]{:S(2)}, u32[]{:S(2)}) collective-permute-start(f32[64,512]{1,0:T(8,128)S(1)} %add_add_fusion.2), channel_id=1, source_target_pairs={{0,8},{4,12},{8,0},{12,4},{1,9},{5,13},{9,1},{13,5},{2,10},{6,14},... | collective-permute-start | bytes 393224 | tf_op jit(solution)/shard_map/ppermute | solution.py:550
  69.9 1.3 %collective-permute-start.19 = (f32[64,512]{1,0:T(8,128)S(1)}, f32[64,512]{1,0:T(8,128)S(1)}, u32[]{:S(2)}, u32[]{:S(2)}) collective-permute-start(f32[64,512]{1,0:T(8,128)S(1)} %add_add_fusion.2), channel_id=1, source_target_pairs={{0,12},{4,0},{8,4},{12,8},{1,13},{5,1},{9,5},{13,9},{2,14},{6,2},{... | collective-permute-start | bytes 393224 | tf_op jit(solution)/shard_map/ppermute | solution.py:550
  71.3 1.9 %field_halves.1 = (bf16[4,1024,256]{2,1,0:T(8,128)(2,1)S(1)}, bf16[4,1024,256]{2,1,0:T(8,128)(2,1)S(1)}) custom-call(s32[5]{0:T(128)S(1)} %copy-done, f32[3,1,512,128]{3,2,1,0:T(8,128)} %collective-permute-done.1.refs_0_, f32[3,1,512,128]{3,2,1,0:T(8,128)S(1)} %collective-permute-done.6.refs_1_, ...), custom_call_target="tpu_custom_call" | custom-call | tf_op jit(solution)/shard_map/field_halves/pallas_call | solution.py:373
  73.2 0.9 collective-permute-done.21
  74.1 3.2 %collective-permute-done.20 = f32[64,512]{1,0:T(8,128)S(1)} collective-permute-done((f32[64,512]{1,0:T(8,128)S(1)}, f32[64,512]{1,0:T(8,128)S(1)}, u32[]{:S(2)}, u32[]{:S(2)}) %collective-permute-start.20) | collective-permute-done | bytes 131104 | tf_op jit(solution)/shard_map/ppermute | solution.py:550
  77.3 0.6 collective-permute-start.14
  77.9 0.1 collective-permute-start.16
  78.0 1.4 %collective-permute-start.24 = (f32[64,512]{1,0:T(8,128)S(1)}, f32[64,512]{1,0:T(8,128)S(1)}, u32[]{:S(2)}, u32[]{:S(2)}) collective-permute-start(f32[64,512]{1,0:T(8,128)S(1)} %add_add_fusion.1.refs_3_), channel_id=1, source_target_pairs={{0,18},{1,19},{2,16},{3,17},{16,2},{17,3},{18,0},{19,1},{4,22},{5,... | collective-permute-start | bytes 393224 | tf_op jit(solution)/shard_map/ppermute | solution.py:545
  79.4 1.5 %collective-permute-start.23 = (f32[64,512]{1,0:T(8,128)S(1)}, f32[64,512]{1,0:T(8,128)S(1)}, u32[]{:S(2)}, u32[]{:S(2)}) collective-permute-start(f32[64,512]{1,0:T(8,128)S(1)} %add_add_fusion.1.refs_3_), channel_id=1, source_target_pairs={{0,2},{1,3},{2,0},{3,1},{16,18},{17,19},{18,16},{19,17},{4,6},{5,7... | collective-permute-start | bytes 393224 | tf_op jit(solution)/shard_map/ppermute | solution.py:545
  80.9 0.7 collective-permute-start.22
  81.5 2.0 %diagonal.1 = (f32[2,512,512]{2,1,0:T(8,128)S(1)}, f32[128,1024]{1,0:T(8,128)S(1)}) custom-call(s32[5]{0:T(128)S(1)} %copy-done, f32[80,512]{1,0:T(8,128)S(1)} %add_add_fusion.refs_0_, f32[80,512]{1,0:T(8,128)S(1)} %collective-permute-done.11.refs_1_, f32[80,512]{1,0:T(8,128)S(1)} %collective-permute-done.7.refs_2_, ...), custom_call_target="tpu_custom_call" | custom-call | tf_op jit(solution)/shard_map/diagonal/pallas_call | solution.py:233
  83.6 1.7 %collective-permute-done.24.refs_6_ = f32[64,512]{1,0:T(8,128)S(1)} collective-permute-done((f32[64,512]{1,0:T(8,128)S(1)}, f32[64,512]{1,0:T(8,128)S(1)}, u32[]{:S(2)}, u32[]{:S(2)}) %collective-permute-start.24) | collective-permute-done | bytes 131104 | tf_op jit(solution)/shard_map/ppermute | solution.py:545
  85.3 2.3 %collective-permute-done.23.refs_5_ = f32[64,512]{1,0:T(8,128)S(1)} collective-permute-done((f32[64,512]{1,0:T(8,128)S(1)}, f32[64,512]{1,0:T(8,128)S(1)}, u32[]{:S(2)}, u32[]{:S(2)}) %collective-permute-start.23) | collective-permute-done | bytes 131104 | tf_op jit(solution)/shard_map/ppermute | solution.py:545
  87.6 0.0 collective-permute-start.26
  87.6 0.5 collective-permute-start.27
  88.1 0.8 collective-permute-done.26.refs_8_
  88.9 0.2 collective-permute-done.27.refs_9_
  89.1 0.3 collective-permute-done.28.refs_10_
  89.5 21.3 %subspace.1 = (f32[32,128]{1,0:T(8,128)}, f32[8,1,32,128]{3,2,1,0:T(8,128)S(1)}, f32[8,1,32,128]{3,2,1,0:T(8,128)S(1)}, f32[8,1,32,128]{3,2,1,0:T(8,128)S(1)}, f32[8,1,32,128]{3,2,1,0:T(8,128)S(1)}) custom-call(s32[5]{0:T(128)S(1)} %copy-done, f32[2,512,512]{2,1,0:T(8,128)S(1)} %get-tuple-element.52.refs_0_, f32[128,1024]{1,0:T(8,128)S(1)} %get-tuple-element.53.refs_1_, ...), custom_call_target="tpu_custom_call" | custom-call | tf_op jit(solution)/shard_map/subspace/pallas_call | solution.py:294
  110.7 2.5 %collective-permute-start.29 = (f32[8,1,32,128]{3,2,1,0:T(8,128)S(1)}, f32[8,1,32,128]{3,2,1,0:T(8,128)S(1)}, u32[]{:S(2)}, u32[]{:S(2)}) collective-permute-start(f32[8,1,32,128]{3,2,1,0:T(8,128)S(1)} %get-tuple-element.66), channel_id=1, source_target_pairs={{0,4},{4,8},{8,12},{12,0},{1,5},{5,9},{9,13},{13,1},{2,6},{6,10},{... | collective-permute-start | bytes 393224 | tf_op jit(solution)/shard_map/ppermute | solution.py:621
  113.2 2.1 %collective-permute-start.30 = (f32[8,1,32,128]{3,2,1,0:T(8,128)S(1)}, f32[8,1,32,128]{3,2,1,0:T(8,128)S(1)}, u32[]{:S(2)}, u32[]{:S(2)}) collective-permute-start(f32[8,1,32,128]{3,2,1,0:T(8,128)S(1)} %get-tuple-element.67), channel_id=1, source_target_pairs={{0,8},{4,12},{8,0},{12,4},{1,9},{5,13},{9,1},{13,5},{2,10},{6,14},... | collective-permute-start | bytes 393224 | tf_op jit(solution)/shard_map/ppermute | solution.py:621
  115.3 0.4 collective-permute-start.31
  115.7 3.5 %collective-permute-done.29.refs_1_ = f32[8,1,32,128]{3,2,1,0:T(8,128)S(1)} collective-permute-done((f32[8,1,32,128]{3,2,1,0:T(8,128)S(1)}, f32[8,1,32,128]{3,2,1,0:T(8,128)S(1)}, u32[]{:S(2)}, u32[]{:S(2)}) %collective-permute-start.29) | collective-permute-done | bytes 131104 | tf_op jit(solution)/shard_map/ppermute | solution.py:621
  119.1 5.2 %collective-permute-done.30.refs_2_ = f32[8,1,32,128]{3,2,1,0:T(8,128)S(1)} collective-permute-done((f32[8,1,32,128]{3,2,1,0:T(8,128)S(1)}, f32[8,1,32,128]{3,2,1,0:T(8,128)S(1)}, u32[]{:S(2)}, u32[]{:S(2)}) %collective-permute-start.30) | collective-permute-done | bytes 131104 | tf_op jit(solution)/shard_map/ppermute | solution.py:621
  124.3 1.4 %join.1 = f32[8,1,32,512]{3,2,1,0:T(8,128)} custom-call(s32[5]{0:T(128)S(1)} %copy-done, f32[8,1,32,128]{3,2,1,0:T(8,128)S(1)} %get-tuple-element.65.refs_0_, f32[8,1,32,128]{3,2,1,0:T(8,128)S(1)} %collective-permute-done.29.refs_1_, f32[8,1,32,128]{3,2,1,0:T(8,128)S(1)} %collective-permute-done.30.refs_2_, f32[8,1,32,128]{3,2,1,0:T(8,128)S(1)} %collective-permute-done.31.refs_3_), custom_call_target="tpu_custom_call" | custom-call | tf_op jit(solution)/shard_map/join/pallas_call | solution.py:507
  (24 shorter events, 0.2 us)
Async XLA Ops:
  2.7 21.6 %collective-permute-start.1 = (f32[3,1,512,128]{3,2,1,0:T(8,128)}, f32[3,1,512,128]{3,2,1,0:T(8,128)}, u32[]{:S(2)}, u32[]{:S(2)}) collective-permute-start(f32[3,1,512,128]{3,2,1,0:T(8,128)} %constant_dynamic-slice_fusion.5), channel_id=1, source_target_pairs={{0,16},{16,0},{1,17},{17,1},{2,18},{18,2},{3,19},{19,3},{4,20},{20... | collective-permute-start | bytes 2359304 | tf_op jit(solution)/shard_map/ppermute | solution.py:576
  16.7 24.3 %copy-start = (s32[5]{0:T(128)S(1)}, s32[5]{0:T(128)}, u32[]{:S(2)}) copy-start(s32[5]{0:T(128)} %stack.23.place_ref) | copy-start | bytes 64
  16.7 1.8 %collective-permute-start = (f32[160,512]{1,0:T(8,128)}, f32[160,512]{1,0:T(8,128)S(1)}, u32[]{:S(2)}, u32[]{:S(2)}) collective-permute-start(f32[160,512]{1,0:T(8,128)} %get-tuple-element.39), channel_id=1, source_target_pairs={{0,1},{1,0},{2,3},{3,2},{4,5},{5,4},{6,7},{7,6},{8,9},{9,8},{10,11... | collective-permute-start | bytes 983048 | tf_op jit(solution)/shard_map/ppermute | solution.py:539
  16.7 24.3 %collective-permute-start.6 = (f32[3,1,512,128]{3,2,1,0:T(8,128)}, f32[3,1,512,128]{3,2,1,0:T(8,128)S(1)}, u32[]{:S(2)}, u32[]{:S(2)}) collective-permute-start(f32[3,1,512,128]{3,2,1,0:T(8,128)} %constant_dynamic-slice_fusion.4), channel_id=1, source_target_pairs={{0,16},{16,0},{1,17},{17,1},{2,18},{18,2},{3,19},{19,3},{4,20},{20... | collective-permute-start | bytes 2359304 | tf_op jit(solution)/shard_map/ppermute | solution.py:576
  24.3 5.5 %collective-permute-start.2 = (f32[80,512]{1,0:T(8,128)S(1)}, f32[80,512]{1,0:T(8,128)S(1)}, u32[]{:S(2)}, u32[]{:S(2)}) collective-permute-start(f32[80,512]{1,0:T(8,128)S(1)} %dynamic-slice_bitcast_fusion), channel_id=1, source_target_pairs={{0,2},{1,3},{2,0},{3,1},{16,18},{17,19},{18,16},{19,17},{4,6},{5,7... | collective-permute-start | bytes 491528 | tf_op jit(solution)/shard_map/ppermute | solution.py:545
  26.5 25.0 %collective-permute-start.8 = (f32[2,1,512,128]{3,2,1,0:T(8,128)}, f32[2,1,512,128]{3,2,1,0:T(8,128)S(1)}, u32[]{:S(2)}, u32[]{:S(2)}) collective-permute-start(f32[2,1,512,128]{3,2,1,0:T(8,128)} %constant_dynamic-slice_fusion.3), channel_id=1, source_target_pairs={{0,16},{16,0},{1,17},{17,1},{2,18},{18,2},{3,19},{19,3},{4,20},{20... | collective-permute-start | bytes 1572872 | tf_op jit(solution)/shard_map/ppermute | solution.py:576
  30.5 13.4 %collective-permute-start.5 = (f32[80,512]{1,0:T(8,128)}, f32[80,512]{1,0:T(8,128)}, u32[]{:S(2)}, u32[]{:S(2)}) collective-permute-start(f32[80,512]{1,0:T(8,128)} %bitcast_add_fusion), channel_id=1, source_target_pairs={{0,4},{4,8},{8,12},{12,0},{1,5},{5,9},{9,13},{13,1},{2,6},{6,10},{... | collective-permute-start | bytes 491528 | tf_op jit(solution)/shard_map/ppermute | solution.py:550
  32.5 11.4 %collective-permute-start.4 = (f32[80,512]{1,0:T(8,128)}, f32[80,512]{1,0:T(8,128)}, u32[]{:S(2)}, u32[]{:S(2)}) collective-permute-start(f32[80,512]{1,0:T(8,128)} %bitcast_add_fusion), channel_id=1, source_target_pairs={{0,8},{4,12},{8,0},{12,4},{1,9},{5,13},{9,1},{13,5},{2,10},{6,14},... | collective-permute-start | bytes 491528 | tf_op jit(solution)/shard_map/ppermute | solution.py:550
  35.1 8.9 %collective-permute-start.3 = (f32[80,512]{1,0:T(8,128)}, f32[80,512]{1,0:T(8,128)}, u32[]{:S(2)}, u32[]{:S(2)}) collective-permute-start(f32[80,512]{1,0:T(8,128)} %bitcast_add_fusion), channel_id=1, source_target_pairs={{0,12},{4,0},{8,4},{12,8},{1,13},{5,1},{9,5},{13,9},{2,14},{6,2},{... | collective-permute-start | bytes 491528 | tf_op jit(solution)/shard_map/ppermute | solution.py:550
  45.2 7.2 %collective-permute-start.7 = (f32[80,512]{1,0:T(8,128)S(1)}, f32[80,512]{1,0:T(8,128)S(1)}, u32[]{:S(2)}, u32[]{:S(2)}) collective-permute-start(f32[80,512]{1,0:T(8,128)S(1)} %add_add_fusion.refs_0_), channel_id=1, source_target_pairs={{0,2},{1,3},{2,0},{3,1},{16,18},{17,19},{18,16},{19,17},{4,6},{5,7... | collective-permute-start | bytes 491528 | tf_op jit(solution)/shard_map/ppermute | solution.py:545
  52.5 2.0 %collective-permute-start.9 = (f32[256,512]{1,0:T(8,128)S(1)}, f32[256,512]{1,0:T(8,128)S(1)}, u32[]{:S(2)}, u32[]{:S(2)}) collective-permute-start(f32[256,512]{1,0:T(8,128)S(1)} %cross_block.4), channel_id=1, source_target_pairs={{0,1},{1,0},{2,3},{3,2},{4,5},{5,4},{6,7},{7,6},{8,9},{9,8},{10,11... | collective-permute-start | bytes 1572872 | tf_op jit(solution)/shard_map/ppermute | solution.py:539
  55.0 5.7 %collective-permute-start.10 = (f32[64,512]{1,0:T(8,128)S(1)}, f32[64,512]{1,0:T(8,128)S(1)}, u32[]{:S(2)}, u32[]{:S(2)}) collective-permute-start(f32[64,512]{1,0:T(8,128)S(1)} %get-tuple-element.49), channel_id=1, source_target_pairs={{0,16},{1,17},{2,18},{3,19},{16,0},{17,1},{18,2},{19,3},{4,20},{5,... | collective-permute-start | bytes 393224 | tf_op jit(solution)/shard_map/ppermute | solution.py:545
  56.9 7.3 %collective-permute-start.17 = (f32[64,512]{1,0:T(8,128)S(1)}, f32[64,512]{1,0:T(8,128)S(1)}, u32[]{:S(2)}, u32[]{:S(2)}) collective-permute-start(f32[64,512]{1,0:T(8,128)S(1)} %get-tuple-element.55), channel_id=1, source_target_pairs={{0,2},{1,3},{2,0},{3,1},{16,18},{17,19},{18,16},{19,17},{4,6},{5,7... | collective-permute-start | bytes 393224 | tf_op jit(solution)/shard_map/ppermute | solution.py:545
  58.4 7.3 %collective-permute-start.18 = (f32[64,512]{1,0:T(8,128)S(1)}, f32[64,512]{1,0:T(8,128)S(1)}, u32[]{:S(2)}, u32[]{:S(2)}) collective-permute-start(f32[64,512]{1,0:T(8,128)S(1)} %get-tuple-element.56), channel_id=1, source_target_pairs={{0,18},{1,19},{2,16},{3,17},{16,2},{17,3},{18,0},{19,1},{4,22},{5,... | collective-permute-start | bytes 393224 | tf_op jit(solution)/shard_map/ppermute | solution.py:545
  60.7 16.5 %collective-permute-start.11 = (f32[80,512]{1,0:T(8,128)S(1)}, f32[80,512]{1,0:T(8,128)S(1)}, u32[]{:S(2)}, u32[]{:S(2)}) collective-permute-start(f32[80,512]{1,0:T(8,128)S(1)} %add_add_fusion.refs_0_), channel_id=1, source_target_pairs={{0,16},{1,17},{2,18},{3,19},{16,0},{17,1},{18,2},{19,3},{4,20},{5,... | collective-permute-start | bytes 491528 | tf_op jit(solution)/shard_map/ppermute | solution.py:545
  63.2 14.1 %collective-permute-start.12 = (f32[80,512]{1,0:T(8,128)S(1)}, f32[80,512]{1,0:T(8,128)S(1)}, u32[]{:S(2)}, u32[]{:S(2)}) collective-permute-start(f32[80,512]{1,0:T(8,128)S(1)} %collective-permute-done.7.refs_2_), channel_id=1, source_target_pairs={{0,16},{1,17},{2,18},{3,19},{16,0},{17,1},{18,2},{19,3},{4,20},{5,... | collective-permute-start | bytes 491528 | tf_op jit(solution)/shard_map/ppermute | solution.py:545
  65.7 8.3 %collective-permute-start.21 = (f32[64,512]{1,0:T(8,128)S(1)}, f32[64,512]{1,0:T(8,128)S(1)}, u32[]{:S(2)}, u32[]{:S(2)}) collective-permute-start(f32[64,512]{1,0:T(8,128)S(1)} %add_add_fusion.2), channel_id=1, source_target_pairs={{0,4},{4,8},{8,12},{12,0},{1,5},{5,9},{9,13},{13,1},{2,6},{6,10},{... | collective-permute-start | bytes 393224 | tf_op jit(solution)/shard_map/ppermute | solution.py:550
  67.3 9.9 %collective-permute-start.20 = (f32[64,512]{1,0:T(8,128)S(1)}, f32[64,512]{1,0:T(8,128)S(1)}, u32[]{:S(2)}, u32[]{:S(2)}) collective-permute-start(f32[64,512]{1,0:T(8,128)S(1)} %add_add_fusion.2), channel_id=1, source_target_pairs={{0,8},{4,12},{8,0},{12,4},{1,9},{5,13},{9,1},{13,5},{2,10},{6,14},... | collective-permute-start | bytes 393224 | tf_op jit(solution)/shard_map/ppermute | solution.py:550
  69.9 7.3 %collective-permute-start.19 = (f32[64,512]{1,0:T(8,128)S(1)}, f32[64,512]{1,0:T(8,128)S(1)}, u32[]{:S(2)}, u32[]{:S(2)}) collective-permute-start(f32[64,512]{1,0:T(8,128)S(1)} %add_add_fusion.2), channel_id=1, source_target_pairs={{0,12},{4,0},{8,4},{12,8},{1,13},{5,1},{9,5},{13,9},{2,14},{6,2},{... | collective-permute-start | bytes 393224 | tf_op jit(solution)/shard_map/ppermute | solution.py:550
  74.1 5.3 %collective-permute-start.13 = (f32[80,512]{1,0:T(8,128)S(1)}, f32[80,512]{1,0:T(8,128)S(1)}, u32[]{:S(2)}, u32[]{:S(2)}) collective-permute-start(f32[80,512]{1,0:T(8,128)S(1)} %add_add_fusion.refs_0_), channel_id=1, source_target_pairs={{0,1},{1,0},{2,3},{3,2},{4,5},{5,4},{6,7},{7,6},{8,9},{9,8},{10,11... | collective-permute-start | bytes 491528 | tf_op jit(solution)/shard_map/ppermute | solution.py:539
  77.3 3.6 %collective-permute-start.15 = (f32[80,512]{1,0:T(8,128)S(1)}, f32[80,512]{1,0:T(8,128)S(1)}, u32[]{:S(2)}, u32[]{:S(2)}) collective-permute-start(f32[80,512]{1,0:T(8,128)S(1)} %collective-permute-done.7.refs_2_), channel_id=1, source_target_pairs={{0,1},{1,0},{2,3},{3,2},{4,5},{5,4},{6,7},{7,6},{8,9},{9,8},{10,11... | collective-permute-start | bytes 491528 | tf_op jit(solution)/shard_map/ppermute | solution.py:539
  77.3 4.2 %collective-permute-start.14 = (f32[80,512]{1,0:T(8,128)S(1)}, f32[80,512]{1,0:T(8,128)S(1)}, u32[]{:S(2)}, u32[]{:S(2)}) collective-permute-start(f32[80,512]{1,0:T(8,128)S(1)} %collective-permute-done.11.refs_1_), channel_id=1, source_target_pairs={{0,1},{1,0},{2,3},{3,2},{4,5},{5,4},{6,7},{7,6},{8,9},{9,8},{10,11... | collective-permute-start | bytes 491528 | tf_op jit(solution)/shard_map/ppermute | solution.py:539
  77.9 3.7 %collective-permute-start.16 = (f32[80,512]{1,0:T(8,128)S(1)}, f32[80,512]{1,0:T(8,128)S(1)}, u32[]{:S(2)}, u32[]{:S(2)}) collective-permute-start(f32[80,512]{1,0:T(8,128)S(1)} %collective-permute-done.12.refs_3_), channel_id=1, source_target_pairs={{0,1},{1,0},{2,3},{3,2},{4,5},{5,4},{6,7},{7,6},{8,9},{9,8},{10,11... | collective-permute-start | bytes 491528 | tf_op jit(solution)/shard_map/ppermute | solution.py:539
  78.0 7.3 %collective-permute-start.24 = (f32[64,512]{1,0:T(8,128)S(1)}, f32[64,512]{1,0:T(8,128)S(1)}, u32[]{:S(2)}, u32[]{:S(2)}) collective-permute-start(f32[64,512]{1,0:T(8,128)S(1)} %add_add_fusion.1.refs_3_), channel_id=1, source_target_pairs={{0,18},{1,19},{2,16},{3,17},{16,2},{17,3},{18,0},{19,1},{4,22},{5,... | collective-permute-start | bytes 393224 | tf_op jit(solution)/shard_map/ppermute | solution.py:545
  79.4 8.2 %collective-permute-start.23 = (f32[64,512]{1,0:T(8,128)S(1)}, f32[64,512]{1,0:T(8,128)S(1)}, u32[]{:S(2)}, u32[]{:S(2)}) collective-permute-start(f32[64,512]{1,0:T(8,128)S(1)} %add_add_fusion.1.refs_3_), channel_id=1, source_target_pairs={{0,2},{1,3},{2,0},{3,1},{16,18},{17,19},{18,16},{19,17},{4,6},{5,7... | collective-permute-start | bytes 393224 | tf_op jit(solution)/shard_map/ppermute | solution.py:545
  80.9 6.7 %collective-permute-start.22 = (f32[64,512]{1,0:T(8,128)S(1)}, f32[64,512]{1,0:T(8,128)S(1)}, u32[]{:S(2)}, u32[]{:S(2)}) collective-permute-start(f32[64,512]{1,0:T(8,128)S(1)} %add_add_fusion.1.refs_3_), channel_id=1, source_target_pairs={{0,16},{1,17},{2,18},{3,19},{16,0},{17,1},{18,2},{19,3},{4,20},{5,... | collective-permute-start | bytes 393224 | tf_op jit(solution)/shard_map/ppermute | solution.py:545
  81.5 6.6 %collective-permute-start.25 = (f32[64,512]{1,0:T(8,128)S(1)}, f32[64,512]{1,0:T(8,128)S(1)}, u32[]{:S(2)}, u32[]{:S(2)}) collective-permute-start(f32[64,512]{1,0:T(8,128)S(1)} %add_add_fusion.1.refs_3_), channel_id=1, source_target_pairs={{0,1},{1,0},{2,3},{3,2},{4,5},{5,4},{6,7},{7,6},{8,9},{9,8},{10,11... | collective-permute-start | bytes 393224 | tf_op jit(solution)/shard_map/ppermute | solution.py:539
  87.6 1.3 %collective-permute-start.26 = (f32[64,512]{1,0:T(8,128)S(1)}, f32[64,512]{1,0:T(8,128)S(1)}, u32[]{:S(2)}, u32[]{:S(2)}) collective-permute-start(f32[64,512]{1,0:T(8,128)S(1)} %collective-permute-done.22.refs_4_), channel_id=1, source_target_pairs={{0,1},{1,0},{2,3},{3,2},{4,5},{5,4},{6,7},{7,6},{8,9},{9,8},{10,11... | collective-permute-start | bytes 393224 | tf_op jit(solution)/shard_map/ppermute | solution.py:539
  87.6 1.5 %collective-permute-start.27 = (f32[64,512]{1,0:T(8,128)S(1)}, f32[64,512]{1,0:T(8,128)S(1)}, u32[]{:S(2)}, u32[]{:S(2)}) collective-permute-start(f32[64,512]{1,0:T(8,128)S(1)} %collective-permute-done.23.refs_5_), channel_id=1, source_target_pairs={{0,1},{1,0},{2,3},{3,2},{4,5},{5,4},{6,7},{7,6},{8,9},{9,8},{10,11... | collective-permute-start | bytes 393224 | tf_op jit(solution)/shard_map/ppermute | solution.py:539
  88.1 1.3 %collective-permute-start.28 = (f32[64,512]{1,0:T(8,128)S(1)}, f32[64,512]{1,0:T(8,128)S(1)}, u32[]{:S(2)}, u32[]{:S(2)}) collective-permute-start(f32[64,512]{1,0:T(8,128)S(1)} %collective-permute-done.24.refs_6_), channel_id=1, source_target_pairs={{0,1},{1,0},{2,3},{3,2},{4,5},{5,4},{6,7},{7,6},{8,9},{9,8},{10,11... | collective-permute-start | bytes 393224 | tf_op jit(solution)/shard_map/ppermute | solution.py:539
  110.7 8.4 %collective-permute-start.29 = (f32[8,1,32,128]{3,2,1,0:T(8,128)S(1)}, f32[8,1,32,128]{3,2,1,0:T(8,128)S(1)}, u32[]{:S(2)}, u32[]{:S(2)}) collective-permute-start(f32[8,1,32,128]{3,2,1,0:T(8,128)S(1)} %get-tuple-element.66), channel_id=1, source_target_pairs={{0,4},{4,8},{8,12},{12,0},{1,5},{5,9},{9,13},{13,1},{2,6},{6,10},{... | collective-permute-start | bytes 393224 | tf_op jit(solution)/shard_map/ppermute | solution.py:621
  113.2 11.1 %collective-permute-start.30 = (f32[8,1,32,128]{3,2,1,0:T(8,128)S(1)}, f32[8,1,32,128]{3,2,1,0:T(8,128)S(1)}, u32[]{:S(2)}, u32[]{:S(2)}) collective-permute-start(f32[8,1,32,128]{3,2,1,0:T(8,128)S(1)} %get-tuple-element.67), channel_id=1, source_target_pairs={{0,8},{4,12},{8,0},{12,4},{1,9},{5,13},{9,1},{13,5},{2,10},{6,14},... | collective-permute-start | bytes 393224 | tf_op jit(solution)/shard_map/ppermute | solution.py:621
  115.3 9.0 %collective-permute-start.31 = (f32[8,1,32,128]{3,2,1,0:T(8,128)S(1)}, f32[8,1,32,128]{3,2,1,0:T(8,128)S(1)}, u32[]{:S(2)}, u32[]{:S(2)}) collective-permute-start(f32[8,1,32,128]{3,2,1,0:T(8,128)S(1)} %get-tuple-element.68), channel_id=1, source_target_pairs={{0,12},{4,0},{8,4},{12,8},{1,13},{5,1},{9,5},{13,9},{2,14},{6,2},{... | collective-permute-start | bytes 393224 | tf_op jit(solution)/shard_map/ppermute | solution.py:621
